TPU v7x, 32 devices: a whole 2x2x4 slice. The times are simulated.
32 devices in a mesh: dp: 8 (over z, y), tensor: 4 (over x, core).
Axes of the slice: x: 2, y: 2, z: 4, core: 2. Of those that a mesh axis runs over, the one named last changes fastest.
Arguments:
- tokens: bfloat16 [8192, 2560], P(('dp', 'tensor')), may hold values from -6 to 6
- cotangent: bfloat16 [8192, 2560], P(('dp', 'tensor')), may hold values from -6 to 6
- doc_lengths: int32 [8, 4], P('dp'), may hold values from 1 to 800, 1024 in all within a row
- query_weight: float32 [2560, 2560], P('dp', 'tensor'), may hold values from -0.125 to 0.125
- keyvalue_weight_full: float32 [2560, 2, 640], P('dp', None, 'tensor'), may hold values from -0.125 to 0.125
- output_weight: float32 [2560, 2560], P('dp', 'tensor'), may hold values from -0.625 to 0.625
- gating_weight: float32 [2560, 2, 7168], P('dp', None, 'tensor'), may hold values from -0.125 to 0.125
- down_weight: float32 [2560, 7168], P('dp', 'tensor'), may hold values from -0.125 to 0.125
- norm_gains: float32 [2, 2560], P(None, 'dp'), may hold values from 0.5 to 1.5
- first_query: float32 [4, 2560, 2560], P(None, 'dp', 'tensor'), may hold values from -64 to 64
- keyvalue_first_moment: float32 [4, 2560, 2, 640], P(None, 'dp', None, 'tensor'), may hold values from -80 to 80
- first_output: float32 [4, 2560, 2560], P(None, 'dp', 'tensor'), may hold values from -8 to 8
- first_gating: float32 [4, 2560, 2, 7168], P(None, 'dp', None, 'tensor'), may hold values from -16 to 16
- first_down: float32 [4, 2560, 7168], P(None, 'dp', 'tensor'), may hold values from -16 to 16
- first_gains: float32 [4, 2, 2560], P(None, None, 'dp'), may hold values from -48 to 48
- second_query: float32 [4, 2560, 2560], P(None, 'dp', 'tensor'), may hold values from 245.76 to 3276.8
- keyvalue_second_moment: float32 [4, 2560, 2, 640], P(None, 'dp', None, 'tensor'), may hold values from 389.12 to 5120
- second_output: float32 [4, 2560, 2560], P(None, 'dp', 'tensor'), may hold values from 3.8912 to 51.2
- second_gating: float32 [4, 2560, 2, 7168], P(None, 'dp', None, 'tensor'), may hold values from 22.528 to 294.912
- second_down: float32 [4, 2560, 7168], P(None, 'dp', 'tensor'), may hold values from 22.528 to 294.912
- second_gains: float32 [4, 2, 2560], P(None, None, 'dp'), may hold values from 139.264 to 1843.2
- moment_query: float32 [2560, 2560], P('dp', 'tensor'), may hold values from -0.015625 to 0.015625
- keyvalue_outer_momentum: float32 [2560, 2, 640], P('dp', None, 'tensor'), may hold values from -0.015625 to 0.015625
- moment_output: float32 [2560, 2560], P('dp', 'tensor'), may hold values from -0.0625 to 0.0625
- moment_gating: float32 [2560, 2, 7168], P('dp', None, 'tensor'), may hold values from -0.015625 to 0.015625
- moment_down: float32 [2560, 7168], P('dp', 'tensor'), may hold values from -0.015625 to 0.015625
- moment_gains: float32 [2, 2560], P(None, 'dp'), may hold values from -0.1875 to 0.1875
Outputs:
- block_output: bfloat16 [8192, 2560], P(('dp', 'tensor'))
- token_grad: bfloat16 [8192, 2560], P(('dp', 'tensor'))
- query_first: float32 [4, 2560, 2560], P(None, 'dp', 'tensor')
- query_second: float32 [4, 2560, 2560], P(None, 'dp', 'tensor')
- query_delta: float32 [2560, 2560], P('dp', 'tensor')
- query_moment: float32 [2560, 2560], P('dp', 'tensor')
- query_master: float32 [2560, 2560], P('dp', 'tensor')
- query_copy: bfloat16 [2560, 2560], P('dp', 'tensor')
- keyvalue_first: float32 [4, 2560, 2, 640], P(None, 'dp', None, 'tensor')
- keyvalue_second: float32 [4, 2560, 2, 640], P(None, 'dp', None, 'tensor')
- keyvalue_delta: float32 [2560, 2, 640], P('dp', None, 'tensor')
- keyvalue_moment: float32 [2560, 2, 640], P('dp', None, 'tensor')
- keyvalue_master: float32 [2560, 2, 640], P('dp', None, 'tensor')
- keyvalue_copy: bfloat16 [2560, 2, 640], P('dp', None, 'tensor')
- output_first: float32 [4, 2560, 2560], P(None, 'dp', 'tensor')
- output_second: float32 [4, 2560, 2560], P(None, 'dp', 'tensor')
- output_delta: float32 [2560, 2560], P('dp', 'tensor')
- output_moment: float32 [2560, 2560], P('dp', 'tensor')
- output_master: float32 [2560, 2560], P('dp', 'tensor')
- output_copy: bfloat16 [2560, 2560], P('dp', 'tensor')
- gating_first: float32 [4, 2560, 2, 7168], P(None, 'dp', None, 'tensor')
- gating_second: float32 [4, 2560, 2, 7168], P(None, 'dp', None, 'tensor')
- gating_delta: float32 [2560, 2, 7168], P('dp', None, 'tensor')
- gating_moment: float32 [2560, 2, 7168], P('dp', None, 'tensor')
- gating_master: float32 [2560, 2, 7168], P('dp', None, 'tensor')
- gating_copy: bfloat16 [2560, 2, 7168], P('dp', None, 'tensor')
- down_first: float32 [4, 2560, 7168], P(None, 'dp', 'tensor')
- down_second: float32 [4, 2560, 7168], P(None, 'dp', 'tensor')
- down_delta: float32 [2560, 7168], P('dp', 'tensor')
- down_moment: float32 [2560, 7168], P('dp', 'tensor')
- down_master: float32 [2560, 7168], P('dp', 'tensor')
- down_copy: bfloat16 [2560, 7168], P('dp', 'tensor')
- gains_first: float32 [4, 2, 2560], P(None, None, 'dp')
- gains_second: float32 [4, 2, 2560], P(None, None, 'dp')
- gains_delta: float32 [2, 2560], P(None, 'dp')
- gains_moment: float32 [2, 2560], P(None, 'dp')
- gains_master: float32 [2, 2560], P(None, 'dp')
- gains_copy: bfloat16 [2, 2560], P(None, 'dp')
Inputs may be any that keep to these rules, and one draw needn't show every extreme that they name: `doc_lengths`: each row holds the lengths of the 4 documents packed in order into one sequence; they sum to 1024, and the longest of each row is exactly 800.
All inputs are finite; a program needn't handle non-finite values.
Results may differ from a plain program's by a relative error of at most 0.023.
Values may be sent and summed in bfloat16 or wider, within the bound.
No kernel may reach another device: no remote copies, remote signals or barrier semaphores. Data moves between devices by JAX's collectives and lax.ppermute only.
A program may use at most 384 MiB of HBM per device.

v0:
```python
import math

import jax
import jax.numpy as jnp
from jax import lax
from jax.sharding import PartitionSpec as P

HEAD_WIDTH = 80
REPLICA_GROUPS = 4
STEP = 8


epsilon = 1e-05
rope_base = 1000000.0
beta_one = 0.9
beta_two = 0.95
adam_epsilon = 1e-08
outer_mu = 0.9
outer_rate = 0.7
inner_rates = (0.05, 0.05, 0.2, 0.05, 0.05, 0.5)
inner_decays = (0.1, 0.1, 0.1, 0.1, 0.1, 0.0)


def matmul_plain(left, right):
    return jnp.dot(left, right, preferred_element_type=jnp.float32)


def matmul_right_t(left, right):
    return lax.dot_general(
        left, right, (((1,), (1,)), ((), ())), preferred_element_type=jnp.float32
    )


def matmul_left_t(left, right):
    return lax.dot_general(
        left, right, (((0,), (0,)), ((), ())), preferred_element_type=jnp.float32
    )


def doc_layout(lengths, token_length):
    ends = jnp.cumsum(lengths)
    starts = ends - lengths
    places = jnp.arange(token_length, dtype=jnp.int32)
    segment = jnp.sum((places[:, None] >= ends[None, :]).astype(jnp.int32), axis=1)
    member = (segment[:, None] == jnp.arange(lengths.shape[0], dtype=jnp.int32)[None, :]).astype(
        jnp.int32
    )
    offset = jnp.sum(member * starts[None, :], axis=1)
    return (segment, places - offset)


def rope_tables(position, head_size):
    half_size = head_size // 2
    frequency = rope_base ** (-2.0 * jnp.arange(half_size, dtype=jnp.float32) / head_size)
    angle = position.astype(jnp.float32)[:, None] * frequency[None, :]
    return (jnp.cos(angle), jnp.sin(angle))


def rotate(value, cosine, sine):
    half_size = value.shape[-1] // 2
    first = value[..., :half_size]
    second = value[..., half_size:]
    cos_wide = cosine[:, None, :]
    sin_wide = sine[:, None, :]
    return jnp.concatenate(
        [first * cos_wide - second * sin_wide, second * cos_wide + first * sin_wide], axis=-1
    )


def norm_inverse(value):
    return lax.rsqrt(jnp.mean(value * value, axis=-1, keepdims=True) + epsilon)


def norm_backward(value, inverse, gain, grad_normed):
    scaled = gain * grad_normed
    grad_value = inverse * scaled - value * inverse**3 * jnp.mean(
        scaled * value, axis=-1, keepdims=True
    )
    grad_gain = jnp.sum(grad_normed * value * inverse, axis=0)
    return (grad_value, grad_gain)


def block_scores(query_block, key_rot, segment, places, start, block, scale):
    scores = (
        jnp.einsum("bkgd,skd->kgbs", query_block, key_rot, preferred_element_type=jnp.float32)
        * scale
    )
    row_index = start + jnp.arange(block, dtype=jnp.int32)
    row_segment = lax.dynamic_slice_in_dim(segment, start, block, 0)
    allowed = (row_segment[:, None] == segment[None, :]) & (row_index[:, None] >= places[None, :])
    return jnp.where(allowed[None, None], scores, -1e30)


def attention_forward(query_groups, key_rot, values, segment, block):
    token_length = query_groups.shape[0]
    places = jnp.arange(token_length, dtype=jnp.int32)
    scale = 1.0 / math.sqrt(query_groups.shape[-1])

    def one_block(start):
        query_block = lax.dynamic_slice_in_dim(query_groups, start, block, 0)
        scores = block_scores(query_block, key_rot, segment, places, start, block, scale)
        top = jnp.max(scores, axis=-1, keepdims=True)
        expo = jnp.exp(scores - top)
        total = jnp.sum(expo, axis=-1, keepdims=True)
        probability = (expo / total).astype(jnp.bfloat16)
        mixed = jnp.einsum(
            "kgbs,skd->bkgd", probability, values, preferred_element_type=jnp.float32
        )
        return (mixed, (top + jnp.log(total))[..., 0])

    starts = jnp.arange(token_length // block, dtype=jnp.int32) * block
    mixed, log_total = lax.map(one_block, starts)
    return (mixed.reshape(query_groups.shape), log_total)


def attention_backward(query_groups, key_rot, values, grad_mixed, log_total, segment, block):
    token_length = query_groups.shape[0]
    places = jnp.arange(token_length, dtype=jnp.int32)
    scale = 1.0 / math.sqrt(query_groups.shape[-1])

    def one_block(carry, inputs):
        grad_key, grad_value = carry
        start, block_total = inputs
        query_block = lax.dynamic_slice_in_dim(query_groups, start, block, 0)
        grad_block = lax.dynamic_slice_in_dim(grad_mixed, start, block, 0)
        scores = block_scores(query_block, key_rot, segment, places, start, block, scale)
        probability = jnp.exp(scores - block_total[..., None])
        probability_low = probability.astype(jnp.bfloat16)
        grad_prob = jnp.einsum(
            "bkgd,skd->kgbs", grad_block, values, preferred_element_type=jnp.float32
        )
        inner = jnp.sum(probability * grad_prob, axis=-1, keepdims=True)
        grad_scores = (probability * (grad_prob - inner)).astype(jnp.bfloat16)
        grad_query = (
            jnp.einsum("kgbs,skd->bkgd", grad_scores, key_rot, preferred_element_type=jnp.float32)
            * scale
        )
        grad_key = (
            grad_key
            + jnp.einsum(
                "kgbs,bkgd->skd", grad_scores, query_block, preferred_element_type=jnp.float32
            )
            * scale
        )
        grad_value = grad_value + jnp.einsum(
            "kgbs,bkgd->skd", probability_low, grad_block, preferred_element_type=jnp.float32
        )
        return ((grad_key, grad_value), grad_query)

    zero_pairs = jnp.zeros(key_rot.shape, jnp.float32)
    starts = jnp.arange(token_length // block, dtype=jnp.int32) * block
    (grad_key, grad_value), grad_query = lax.scan(
        one_block, (zero_pairs, zero_pairs), (starts, log_total)
    )
    return (grad_query.reshape(query_groups.shape), grad_key, grad_value)


def to_sources(grad, pieces):
    return grad.reshape((pieces, grad.shape[0] // pieces) + grad.shape[1:])


def group_totals(received):
    return jnp.sum(
        received.reshape(
            (REPLICA_GROUPS, received.shape[0] // REPLICA_GROUPS) + received.shape[1:]
        ),
        axis=1,
    )


def optimize(weight, grad, first, second, moment, rate, decay):
    first_new = beta_one * first + (1.0 - beta_one) * grad
    second_new = beta_two * second + (1.0 - beta_two) * grad * grad
    correct_one = 1.0 - beta_one**STEP
    correct_two = 1.0 - beta_two**STEP
    direction = (
        first_new / correct_one / (jnp.sqrt(second_new / correct_two) + adam_epsilon)
        + decay * weight[None]
    )
    delta = jnp.mean(rate * direction, axis=0)
    moment_new = outer_mu * moment + delta
    weight_new = weight - outer_rate * (delta + outer_mu * moment_new)
    return (first_new, second_new, delta, moment_new, weight_new, weight_new.astype(jnp.bfloat16))


def per_device(
    tokens,
    cotangent,
    doc_lengths,
    query_weight,
    keyvalue_weight_full,
    output_weight,
    gating_weight,
    down_weight,
    norm_gains,
    first_query,
    keyvalue_first_moment,
    first_output,
    first_gating,
    first_down,
    first_gains,
    second_query,
    keyvalue_second_moment,
    second_output,
    second_gating,
    second_down,
    second_gains,
    moment_query,
    keyvalue_outer_momentum,
    moment_output,
    moment_gating,
    moment_down,
    moment_gains,
):
    low_type = jnp.bfloat16
    query_all, keyvalue_all, output_all, gating_all, down_all, gains_all = (
        lax.all_gather(query_weight.astype(low_type), "dp", axis=0, tiled=True),
        lax.all_gather(keyvalue_weight_full.astype(low_type), "dp", axis=0, tiled=True),
        lax.all_gather(output_weight.astype(low_type), "dp", axis=0, tiled=True),
        lax.all_gather(gating_weight.astype(low_type), "dp", axis=0, tiled=True),
        lax.all_gather(down_weight.astype(low_type), "dp", axis=0, tiled=True),
        lax.all_gather(norm_gains.astype(low_type), "dp", axis=1, tiled=True),
    )
    gain_one = gains_all[0].astype(jnp.float32)
    gain_two = gains_all[1].astype(jnp.float32)
    local_rows = tokens.shape[0]
    token_length = local_rows * lax.axis_size("tensor")
    width = tokens.shape[1]
    pieces = lax.axis_size("dp")
    heads_local = query_all.shape[1] // HEAD_WIDTH
    pairs_local = keyvalue_all.shape[2] // HEAD_WIDTH
    hidden_local = gating_all.shape[2]
    replica_group_size = heads_local // pairs_local
    block = min(512, token_length)
    keyvalue_flat = keyvalue_all.reshape(width, 2 * pairs_local * HEAD_WIDTH)
    gating_flat = gating_all.reshape(width, 2 * hidden_local)
    segment, position = doc_layout(doc_lengths[0], token_length)
    cosine, sine = rope_tables(position, HEAD_WIDTH)
    hidden = tokens.astype(jnp.float32)
    inverse_one = norm_inverse(hidden)
    first_normalized = (hidden * inverse_one * gain_one).astype(low_type)
    normed_one_all = lax.all_gather(first_normalized, "tensor", axis=0, tiled=True)
    query = matmul_plain(normed_one_all, query_all).reshape(token_length, heads_local, HEAD_WIDTH)
    keyvalue_proj = matmul_plain(normed_one_all, keyvalue_flat).reshape(
        token_length, 2, pairs_local, HEAD_WIDTH
    )
    query_groups = (
        rotate(query, cosine, sine)
        .astype(low_type)
        .reshape(token_length, pairs_local, replica_group_size, HEAD_WIDTH)
    )
    key_rot = rotate(keyvalue_proj[:, 0], cosine, sine).astype(low_type)
    values = keyvalue_proj[:, 1].astype(low_type)
    mixed, log_total = attention_forward(query_groups, key_rot, values, segment, block)
    mixed_low = mixed.reshape(token_length, heads_local * HEAD_WIDTH).astype(low_type)
    attention = lax.psum_scatter(
        matmul_right_t(mixed_low, output_all).astype(jnp.bfloat16),
        "tensor",
        scatter_dimension=0,
        tiled=True,
    ).astype(jnp.float32)
    hidden_one = hidden + attention
    inverse_two = norm_inverse(hidden_one)
    normed_two = (hidden_one * inverse_two * gain_two).astype(low_type)
    normed_two_all = lax.all_gather(normed_two, "tensor", axis=0, tiled=True)
    gating = matmul_plain(normed_two_all, gating_flat).reshape(token_length, 2, hidden_local)
    gate_part = gating[:, 0]
    up_part = gating[:, 1]
    sigmoid_gate = jax.nn.sigmoid(gate_part)
    silu_gate = gate_part * sigmoid_gate
    activated = (silu_gate * up_part).astype(low_type)
    feed = lax.psum_scatter(
        matmul_right_t(activated, down_all).astype(jnp.bfloat16),
        "tensor",
        scatter_dimension=0,
        tiled=True,
    ).astype(jnp.float32)
    block_output = (hidden_one + feed).astype(low_type)
    cotangent_all = lax.all_gather(cotangent, "tensor", axis=0, tiled=True)
    grad_activated = matmul_plain(cotangent_all, down_all)
    grad_down = matmul_left_t(cotangent_all, activated)
    grad_gate = grad_activated * up_part * sigmoid_gate * (1.0 + gate_part * (1.0 - sigmoid_gate))
    grad_up = grad_activated * silu_gate
    grad_gating_flat = (
        jnp.stack([grad_gate, grad_up], axis=1)
        .astype(low_type)
        .reshape(token_length, 2 * hidden_local)
    )
    grad_gating = matmul_left_t(normed_two_all, grad_gating_flat).reshape(width, 2, hidden_local)
    feed_received = (
        lax.all_to_all(
            to_sources(grad_gating, pieces).astype(jnp.bfloat16),
            "dp",
            split_axis=0,
            concat_axis=0,
            tiled=True,
        ).astype(jnp.float32),
        lax.all_to_all(
            to_sources(grad_down, pieces).astype(jnp.bfloat16),
            "dp",
            split_axis=0,
            concat_axis=0,
            tiled=True,
        ).astype(jnp.float32),
    )
    grad_normed_two = lax.psum_scatter(
        matmul_right_t(grad_gating_flat, gating_flat).astype(jnp.bfloat16),
        "tensor",
        scatter_dimension=0,
        tiled=True,
    ).astype(jnp.float32)
    grad_hidden_two, grad_gain_two = norm_backward(
        hidden_one, inverse_two, gain_two, grad_normed_two
    )
    grad_hidden_one = cotangent.astype(jnp.float32) + grad_hidden_two
    grad_hidden_all = lax.all_gather(grad_hidden_one.astype(low_type), "tensor", axis=0, tiled=True)
    grad_mixed = matmul_plain(grad_hidden_all, output_all).astype(low_type)
    grad_output = matmul_left_t(grad_hidden_all, mixed_low)
    grad_query_rot, grad_key_rot, grad_values = attention_backward(
        query_groups,
        key_rot,
        values,
        grad_mixed.reshape(token_length, pairs_local, replica_group_size, HEAD_WIDTH),
        log_total,
        segment,
        block,
    )
    grad_query = (
        rotate(grad_query_rot.reshape(token_length, heads_local, HEAD_WIDTH), cosine, -sine)
        .reshape(token_length, heads_local * HEAD_WIDTH)
        .astype(low_type)
    )
    grad_keyvalue = (
        jnp.stack([rotate(grad_key_rot, cosine, -sine), grad_values], axis=1)
        .reshape(token_length, 2 * pairs_local * HEAD_WIDTH)
        .astype(low_type)
    )
    grad_query_weight = matmul_left_t(normed_one_all, grad_query)
    grad_keyvalue_weight = matmul_left_t(normed_one_all, grad_keyvalue).reshape(
        width, 2, pairs_local * HEAD_WIDTH
    )
    grad_normed_one = lax.psum_scatter(
        (
            matmul_right_t(grad_query, query_all) + matmul_right_t(grad_keyvalue, keyvalue_flat)
        ).astype(jnp.bfloat16),
        "tensor",
        scatter_dimension=0,
        tiled=True,
    ).astype(jnp.float32)
    grad_hidden_norm, grad_gain_one = norm_backward(hidden, inverse_one, gain_one, grad_normed_one)
    token_grad = (grad_hidden_one + grad_hidden_norm).astype(low_type)
    grad_gains = jnp.stack([grad_gain_one, grad_gain_two], axis=0)
    gains_sources = grad_gains.reshape(2, pieces, width // pieces).transpose(1, 0, 2)
    heads_received = (
        lax.all_to_all(
            to_sources(grad_query_weight, pieces).astype(jnp.bfloat16),
            "dp",
            split_axis=0,
            concat_axis=0,
            tiled=True,
        ).astype(jnp.float32),
        lax.all_to_all(
            to_sources(grad_keyvalue_weight, pieces).astype(jnp.bfloat16),
            "dp",
            split_axis=0,
            concat_axis=0,
            tiled=True,
        ).astype(jnp.float32),
        lax.all_to_all(
            to_sources(grad_output, pieces).astype(jnp.bfloat16),
            "dp",
            split_axis=0,
            concat_axis=0,
            tiled=True,
        ).astype(jnp.float32),
        lax.all_to_all(
            gains_sources.astype(jnp.bfloat16), "dp", split_axis=0, concat_axis=0, tiled=True
        ).astype(gains_sources.dtype),
    )
    received = (
        heads_received[0],
        heads_received[1],
        heads_received[2],
        feed_received[0],
        feed_received[1],
        heads_received[3],
    )
    totals = [group_totals(part) for part in received]
    totals[5] = lax.psum(totals[5], "tensor")
    masters = (
        query_weight,
        keyvalue_weight_full,
        output_weight,
        gating_weight,
        down_weight,
        norm_gains,
    )
    firsts = (
        first_query,
        keyvalue_first_moment,
        first_output,
        first_gating,
        first_down,
        first_gains,
    )
    seconds = (
        second_query,
        keyvalue_second_moment,
        second_output,
        second_gating,
        second_down,
        second_gains,
    )
    moments = (
        moment_query,
        keyvalue_outer_momentum,
        moment_output,
        moment_gating,
        moment_down,
        moment_gains,
    )
    updated = [
        optimize(
            masters[kind],
            totals[kind],
            firsts[kind],
            seconds[kind],
            moments[kind],
            inner_rates[kind],
            inner_decays[kind],
        )
        for kind in range(6)
    ]
    qry, kvl, out, gat, dwn, gns = updated
    return (
        block_output,
        token_grad,
        qry[0],
        qry[1],
        qry[2],
        qry[3],
        qry[4],
        qry[5],
        kvl[0],
        kvl[1],
        kvl[2],
        kvl[3],
        kvl[4],
        kvl[5],
        out[0],
        out[1],
        out[2],
        out[3],
        out[4],
        out[5],
        gat[0],
        gat[1],
        gat[2],
        gat[3],
        gat[4],
        gat[5],
        dwn[0],
        dwn[1],
        dwn[2],
        dwn[3],
        dwn[4],
        dwn[5],
        gns[0],
        gns[1],
        gns[2],
        gns[3],
        gns[4],
        gns[5],
    )


def solution(mesh):
    return jax.shard_map(
        per_device,
        mesh=mesh,
        in_specs=(
            P(("dp", "tensor"), None),
            P(("dp", "tensor"), None),
            P("dp", None),
            P("dp", "tensor"),
            P("dp", None, "tensor"),
            P("dp", "tensor"),
            P("dp", None, "tensor"),
            P("dp", "tensor"),
            P(None, "dp"),
            P(None, "dp", "tensor"),
            P(None, "dp", None, "tensor"),
            P(None, "dp", "tensor"),
            P(None, "dp", None, "tensor"),
            P(None, "dp", "tensor"),
            P(None, None, "dp"),
            P(None, "dp", "tensor"),
            P(None, "dp", None, "tensor"),
            P(None, "dp", "tensor"),
            P(None, "dp", None, "tensor"),
            P(None, "dp", "tensor"),
            P(None, None, "dp"),
            P("dp", "tensor"),
            P("dp", None, "tensor"),
            P("dp", "tensor"),
            P("dp", None, "tensor"),
            P("dp", "tensor"),
            P(None, "dp"),
        ),
        out_specs=(
            P(("dp", "tensor"), None),
            P(("dp", "tensor"), None),
            P(None, "dp", "tensor"),
            P(None, "dp", "tensor"),
            P("dp", "tensor"),
            P("dp", "tensor"),
            P("dp", "tensor"),
            P("dp", "tensor"),
            P(None, "dp", None, "tensor"),
            P(None, "dp", None, "tensor"),
            P("dp", None, "tensor"),
            P("dp", None, "tensor"),
            P("dp", None, "tensor"),
            P("dp", None, "tensor"),
            P(None, "dp", "tensor"),
            P(None, "dp", "tensor"),
            P("dp", "tensor"),
            P("dp", "tensor"),
            P("dp", "tensor"),
            P("dp", "tensor"),
            P(None, "dp", None, "tensor"),
            P(None, "dp", None, "tensor"),
            P("dp", None, "tensor"),
            P("dp", None, "tensor"),
            P("dp", None, "tensor"),
            P("dp", None, "tensor"),
            P(None, "dp", "tensor"),
            P(None, "dp", "tensor"),
            P("dp", "tensor"),
            P("dp", "tensor"),
            P("dp", "tensor"),
            P("dp", "tensor"),
            P(None, None, "dp"),
            P(None, None, "dp"),
            P(None, "dp"),
            P(None, "dp"),
            P(None, "dp"),
            P(None, "dp"),
        ),
        check_vma=False,
    )
```

profile of v0, /device:TPU:0, one launch (start us, length us, event | category | flops | bytes accessed | tf_op | source)
XLA Modules:
  0.0 2248.3 jit_solution(12429363653382114276)
XLA Ops:
  11.7 27.8 %all-gather = bf16[8,320,2]{1,2,0:T(2,128)(2,1)S(1)} all-gather(bf16[1,320,2]{1,2,0:T(2,128)(2,1)S(1)} %get-tuple-element.514), channel_id=1, replica_groups=mesh['dp'=8,'tensor'=4] {'dp'}, dimensions={0}, use_global_device_ids=true | all-gather | bytes 11520 | tf_op jit(solution)/shard_map/all_gather | solution.py:222
  48.8 19.5 all-gather.15.cloned.1.call-done
  68.2 5.8 copy.176
  74.1 35.4 %all-gather.11.cloned.1.call-done = bf16[1024,2560]{1,0:T(8,128)(2,1)} async-done(((bf16[256,2560]{1,0:T(8,128)(2,1)}), bf16[1024,2560]{1,0:T(8,128)(2,1)}) %all-gather.11.cloned.1.call-update) | async-done | bytes 5242896 | tf_op jit(solution)/shard_map/all_gather | solution.py:242
  113.9 60.3 %all-gather.13.cloned.1.call-done = bf16[2560,640]{1,0:T(8,128)(2,1)} async-done(((bf16[320,640]{1,0:T(8,128)(2,1)}), bf16[2560,640]{1,0:T(8,128)(2,1)}) %all-gather.13.cloned.1.call-update) | async-done | bytes 3276816 | tf_op jit(solution)/shard_map/all_gather | solution.py:217
  174.2 6.6 fusion.105
  182.7 34.8 %while.28 = (s32[]{:T(128)}, bf16[2,512,2,4,80]{1,4,3,2,0:T(8,128)(2,1)S(1)}, f32[2,2,4,512]{3,2,1,0:T(4,128)S(1)}, s32[2]{0:T(128)S(1)}, s32[1024]{0:T(1024)S(1...) while((s32[]{:T(128)}, ...), condition=%wide.region_7.8_spmd.clone, body=%wide.region_4.7_spmd.clone.sunk | while | flops 1394078208 | bytes 55195832 | solution.py:112
  219.3 18.1 all-gather.17.cloned.1.call-done
  237.4 8.0 convolution_convert_fusion.2
  249.6 45.9 %reduce-scatter.5.cloned.1.call-done = bf16[256,2560]{1,0:T(8,128)(2,1)} async-done(((bf16[1024,2560]{1,0:T(8,128)(2,1)}), bf16[256,2560]{1,0:T(8,128)(2,1)}) %reduce-scatter.5.cloned.1.call-update) | async-done | bytes 1310736 | tf_op jit(solution)/shard_map/reduce_scatter | solution.py:256
  299.9 350.4 %all-gather.21.cloned.1.call-done = bf16[2560,2,1792]{2,0,1:T(8,128)(2,1)} async-done(((bf16[320,2,1792]{2,0,1:T(8,128)(2,1)}), bf16[2560,2,1792]{2,0,1:T(8,128)(2,1)}) %all-gather.21.cloned.1.call-update) | async-done | bytes 18350096 | tf_op jit(solution)/shard_map/all_gather | solution.py:220
  650.3 25.5 %copy.179 = bf16[2560,2,1792]{0,2,1:T(8,128)(2,1)} copy(bf16[2560,2,1792]{2,0,1:T(8,128)(2,1)} %all-gather.21.cloned.1.call-done) | data formatting | bytes 36700160 | tf_op jit(solution)/shard_map/all_gather | solution.py:220
  675.8 17.1 all-gather.19.cloned.1.call-done
  692.9 27.5 %fusion.52 = f32[1024,2,1792]{2,0,1:T(8,128)} fusion(bf16[2560,2,1792]{0,2,1:T(8,128)(2,1)} %copy.179, bf16[1024,2560]{1,0:T(8,128)(2,1)} %all-gather.19.cloned.1.call-done), kind=kOutput, calls=%fused_computation.63 | convolution fusion | flops 18790481920 | bytes 38273024 | tf_op jit(solution)/shard_map/dot_general | solution.py:25
  720.4 7.8 multiply_convert_fusion
  728.2 6.9 all-gather.25.cloned.1.call-done
  735.0 15.1 fusion.55
  750.2 12.7 copy.192
  772.1 196.8 %all-to-all-done.4 = bf16[8,320,1792]{2,1,0:T(8,128)(2,1)} async-done(((bf16[8,320,1792]{2,1,0:T(8,128)(2,1)}), bf16[8,320,1792]{2,1,0:T(8,128)(2,1)}, u32[]{:S(2)}, u32[]{:S(2)}) %all-to-all-start.4) | async-done | bytes 9175072 | tf_op jit(solution)/shard_map/all_to_all | solution.py:298
  968.8 9.6 convert_reduce_fusion.1
  978.4 18.2 multiply_reduce_fusion.1
  1000.8 132.9 %all-gather.23.cloned.1.call-done = bf16[2560,1792]{1,0:T(8,128)(2,1)} async-done(((bf16[320,1792]{1,0:T(8,128)(2,1)}), bf16[2560,1792]{1,0:T(8,128)(2,1)}) %all-gather.23.cloned.1.call-update) | async-done | bytes 9175056 | tf_op jit(solution)/shard_map/all_gather | solution.py:221
  1133.8 19.1 multiply_bitcast_fusion.1
  1155.9 23.0 %bitcast_convert_fusion = bf16[1024,2560]{1,0:T(8,128)(2,1)} fusion(bf16[2560,2,1792]{2,0,1:T(8,128)(2,1)} %all-gather.21.cloned.1.call-done, bf16[1024,1,1792]{2,0,1:T(8,128)(2,1)S(1)} %get-tuple-element.490, bf16[1024,1,1792]{2,0,1:T(8,128)(2,1)S(1)} %get-tuple-element.489), kind=kOutput, calls=%fused_computation.73 | convolution fusion | flops 18796773376 | bytes 30932992 | tf_op jit(solution)/shard_map/dot_general | solution.py:29
  1179.2 49.5 %reduce-scatter.9.cloned.1.call-done = bf16[256,2560]{1,0:T(8,128)(2,1)} async-done(((bf16[1024,2560]{1,0:T(8,128)(2,1)}), bf16[256,2560]{1,0:T(8,128)(2,1)}) %reduce-scatter.9.cloned.1.call-update) | async-done | bytes 1310736 | tf_op jit(solution)/shard_map/reduce_scatter | solution.py:306
  1234.9 8.0 copy.181
  1242.9 32.6 %all-gather.27.cloned.1.call-done = bf16[1024,2560]{1,0:T(8,128)(2,1)} async-done(((bf16[256,2560]{1,0:T(8,128)(2,1)}), bf16[1024,2560]{1,0:T(8,128)(2,1)}) %all-gather.27.cloned.1.call-update) | async-done | bytes 5242896 | tf_op jit(solution)/shard_map/all_gather | solution.py:316
  1275.5 8.1 convolution_convert_fusion.7
  1283.6 148.4 %while.29 = (s32[]{:T(128)}, f32[1024,2,80]{0,2,1:T(8,128)}, f32[1024,2,80]{0,2,1:T(8,128)}, f32[2,512,2,4,80]{1,0,4,3,2:T(2,128)}, s32[2]{0:T(128)S(1)}, /*inde...) while((s32[]{:T(128)}, f32[1024,2,80]{0,2,1:T(8,128)}, ...), condition=%wide.region_15.16_spmd.clone, body=%wide.region_13.15_spmd.clone.sunk | while | flops 3421073920 | bytes 243595680 | solution.py:152
  1292.3 12.0 fusion.166
  1304.3 10.8 fusion.167
  1315.1 6.3 fusion.168
  1321.4 8.3 fusion.169
  1333.7 24.2 %dynamic_update_slice.21 = f32[2,512,2,4,80]{1,0,4,3,2:T(2,128)} dynamic-update-slice(f32[2,512,2,4,80]{1,0,4,3,2:T(2,128)} %get-tuple-element.693, f32[1,512,2,4,80]{1,0,4,3,2:T(1,128)S(1)} %copy.253, s32[]{:T(128)S(6)} %copy.270, s32[]{:T(128)} %constant.49.clone.1..sunk.1, s32[]{:T(128)} %constant.49.clone.1..sunk.1, s32[]{:T(128)} %constant.49.clone.1..sunk.1, s32[]{:T(128)} %constant.49.clone.1..sunk.1) | dynamic-update-slice | bytes 2621444 | tf_op jit(solution)/shard_map/while/body/jit(dynamic_update_index_in_dim)/dynamic_update_slice | solution.py:112
  1366.2 12.0 fusion.166
  1378.2 10.8 fusion.167
  1389.0 6.3 fusion.168
  1395.3 8.3 fusion.169
  1407.6 24.2 %dynamic_update_slice.21 = f32[2,512,2,4,80]{1,0,4,3,2:T(2,128)} dynamic-update-slice(f32[2,512,2,4,80]{1,0,4,3,2:T(2,128)} %get-tuple-element.693, f32[1,512,2,4,80]{1,0,4,3,2:T(1,128)S(1)} %copy.253, s32[]{:T(128)S(6)} %copy.270, s32[]{:T(128)} %constant.49.clone.1..sunk.1, s32[]{:T(128)} %constant.49.clone.1..sunk.1, s32[]{:T(128)} %constant.49.clone.1..sunk.1, s32[]{:T(128)} %constant.49.clone.1..sunk.1) | dynamic-update-slice | bytes 2621444 | tf_op jit(solution)/shard_map/while/body/jit(dynamic_update_index_in_dim)/dynamic_update_slice | solution.py:112
  1435.3 7.3 convolution_convert_fusion.6
  1453.7 6.9 fusion.106
  1460.6 5.7 convolution_convert_fusion.5
  1466.3 27.7 %all-to-all-done.1 = bf16[8,320,2,160]{1,3,2,0:T(8,128)(2,1)} async-done(((bf16[8,320,2,160]{1,3,2,0:T(8,128)(2,1)}), bf16[8,320,2,160]{1,3,2,0:T(8,128)(2,1)}, u32[]{:S(2)}, u32[]{:S(2)}) %all-to-all-start.1) | async-done | bytes 1638432 | tf_op jit(solution)/shard_map/all_to_all | solution.py:362
  1497.7 10.0 add_convert_fusion
  1507.7 8.2 copy.183
  1515.9 10.0 convolution_convert_fusion.4
  1526.0 45.4 %all-to-all-done = bf16[8,320,640]{2,1,0:T(8,128)(2,1)S(1)} async-done(((bf16[8,320,640]{2,1,0:T(8,128)(2,1)}), bf16[8,320,640]{2,1,0:T(8,128)(2,1)S(1)}, u32[]{:S(2)}, u32[]{:S(2)}) %all-to-all-start) | async-done | bytes 3276832 | tf_op jit(solution)/shard_map/all_to_all | solution.py:355
  1575.8 7.9 copy.186
  1583.7 6.9 maximum_convert_fusion
  1590.6 10.0 copy.187
  1603.6 45.2 %all-to-all-done.2 = bf16[8,320,640]{2,1,0:T(8,128)(2,1)} async-done(((bf16[8,320,640]{2,1,0:T(8,128)(2,1)}), bf16[8,320,640]{2,1,0:T(8,128)(2,1)}, u32[]{:S(2)}, u32[]{:S(2)}) %all-to-all-start.2) | async-done | bytes 3276832 | tf_op jit(solution)/shard_map/all_to_all | solution.py:369
  1652.9 26.8 %convolution_convert_fusion = bf16[8,320,2,1792]{3,1,2,0:T(8,128)(2,1)} fusion(bf16[8,320,1024,1]{2,1,3,0:T(8,128)(2,1)} %bitcast.323, bf16[1024,2,1792]{0,2,1:T(8,128)(2,1)} %copy.187), kind=kOutput, calls=%fused_computation.71 | convolution fusion | flops 18799656960 | bytes 30932992 | tf_op jit(solution)/shard_map/dot_general | solution.py:35
  1679.7 6.0 all-to-all-start.3
  1685.8 15.0 convolution_convert_fusion.3
  1736.4 16.4 reduce-scatter.7.cloned.1.call-done
  1758.2 10.9 psum.7
  1770.4 312.0 %all-to-all-done.3 = bf16[8,320,2,1792]{3,1,2,0:T(8,128)(2,1)} async-done(((bf16[8,320,2,1792]{3,1,2,0:T(8,128)(2,1)}), bf16[8,320,2,1792]{3,1,2,0:T(8,128)(2,1)}, u32[]{:S(2)}, u32[]{:S(2)}) %all-to-all-start.3) | async-done | bytes 18350112 | tf_op jit(solution)/shard_map/all_to_all | solution.py:291
  2082.3 17.5 convert_reduce_fusion
  2099.8 37.0 %multiply_reduce_fusion = (f32[320,2,1792]{2,0,1:T(8,128)S(1)}, f32[4,320,2,1792]{3,1,2,0:T(8,128)}, f32[4,320,2,1792]{3,1,2,0:T(8,128)}) fusion(f32[320,2,1792]{2,0,1:T(8,128)} %copy.189, f32[4,320,2,1792]{3,1,2,0:T(8,128)} %convert_reduce_fusion, f32[4,320,2,1792]{3,2,1,0:T(2,128)} %param.49, f32[4,320,2,1792]{3,2,1,0:T(2,128)} %param.43), kind=kLoop, calls=%fused_computation.68 | loop fusion | flops 63078400 | bytes 100925440 | tf_op jit(solution)/shard_map/reduce_sum | solution.py:180
  2136.8 37.6 %copy.194 = f32[4,320,2,1792]{3,2,1,0:T(2,128)} copy(f32[4,320,2,1792]{3,1,2,0:T(8,128)} %get-tuple-element.463) | data formatting | bytes 36700160
  2174.4 37.5 %copy.195 = f32[4,320,2,1792]{3,2,1,0:T(2,128)} copy(f32[4,320,2,1792]{3,1,2,0:T(8,128)} %get-tuple-element.462) | data formatting | bytes 36700160
  2211.9 6.4 fusion.96
  2218.3 8.1 copy.196
  2226.5 5.7 copy.197
  (306 shorter events, 185.4 us)
Async XLA Ops:
  7.2 35.9 %copy-start.2 = (bf16[256,2560]{1,0:T(8,128)(2,1)S(1)}, bf16[256,2560]{1,0:T(8,128)(2,1)}, u32[]{:S(2)}) copy-start(bf16[256,2560]{1,0:T(8,128)(2,1)} %param.31) | copy-start | bytes 3932164
  7.2 61.0 %all-gather.15.cloned.1.call-start = ((), (), s32[]{:S(2)}) async-start(), calls=%async_computation.12 | async-start | bytes 2949120 | tf_op jit(solution)/shard_map/all_gather | solution.py:218
  9.4 35.2 %copy-start.22 = (f32[320,640]{1,0:T(8,128)S(1)}, f32[320,640]{1,0:T(8,128)}, u32[]{:S(2)}) copy-start(f32[320,640]{1,0:T(8,128)} %param.34) | copy-start | bytes 2457604
  10.4 99.1 %all-gather.11.cloned.1.call-start = ((), (), s32[]{:S(2)}) async-start(), calls=%async_computation.10 | async-start | bytes 6553600 | tf_op jit(solution)/shard_map/all_gather | solution.py:242
  44.6 129.7 %all-gather.13.cloned.1.call-start = ((), (), s32[]{:S(2)}) async-start(), calls=%async_computation.11 | async-start | bytes 3686400 | tf_op jit(solution)/shard_map/all_gather | solution.py:217
  45.8 191.7 %all-gather.17.cloned.1.call-start = ((), (), s32[]{:S(2)}) async-start(), calls=%async_computation.13 | async-start | bytes 3686400 | tf_op jit(solution)/shard_map/all_gather | solution.py:219
  47.0 248.6 %reduce-scatter.5.cloned.1.call-start = ((), (), s32[]{:S(2)}) async-start(), calls=%async_computation.14 | async-start | bytes 6553600 | tf_op jit(solution)/shard_map/reduce_scatter | solution.py:256
  48.8 132.5 %copy-start.18 = (f32[1024,40]{0,1:T(8,128)}, f32[1024,40]{0,1:T(8,128)S(1)}, u32[]{:S(2)}) copy-start(f32[1024,40]{0,1:T(8,128)S(1)} %get-tuple-element.512) | copy-start | bytes 491524
  74.0 39.8 %copy-start.17 = (bf16[2560,2,160]{0,2,1:T(8,128)(2,1)}, bf16[2560,2,160]{0,2,1:T(8,128)(2,1)S(1)}, u32[]{:S(2)}) copy-start(bf16[2560,2,160]{0,2,1:T(8,128)(2,1)S(1)} %copy.176) | copy-start | bytes 4915204
  217.5 27.9 %copy-start.1 = (bf16[1024,2,4,80]{0,3,2,1:T(8,128)(2,1)}, bf16[1024,2,4,80]{0,3,2,1:T(8,128)(2,1)S(1)}, u32[]{:S(2)}) copy-start(bf16[1024,2,4,80]{0,3,2,1:T(8,128)(2,1)S(1)} %get-tuple-element.731) | copy-start | bytes 3932164
  217.6 27.8 %copy-start.5 = (bf16[1024,2,80]{0,2,1:T(8,128)(2,1)}, bf16[1024,2,80]{0,2,1:T(8,128)(2,1)S(1)}, u32[]{:S(2)}) copy-start(bf16[1024,2,80]{0,2,1:T(8,128)(2,1)S(1)} %get-tuple-element.732) | copy-start | bytes 983044
  217.6 27.8 %copy-start.12 = (bf16[1024,2,80]{0,2,1:T(8,128)(2,1)}, bf16[1024,2,80]{0,2,1:T(8,128)(2,1)S(1)}, u32[]{:S(2)}) copy-start(bf16[1024,2,80]{0,2,1:T(8,128)(2,1)S(1)} %get-tuple-element.742) | copy-start | bytes 983044
  217.6 27.8 %copy-start.40 = (s32[1024]{0:T(1024)}, s32[1024]{0:T(1024)S(1)}, u32[]{:S(2)}) copy-start(s32[1024]{0:T(1024)S(1)} %get-tuple-element.778) | copy-start | bytes 12292
  217.6 27.8 %copy-start.49 = (f32[2,2,4,512]{3,2,1,0:T(4,128)}, f32[2,2,4,512]{3,2,1,0:T(4,128)S(1)}, u32[]{:S(2)}) copy-start(f32[2,2,4,512]{3,2,1,0:T(4,128)S(1)} %get-tuple-element.684) | copy-start | bytes 98308
  217.6 27.8 %copy-start.69 = (s32[2]{0:T(128)}, s32[2]{0:T(128)S(1)}, u32[]{:S(2)}) copy-start(s32[2]{0:T(128)S(1)} %get-tuple-element.784) | copy-start | bytes 28
  219.3 26.1 %copy-start.38 = (bf16[80,8,2,512]{3,1,2,0:T(8,128)(2,1)}, bf16[80,8,2,512]{3,1,2,0:T(8,128)(2,1)S(1)}, u32[]{:S(2)}) copy-start(bf16[80,8,2,512]{3,1,2,0:T(8,128)(2,1)S(1)} %copy.233) | copy-start | bytes 3932164
  245.5 50.1 %copy-start.3 = (bf16[256,2560]{1,0:T(8,128)(2,1)S(1)}, bf16[256,2560]{1,0:T(8,128)(2,1)}, u32[]{:S(2)}) copy-start(bf16[256,2560]{1,0:T(8,128)(2,1)} %param.31) | copy-start | bytes 3932164
  245.5 404.8 %all-gather.21.cloned.1.call-start = ((), (), s32[]{:S(2)}) async-start(), calls=%async_computation.16 | async-start | bytes 20643840 | tf_op jit(solution)/shard_map/all_gather | solution.py:220
  249.6 48.0 %copy-start.47 = (f32[2560]{0:T(1024)S(1)}, f32[2560]{0:T(1024)}, u32[]{:S(2)}) copy-start(f32[2560]{0:T(1024)} %get-tuple-element.405) | copy-start | bytes 30724
  249.6 443.4 %all-gather.19.cloned.1.call-start = ((), (), s32[]{:S(2)}) async-start(), calls=%async_computation.15 | async-start | bytes 6553600 | tf_op jit(solution)/shard_map/all_gather | solution.py:265
  297.5 934.6 %copy-start.52 = (f32[256]{0:T(256)}, f32[256]{0:T(256)S(1)}, u32[]{:S(2)}) copy-start(f32[256]{0:T(256)S(1)} %get-tuple-element.518) | copy-start | bytes 3076
  297.5 934.6 %copy-start.61 = (f32[256]{0:T(256)}, f32[256]{0:T(256)S(1)}, u32[]{:S(2)}) copy-start(f32[256]{0:T(256)S(1)} %get-tuple-element.517) | copy-start | bytes 3076
  299.2 435.9 %all-gather.25.cloned.1.call-start = ((), (), s32[]{:S(2)}) async-start(), calls=%async_computation.19 | async-start | bytes 6553600 | tf_op jit(solution)/shard_map/all_gather | solution.py:279
  762.9 206.0 %all-to-all-start.4 = ((bf16[8,320,1792]{2,1,0:T(8,128)(2,1)}), bf16[8,320,1792]{2,1,0:T(8,128)(2,1)}, u32[]{:S(2)}, u32[]{:S(2)}) async-start(bf16[8,320,1792]{2,1,0:T(8,128)(2,1)} %bitcast.312), calls=%async_computation.8 | async-start | bytes 18350080 | tf_op jit(solution)/shard_map/all_to_all | solution.py:298
  768.4 365.4 %all-gather.23.cloned.1.call-start = ((), (), s32[]{:S(2)}) async-start(), calls=%async_computation.17 | async-start | bytes 10321920 | tf_op jit(solution)/shard_map/all_gather | solution.py:221
  978.4 18.2 copy-start.15
  978.4 18.2 copy-start.33
  1000.6 228.0 %reduce-scatter.9.cloned.1.call-start = ((), (), s32[]{:S(2)}) async-start(), calls=%async_computation.20 | async-start | bytes 6553600 | tf_op jit(solution)/shard_map/reduce_scatter | solution.py:306
  1178.9 96.5 %all-gather.27.cloned.1.call-start = ((), (), s32[]{:S(2)}) async-start(), calls=%async_computation.21 | async-start | bytes 6553600 | tf_op jit(solution)/shard_map/all_gather | solution.py:316
  1242.9 40.7 %copy-start.6 = (bf16[1024,2,80]{0,2,1:T(8,128)(2,1)S(1)}, bf16[1024,2,80]{0,2,1:T(8,128)(2,1)}, u32[]{:S(2)}) copy-start(bf16[1024,2,80]{0,2,1:T(8,128)(2,1)} %copy-done.5) | copy-start | bytes 983044
  1242.9 40.7 %copy-start.41 = (s32[1024]{0:T(1024)S(1)}, s32[1024]{0:T(1024)}, u32[]{:S(2)}) copy-start(s32[1024]{0:T(1024)} %copy-done.40) | copy-start | bytes 12292
  1242.9 40.7 %copy-start.70 = (s32[2]{0:T(128)S(1)}, s32[2]{0:T(128)}, u32[]{:S(2)}) copy-start(s32[2]{0:T(128)} %copy-done.69) | copy-start | bytes 28
  1283.6 148.4 %copy-start.19 = (f32[1024,40]{0,1:T(8,128)S(1)}, f32[1024,40]{0,1:T(8,128)}, u32[]{:S(2)}) copy-start(f32[1024,40]{0,1:T(8,128)} %copy-done.18) | copy-start | bytes 491524
  1290.2 14.1 copy-start
  1315.1 14.6 slice-start
  1321.4 8.3 slice-start.1
  1364.1 14.1 copy-start
  1388.9 14.6 slice-start
  1395.3 8.3 slice-start.1
  1442.6 51.5 %all-to-all-start.1 = ((bf16[8,320,2,160]{1,3,2,0:T(8,128)(2,1)}), bf16[8,320,2,160]{1,3,2,0:T(8,128)(2,1)}, u32[]{:S(2)}, u32[]{:S(2)}) async-start(bf16[8,320,2,160]{1,3,2,0:T(8,128)(2,1)} %convolution_convert_fusion.6), calls=%async_computation.5 | async-start | bytes 3932160 | tf_op jit(solution)/shard_map/all_to_all | solution.py:362
  1494.0 77.3 %all-to-all-start = ((bf16[8,320,640]{2,1,0:T(8,128)(2,1)}), bf16[8,320,640]{2,1,0:T(8,128)(2,1)S(1)}, u32[]{:S(2)}, u32[]{:S(2)}) async-start(bf16[8,320,640]{2,1,0:T(8,128)(2,1)} %convolution_convert_fusion.5), calls=%async_computation.4 | async-start | bytes 6553600 | tf_op jit(solution)/shard_map/all_to_all | solution.py:355
  1497.7 103.0 %reduce-scatter.11.cloned.1.call-start = ((), (), s32[]{:S(2)}) async-start(), calls=%async_computation.22 | async-start | bytes 6553600 | tf_op jit(solution)/shard_map/reduce_scatter | solution.py:342
  1571.4 77.5 %all-to-all-start.2 = ((bf16[8,320,640]{2,1,0:T(8,128)(2,1)}), bf16[8,320,640]{2,1,0:T(8,128)(2,1)}, u32[]{:S(2)}, u32[]{:S(2)}) async-start(bf16[8,320,640]{2,1,0:T(8,128)(2,1)} %convolution_convert_fusion.4), calls=%async_computation.6 | async-start | bytes 6553600 | tf_op jit(solution)/shard_map/all_to_all | solution.py:369
  1590.6 10.1 copy-start.54
  1590.6 10.1 copy-start.4
  1590.6 10.1 copy-start.51
  1590.6 10.1 copy-start.56
  1648.8 30.9 %all-to-all-start.5 = ((bf16[8,2,320]{2,1,0:T(2,128)(2,1)}), bf16[8,2,320]{2,1,0:T(2,128)(2,1)S(1)}, u32[]{:S(2)}, u32[]{:S(2)}) async-start(bf16[8,2,320]{2,1,0:T(2,128)(2,1)} %copy.193), calls=%async_computation.9 | async-start | bytes 24576 | tf_op jit(solution)/shard_map/all_to_all | solution.py:376
  1679.7 402.6 %all-to-all-start.3 = ((bf16[8,320,2,1792]{3,1,2,0:T(8,128)(2,1)}), bf16[8,320,2,1792]{3,1,2,0:T(8,128)(2,1)}, u32[]{:S(2)}, u32[]{:S(2)}) async-start(bf16[8,320,2,1792]{3,1,2,0:T(8,128)(2,1)} %convolution_convert_fusion), calls=%async_computation.7 | async-start | bytes 36700160 | tf_op jit(solution)/shard_map/all_to_all | solution.py:291
  1685.7 67.0 %reduce-scatter.7.cloned.1.call-start = ((), (), s32[]{:S(2)}) async-start(), calls=%async_computation.18 | async-start | bytes 6553600 | tf_op jit(solution)/shard_map/reduce_scatter | solution.py:272
  1734.5 18.2 copy-start.8
  1734.5 18.2 copy-start.48
  1734.5 18.2 copy-start.53
  1734.5 18.2 copy-start.62
  1734.5 18.2 copy-start.64
  1734.6 18.2 copy-start.65
  1752.8 16.3 copy-start.57
  1752.8 16.3 copy-start.59
  1752.8 16.3 copy-start.60
  1752.8 16.9 copy-start.58
  1752.9 16.9 copy-start.66
  2136.8 75.1 %slice-start.2 = ((s8[4587520]{0:T(1024)(128)(4,1)}), s8[4194304]{0:T(1024)(128)(4,1)S(1)}, s32[]{:S(2)}) async-start(s8[4587520]{0:T(1024)(128)(4,1)} %bitcast.310), calls=%async_computation.25 | async-start | bytes 8388608
  2174.4 37.5 %slice-start.3 = ((s8[4587520]{0:T(1024)(128)(4,1)}), s8[393216]{0:T(1024)(128)(4,1)S(1)}, s32[]{:S(2)}) async-start(s8[4587520]{0:T(1024)(128)(4,1)} %bitcast.310), calls=%async_computation.26 | async-start | bytes 786432
  2218.3 8.1 copy-start.9
  (38 other events, 145.4 us)
Sparse Core Ops, SparseCore 0:
  10.8 57.3 all-gather.14
  70.4 39.0 all-gather.10
  112.2 61.9 all-gather.12
  176.8 60.5 all-gather.16
  245.6 49.9 reduce-scatter.4
  297.6 352.6 all-gather.20
  652.5 40.3 all-gather.18
  694.6 40.4 all-gather.24
  1000.7 132.9 all-gather.22
  1179.0 49.5 reduce-scatter.8
  1235.0 40.4 all-gather.26
  1507.9 51.7 reduce-scatter.10
  1700.9 51.8 reduce-scatter.6
where the time goes:
time: 2260 us; the launch traced here: 2250 us
  waiting for transfers between devices  1410 us (62%)
  matrix products  277 us (12%)
  local copies, waits for them, and re-layouts  256 us (11%)
  other arithmetic  209 us (9%)
  blocking collectives  38.7 us (2%)
  starting transfers between devices  30.5 us (1%)
    all_gather x1, waiting for transfers between devices, per_device(): lax.all_gather(gating_weight.astype(low_type), 'dp', axis=0, tiled=True)  350 us
    all_to_all x1, waiting for transfers between devices, per_device(): lax.all_to_all(to_sources(grad_gating, pieces).astype(jnp.bfloat16), 'dp'...  312 us
    all_to_all x1, waiting for transfers between devices, per_device(): lax.all_to_all(to_sources(grad_down, pieces).astype(jnp.bfloat16), 'dp',...  197 us
    all_gather x1, waiting for transfers between devices, per_device(): lax.all_gather(down_weight.astype(low_type), 'dp', axis=0, tiled=True)  133 us
    unnamed x151, local copies, waits for them, and re-layouts  113 us
    reduce_sum x6, other arithmetic, optimize(): delta = jnp.mean(rate * direction, axis=0)  68.6 us
    dot_general x5, matrix products, matmul_plain(): return jnp.dot(left, right, preferred_element_type=jnp.float32)  65.6 us
    dot_general x5, matrix products, matmul_left_t(): lax.dot_general(left, right, (((0,), (0,)), ((), ())), preferred_element_...  65 us
  transfers between devices with their start and end apart: 19, of which 17 were waited for; matrix products, arithmetic and copies ran while one was open for 13% of the time, Pallas kernels for 0%

commit v1 on v0

v1 whole, which is shorter than its diff:
```python
import functools
import math

import jax
import jax.numpy as jnp
import numpy as np
from jax import lax
from jax.experimental import pallas as pl
from jax.experimental.pallas import tpu as pltpu
from jax.sharding import Mesh, PartitionSpec as P

HEAD_WIDTH = 80
REPLICA_GROUPS = 4
STEP = 8
LANES = 128
HEADS = 4
TILE = 256
PACK = 512
WIDE = 768
HALF = 64
VMEM_BYTES = 58 * 2**20

epsilon = 1e-05
rope_base = 1000000.0
beta_one = 0.9
beta_two = 0.95
adam_epsilon = 1e-08
outer_mu = 0.9
outer_rate = 0.7
inner_rates = (0.05, 0.05, 0.2, 0.05, 0.05, 0.5)
inner_decays = (0.1, 0.1, 0.1, 0.1, 0.1, 0.0)
correct_one = 1.0 - beta_one**STEP
correct_two = 1.0 - beta_two**STEP

low_type = jnp.bfloat16
f32 = jnp.float32

NN = (((1,), (0,)), ((), ()))
NT = (((1,), (1,)), ((), ()))
TN = (((0,), (0,)), ((), ()))

CHUNKS = ((0, 3), (3, 7))


def after(value, *earlier):
    return lax.optimization_barrier((value, earlier))[0]


def dot(left, right, dims=NN):
    return lax.dot_general(left, right, dims, preferred_element_type=f32)


def params(**kwargs):
    return pltpu.CompilerParams(vmem_limit_bytes=VMEM_BYTES, **kwargs)


def cost(flops, size):
    return pl.CostEstimate(flops=int(flops), bytes_accessed=int(size), transcendentals=0)


SHORT = pl.CostEstimate(flops=1, bytes_accessed=1, transcendentals=0)


def resident(shape):
    zeros = (0,) * len(shape)
    return pl.BlockSpec(shape, lambda *_: zeros, pipeline_mode=pl.Buffered(1))


def projection_selector():
    table = np.zeros((PACK, WIDE), np.float32)
    for head in range(HEADS + 1):
        for place in range(HEAD_WIDTH):
            half, rest = divmod(place, HEAD_WIDTH // 2)
            table[head * HEAD_WIDTH + place, head * LANES + half * HALF + rest] = 1.0
    for place in range(HEAD_WIDTH):
        table[(HEADS + 1) * HEAD_WIDTH + place, (HEADS + 1) * LANES + place] = 1.0
    return table


def output_selector():
    table = np.zeros((HEADS * HEAD_WIDTH, HEADS * LANES), np.float32)
    for head in range(HEADS):
        for place in range(HEAD_WIDTH):
            table[head * HEAD_WIDTH + place, head * LANES + place] = 1.0
    return table


def gains_selector():
    table = np.zeros((8, PACK), np.float32)
    table[0, (HEADS + 2) * HEAD_WIDTH] = 1.0
    table[1, (HEADS + 2) * HEAD_WIDTH + 1] = 1.0
    return table


def seen_from(place_ref, piece):
    return lax.bitwise_xor(piece, place_ref[3])


def piece_specs(width, piece):
    return [pl.BlockSpec((TILE, width), lambda *at: (lax.shift_right_logical(piece(*at), 1), 0))] * 2


def piece_shapes(total, width):
    return [jax.ShapeDtypeStruct((total // 2, width), low_type)] * 2


def write_piece(piece, kept, sent, value):
    odd = lax.bitwise_and(piece, 1)

    @pl.when(odd == 0)
    def _():
        kept[...] = value

    @pl.when(odd == 1)
    def _():
        sent[...] = value


def first_row(place, step, blocks, rows):
    return pl.multiple_of(lax.rem(place - step + blocks, blocks) * rows, LANES if blocks > 1 else rows)


def assemble(place, blocks, target):
    rows = blocks[0].shape[0]
    for step, block in enumerate(blocks):
        target[pl.ds(first_row(place, step, len(blocks), rows), rows), :] = block[...]


def projection_kernel(count, place_ref, tokens, *refs):
    blocks, (select, pick, cosine, sine, normed, heads, gains, wide) = refs[:count], refs[count:]

    @pl.when(pl.program_id(0) == 0)
    def _():
        rows = blocks[0].shape[0]
        for step, block in enumerate(blocks):
            start = first_row(place_ref[0], step, count, rows)
            value = block[...]
            wide[pl.ds(start, rows), :] = dot(value, select[...]).astype(low_type)
            gains[:, pl.ds(start, rows)] = dot(pick[...], value, NT)

    value = tokens[...].astype(f32)
    inverse = lax.rsqrt(jnp.mean(value * value, axis=-1, keepdims=True) + epsilon)
    low = (value * inverse * gains[0:1, :]).astype(low_type)
    normed[...] = low
    result = dot(low, wide[...])
    cos_tile = cosine[...]
    sin_tile = sine[...]
    for head in range(HEADS + 1):
        part = result[:, head * LANES : (head + 1) * LANES]
        turned = part * cos_tile + pltpu.roll(part, HALF, 1) * sin_tile
        heads[:, head * LANES : (head + 1) * LANES] = turned.astype(low_type)
    heads[:, (HEADS + 1) * LANES :] = result[:, (HEADS + 1) * LANES :].astype(low_type)


def project(place, tokens, blocks, cosine, sine):
    total, width = tokens.shape
    tile = lambda columns: pl.BlockSpec((TILE, columns), lambda i, p: (i, 0))
    return pl.pallas_call(
        functools.partial(projection_kernel, len(blocks)),
        grid_spec=pltpu.PrefetchScalarGridSpec(
            num_scalar_prefetch=1,
            grid=(total // TILE,),
            in_specs=[tile(width)]
            + [resident((block.shape[0], PACK)) for block in blocks]
            + [
                resident((PACK, WIDE)),
                resident((8, PACK)),
                tile(LANES),
                tile(LANES),
            ],
            out_specs=[
                tile(width),
                tile(WIDE),
                pl.BlockSpec((8, width), lambda *_: (0, 0)),
                pl.BlockSpec((width, WIDE), lambda *_: (0, 0)),
            ],
        ),
        out_shape=[
            jax.ShapeDtypeStruct((total, width), low_type),
            jax.ShapeDtypeStruct((total, WIDE), low_type),
            jax.ShapeDtypeStruct((8, width), f32),
            jax.ShapeDtypeStruct((width, WIDE), low_type),
        ],
        compiler_params=params(),
        cost_estimate=cost(2 * total * width * WIDE, 4 * total * width + 3 * width * WIDE * 2),
        name="projection",
    )(
        place,
        tokens,
        *blocks,
        jnp.asarray(projection_selector(), low_type),
        jnp.asarray(gains_selector(), low_type),
        cosine,
        sine,
    )


SCORE_SCALE = math.log2(math.e) / math.sqrt(HEAD_WIDTH)
GRAD_SCALE = 1.0 / math.sqrt(HEAD_WIDTH)


def allowed_pairs(block, width, starts):
    key_index = lax.broadcasted_iota(jnp.int32, (width, TILE), 0)
    row_index = block * TILE + lax.broadcasted_iota(jnp.int32, (1, TILE), 1)
    return (key_index >= starts) & (key_index <= row_index)


def widen_output(place_ref, blocks, select, wide):
    @pl.when((pl.program_id(0) == 0) & (pl.program_id(1) == 0))
    def _():
        rows = blocks[0].shape[0]
        for step, block in enumerate(blocks):
            start = first_row(place_ref[0], step, len(blocks), rows)
            value = block[:, PACK:]
            wide[pl.ds(start, rows), :] = dot(value, select[...]).astype(low_type)


def attention_kernel(count, blocks_per, place_ref, query, key, value, starts, *refs):
    blocks, (select, mixed, totals, kept, sent, wide) = refs[:count], refs[count:]
    widen_output(place_ref, blocks, select, wide)

    for block in range(blocks_per):

        @pl.when(pl.program_id(1) == block)
        def _(block=block):
            width = (block + 1) * TILE
            allowed = allowed_pairs(block, width, starts[0:1, :])
            keys = key[0:width, :]
            values = value[0:width, :]
            for head in range(HEADS):
                lanes = slice(head * LANES, (head + 1) * LANES)
                scores = dot(keys, query[:, lanes], NT) * SCORE_SCALE
                scores = jnp.where(allowed, scores, -1e30)
                top = jnp.max(scores, axis=0, keepdims=True)
                expo = jnp.exp2(scores - top)
                total = jnp.sum(expo, axis=0, keepdims=True)
                out = dot(values, expo.astype(low_type), TN) * (1.0 / total)
                mixed[:, lanes] = out.T.astype(low_type)
                totals[head : head + 1, :] = top + jnp.log2(total)

    piece = pl.program_id(0) * blocks_per + pl.program_id(1)
    value = dot(mixed[...], wide[...], NT).astype(low_type)
    write_piece(seen_from(place_ref, piece), kept, sent, value)


def attend(place, heads, starts, blocks, sequence):
    total = heads.shape[0]
    width = blocks[0].shape[0] * len(blocks)
    per = sequence // TILE
    tile = lambda size, column: pl.BlockSpec((TILE, size), lambda s, i, *_: (s * per + i, column))
    full = lambda column: pl.BlockSpec((sequence, LANES), lambda s, i, *_: (s, column))
    line = pl.BlockSpec((8, TILE), lambda s, i, *_: (0, s * per + i))
    return pl.pallas_call(
        functools.partial(attention_kernel, len(blocks), per),
        grid_spec=pltpu.PrefetchScalarGridSpec(
            num_scalar_prefetch=1,
            grid=(total // sequence, per),
            in_specs=[
                tile(HEADS * LANES, 0),
                full(HEADS),
                full(HEADS + 1),
                line,
            ]
            + [resident(block.shape) for block in blocks]
            + [resident((HEADS * HEAD_WIDTH, HEADS * LANES))],
            out_specs=[tile(HEADS * LANES, 0), line]
            + piece_specs(width, lambda s, i, p: seen_from(p, s * per + i)),
            scratch_shapes=[pltpu.VMEM((width, HEADS * LANES), low_type)],
        ),
        out_shape=[
            jax.ShapeDtypeStruct((total, HEADS * LANES), low_type),
            jax.ShapeDtypeStruct((8, total), f32),
        ]
        + piece_shapes(total, width),
        compiler_params=params(),
        cost_estimate=cost(20e9, 4 * total * width),
        name="attention",
    )(place, heads, heads, heads, starts, *blocks, jnp.asarray(output_selector(), low_type))


def attention_grad_kernel(
    count,
    blocks_per,
    place_ref,
    grad_hidden,
    query,
    key,
    value,
    totals,
    starts,
    cosine,
    sine,
    cos_all,
    sin_all,
    *refs,
):
    blocks, (select, grad_query, grad_pair, wide, key_sum, value_sum) = refs[:count], refs[count:]
    widen_output(place_ref, blocks, select, wide)

    @pl.when(pl.program_id(1) == 0)
    def _():
        key_sum[...] = jnp.zeros_like(key_sum)
        value_sum[...] = jnp.zeros_like(value_sum)

    grad_mixed = dot(grad_hidden[...], wide[...]).astype(low_type)
    cos_tile = cosine[...]
    sin_tile = sine[...]
    for block in range(blocks_per):

        @pl.when(pl.program_id(1) == block)
        def _(block=block):
            width = (block + 1) * TILE
            allowed = allowed_pairs(block, width, starts[0:1, :])
            keys = key[0:width, :]
            values = value[0:width, :]
            key_part = jnp.zeros((width, LANES), f32)
            value_part = jnp.zeros((width, LANES), f32)
            for head in range(HEADS):
                lanes = slice(head * LANES, (head + 1) * LANES)
                queries = query[:, lanes]
                grads = grad_mixed[:, lanes]
                scores = dot(keys, queries, NT) * SCORE_SCALE
                scores = jnp.where(allowed, scores, -1e30)
                prob = jnp.exp2(scores - totals[head : head + 1, :])
                grad_prob = dot(values, grads, NT)
                inner = jnp.sum(prob * grad_prob, axis=0, keepdims=True)
                grad_scores = (prob * (grad_prob - inner)).astype(low_type)
                key_part = key_part + dot(grad_scores, queries)
                value_part = value_part + dot(prob.astype(low_type), grads)
                turned = dot(keys, grad_scores, TN).T * GRAD_SCALE
                turned = turned * cos_tile - pltpu.roll(turned, HALF, 1) * sin_tile
                grad_query[:, lanes] = turned.astype(low_type)
            key_sum[0:width, :] += key_part
            value_sum[0:width, :] += value_part

    @pl.when(pl.program_id(1) == blocks_per - 1)
    def _():
        grad_key = key_sum[...] * GRAD_SCALE
        grad_key = grad_key * cos_all[...] - pltpu.roll(grad_key, HALF, 1) * sin_all[...]
        grad_pair[:, :LANES] = grad_key.astype(low_type)
        grad_pair[:, LANES:] = value_sum[...].astype(low_type)


def attend_grad(place, grad_hidden, heads, totals, starts, cosine, sine, blocks, sequence):
    total, width = grad_hidden.shape
    per = sequence // TILE
    tile = lambda size, column: pl.BlockSpec((TILE, size), lambda s, i, p: (s * per + i, column))
    full = lambda size, column: pl.BlockSpec((sequence, size), lambda s, i, p: (s, column))
    line = pl.BlockSpec((8, TILE), lambda s, i, p: (0, s * per + i))
    return pl.pallas_call(
        functools.partial(attention_grad_kernel, len(blocks), per),
        grid_spec=pltpu.PrefetchScalarGridSpec(
            num_scalar_prefetch=1,
            grid=(total // sequence, per),
            in_specs=[
                tile(width, 0),
                tile(HEADS * LANES, 0),
                full(LANES, HEADS),
                full(LANES, HEADS + 1),
                line,
                line,
                tile(LANES, 0),
                tile(LANES, 0),
                full(LANES, 0),
                full(LANES, 0),
            ]
            + [resident(block.shape) for block in blocks]
            + [resident((HEADS * HEAD_WIDTH, HEADS * LANES))],
            out_specs=[tile(HEADS * LANES, 0), full(2 * LANES, 0)],
            scratch_shapes=[
                pltpu.VMEM((width, HEADS * LANES), low_type),
                pltpu.VMEM((sequence, LANES), f32),
                pltpu.VMEM((sequence, LANES), f32),
            ],
        ),
        out_shape=[
            jax.ShapeDtypeStruct((total, HEADS * LANES), low_type),
            jax.ShapeDtypeStruct((total, 2 * LANES), low_type),
        ],
        compiler_params=params(),
        cost_estimate=cost(30e9, 4 * total * width),
        name="attention_grad",
    )(
        place,
        grad_hidden,
        heads,
        heads,
        heads,
        totals,
        starts,
        cosine,
        sine,
        cosine,
        sine,
        *blocks,
        jnp.asarray(output_selector(), low_type),
    )


def projection_grad_kernel(place_ref, grad_query, grad_pair, tokens, wide, kept, sent, gain_sums):
    grad = dot(grad_query[...], wide[:, : HEADS * LANES], NT)
    grad = grad + dot(grad_pair[...], wide[:, HEADS * LANES :], NT)
    write_piece(seen_from(place_ref, pl.program_id(0)), kept, sent, grad.astype(low_type))
    value = tokens[...].astype(f32)
    inverse = lax.rsqrt(jnp.mean(value * value, axis=-1, keepdims=True) + epsilon)
    product = grad * (value * inverse)
    sums = jnp.sum(product.reshape(TILE // 8, 8, product.shape[1]), axis=0)

    @pl.when(pl.program_id(0) == 0)
    def _():
        gain_sums[...] = sums

    @pl.when(pl.program_id(0) != 0)
    def _():
        gain_sums[...] += sums


def project_grad(place, grad_query, grad_pair, tokens, wide):
    total, width = tokens.shape
    tile = lambda columns: pl.BlockSpec((TILE, columns), lambda i, *_: (i, 0))
    return pl.pallas_call(
        projection_grad_kernel,
        grid_spec=pltpu.PrefetchScalarGridSpec(
            num_scalar_prefetch=1,
            grid=(total // TILE,),
            in_specs=[
                tile(HEADS * LANES),
                tile(2 * LANES),
                tile(width),
                resident((width, WIDE)),
            ],
            out_specs=piece_specs(width, lambda i, p: seen_from(p, i)) + [pl.BlockSpec((8, width), lambda i, *_: (0, 0))],
        ),
        out_shape=piece_shapes(total, width) + [jax.ShapeDtypeStruct((8, width), f32)],
        compiler_params=params(),
        cost_estimate=SHORT,
        name="projection_grad",
    )(place, grad_query, grad_pair, tokens, wide)


def pack_kernel(place_ref, gating, down, *outs):
    kept, sent = outs[: len(CHUNKS)], outs[len(CHUNKS) :]

    def write(targets):
        for (first, last), target in zip(CHUNKS, targets):
            count = last - first
            for tile in range(first, last):
                lanes = slice(tile * LANES, (tile + 1) * LANES)
                place = (tile - first) * 2 * LANES
                target[:, place : place + LANES] = gating[:, 0, lanes].astype(low_type)
                target[:, place + LANES : place + 2 * LANES] = gating[:, 1, lanes].astype(low_type)
                place = (2 * count + tile - first) * LANES
                target[:, place : place + LANES] = down[:, lanes].astype(low_type)

    @pl.when(pl.program_id(0) == 0)
    def _():
        write(sent)

    @pl.when(pl.program_id(0) == 1)
    def _():
        write(kept)


def pack_feed(place, gating, down):
    rows, _, hidden = gating.shape
    half = hidden // 2
    side = lambda i, place_ref: jnp.where(i == 0, 1 - place_ref[1], place_ref[1])
    shapes = [(rows, 3 * LANES * (last - first)) for first, last in CHUNKS] * 2
    return pl.pallas_call(
        pack_kernel,
        grid_spec=pltpu.PrefetchScalarGridSpec(
            num_scalar_prefetch=1,
            grid=(2,),
            in_specs=[
                pl.BlockSpec((rows, 2, half), lambda i, p: (0, 0, side(i, p))),
                pl.BlockSpec((rows, half), lambda i, p: (0, side(i, p))),
            ],
            out_specs=[pl.BlockSpec(shape, lambda *_: (0, 0)) for shape in shapes],
        ),
        out_shape=[jax.ShapeDtypeStruct(shape, low_type) for shape in shapes],
        compiler_params=params(),
        cost_estimate=cost(0, 18 * rows * hidden),
        name="pack_feed",
    )(place, gating, down)


def feed_kernel(count, tiles, place_ref, normed, grad_out, *refs):
    blocks, (hidden, grad_pair, weights) = refs[:count], refs[count:]

    @pl.when(pl.program_id(0) == 0)
    def _():
        assemble(place_ref[0], blocks, weights)

    pair = dot(normed[...], weights[:, : 2 * tiles * LANES])
    grad_hidden = dot(grad_out[...], weights[:, 2 * tiles * LANES :])
    for tile in range(tiles):
        place = 2 * tile * LANES
        gate = pair[:, place : place + LANES]
        up = pair[:, place + LANES : place + 2 * LANES]
        grad = grad_hidden[:, tile * LANES : (tile + 1) * LANES]
        sigma = 1.0 / (1.0 + jnp.exp(-gate))
        silu = gate * sigma
        hidden[:, tile * LANES : (tile + 1) * LANES] = (silu * up).astype(low_type)
        grad_gate = grad * up * sigma * (1.0 + gate * (1.0 - sigma))
        grad_pair[:, place : place + LANES] = grad_gate.astype(low_type)
        grad_pair[:, place + LANES : place + 2 * LANES] = (grad * silu).astype(low_type)


def feed(place, normed, grad_out, blocks):
    total, width = normed.shape
    rows, columns = blocks[0].shape
    tiles = columns // (3 * LANES)
    tile = lambda size: pl.BlockSpec((TILE, size), lambda i, p: (i, 0))
    return pl.pallas_call(
        functools.partial(feed_kernel, len(blocks), tiles),
        grid_spec=pltpu.PrefetchScalarGridSpec(
            num_scalar_prefetch=1,
            grid=(total // TILE,),
            in_specs=[tile(width), tile(width)] + [resident(block.shape) for block in blocks],
            out_specs=[tile(tiles * LANES), tile(2 * tiles * LANES)],
            scratch_shapes=[pltpu.VMEM((width, columns), low_type)],
        ),
        out_shape=[
            jax.ShapeDtypeStruct((total, tiles * LANES), low_type),
            jax.ShapeDtypeStruct((total, 2 * tiles * LANES), low_type),
        ],
        compiler_params=params(),
        cost_estimate=cost(2 * total * width * columns, 4 * total * width + 2 * width * columns),
        name="feed",
    )(place, normed, grad_out, *blocks)


def spread_kernel(counts, place_ref, *refs):
    parts = len(counts)
    values, rest = refs[:parts], refs[parts:]
    chunks = []
    for count in counts:
        chunks.append(rest[:count])
        rest = rest[count:]
    kept, sent, wholes = rest[0], rest[1], rest[2:]

    @pl.when(pl.program_id(0) == 0)
    def _():
        for blocks, whole in zip(chunks, wholes):
            assemble(place_ref[0], blocks, whole)

    total = dot(values[0][...], wholes[0][...], NT)
    for value, whole in zip(values[1:], wholes[1:]):
        total = total + dot(value[...], whole[...], NT)
    write_piece(pl.program_id(0), kept, sent, total.astype(low_type))


def spread(place, values, chunks, column):
    total = values[0].shape[0]
    width = chunks[0][0].shape[0] * len(chunks[0])
    tile = lambda size: pl.BlockSpec((TILE, size), lambda i, p: (i, 0))
    return pl.pallas_call(
        functools.partial(spread_kernel, tuple(len(blocks) for blocks in chunks)),
        grid_spec=pltpu.PrefetchScalarGridSpec(
            num_scalar_prefetch=1,
            grid=(total // TILE,),
            in_specs=[tile(value.shape[1]) for value in values]
            + [
                pl.BlockSpec(
                    (block.shape[0], value.shape[1]), lambda *_: (0, column), pipeline_mode=pl.Buffered(1)
                )
                for value, blocks in zip(values, chunks)
                for block in blocks
            ],
            out_specs=piece_specs(width, lambda i, p: i),
            scratch_shapes=[pltpu.VMEM((width, value.shape[1]), low_type) for value in values],
        ),
        out_shape=piece_shapes(total, width),
        compiler_params=params(),
        cost_estimate=SHORT,
        name="spread",
    )(place, *values, *[block for blocks in chunks for block in blocks])


ROW_TILE = 640


def weight_grad_kernel(parts, select_count, split, place_ref, *refs):
    lefts, rights, rest = refs[:parts], refs[parts : 2 * parts], refs[2 * parts :]
    select, outs = rest[:select_count], rest[select_count:]

    def compute(left, right, offset):
        value = dot(left[...], right[...], TN).astype(low_type)
        if select_count:
            return dot(value, select[0][:, offset : offset + right.shape[1]], NT)
        return value

    def write(targets, value, columns, again):
        size = targets[0].shape[0]
        for place, target in enumerate(targets):
            rows = value[place * size : (place + 1) * size]
            if again:
                rows = rows + target[:, columns].astype(f32)
            target[:, columns] = rows.astype(low_type)

    for block in range(len(outs) // split):
        targets = outs[block * split : (block + 1) * split]

        @pl.when(pl.program_id(0) == block)
        def _(targets=targets):
            offset = 0
            for left, right in zip(lefts, rights):
                value = compute(left, right, offset)
                columns = slice(None) if select_count else slice(offset, offset + right.shape[1])
                again = select_count and offset
                offset += right.shape[1]
                if split == 1:
                    write(targets, value, columns, again)
                    continue

                @pl.when(place_ref[1] == 0)
                def _(value=value, columns=columns, again=again):
                    write(targets, value, columns, again)

                @pl.when(place_ref[1] != 0)
                def _(value=value, columns=columns, again=again):
                    write(targets[::-1], value, columns, again)


def weight_grad(place, blocks, pairs, select=None):
    total, width = pairs[0][0].shape
    rows = width // blocks
    split = 1 if blocks == 1 else 2
    row_tile = math.gcd(rows, ROW_TILE)
    row_tiles = rows // row_tile
    columns = sum(right.shape[1] for _, right in pairs)
    out_columns = columns if select is None else select.shape[0]
    first = lambda b, r, p: lax.rem(p[0] - b + blocks, blocks) * row_tiles + r
    extra = [] if select is None else [jnp.asarray(select, low_type)]
    return pl.pallas_call(
        functools.partial(weight_grad_kernel, len(pairs), len(extra), split),
        grid_spec=pltpu.PrefetchScalarGridSpec(
            num_scalar_prefetch=1,
            grid=(blocks, row_tiles),
            in_specs=[pl.BlockSpec((total, row_tile), lambda b, r, p: (0, first(b, r, p))) for _ in pairs]
            + [resident(right.shape) for _, right in pairs]
            + [resident(value.shape) for value in extra],
            out_specs=[pl.BlockSpec((row_tile // split, out_columns), lambda b, r, p: (r, 0))] * (blocks * split),
        ),
        out_shape=[jax.ShapeDtypeStruct((rows // split, out_columns), low_type)] * (blocks * split),
        compiler_params=params(),
        cost_estimate=cost(2 * total * width * columns, 2 * total * (columns + width * len(pairs))),
        name="weight_grad",
    )(place, *[left for left, _ in pairs], *[right for _, right in pairs], *extra)


ROOT_TWO = math.sqrt(correct_two)


def adam_step(grad, first, second, reciprocal):
    first_new = beta_one * first + (1.0 - beta_one) * grad
    second_new = beta_two * second + ((1.0 - beta_two) * grad) * grad
    root = second_new * lax.rsqrt(jnp.maximum(second_new, 1e-30)) + adam_epsilon * ROOT_TWO
    return first_new, second_new, first_new * reciprocal(root)


def mean_step(total, weight, rate, decay):
    return (rate * ROOT_TWO / correct_one / REPLICA_GROUPS) * total + (rate * decay) * weight


def outer_step(weight, delta, moment):
    moment_new = outer_mu * moment + delta
    return moment_new, weight - outer_rate * (delta + outer_mu * moment_new)


PAIR_ROWS = 4


def feed_update_kernel(place_ref, *refs):
    slots = REPLICA_GROUPS * len(CHUNKS)
    own, other, rest = refs[:slots], refs[slots : 2 * slots], refs[2 * slots :]
    (
        gate_first,
        gate_second,
        gate_weight,
        gate_moment,
        down_first,
        down_second,
        down_weight,
        down_moment,
        gate_first_new,
        gate_second_new,
        gate_delta,
        gate_moment_new,
        gate_master,
        gate_copy,
        down_first_new,
        down_second_new,
        down_delta,
        down_moment_new,
        down_master,
        down_copy,
        gate_grads,
    ) = rest
    near = place_ref[1] == 0
    quick = lambda value: pl.reciprocal(value, approx=True)
    half = down_weight.shape[1] // 2
    groups = [lax.rem(place_ref[2] + k, REPLICA_GROUPS) for k in range(REPLICA_GROUPS)]

    def update(grads, at, first, second, weight, moment, outs, rate, decay):
        first_new, second_new, delta_out, moment_new, master, copy = outs
        start = weight[at]
        total = None
        for group, grad in zip(groups, grads):
            here = (group,) + at
            one, two, step = adam_step(grad, first[here], second[here], quick)
            first_new[here] = one
            second_new[here] = two
            total = step if total is None else total + step
        delta = mean_step(total, start, rate, decay)
        new_moment, new_weight = outer_step(start, delta, moment[at])
        delta_out[at] = delta
        moment_new[at] = new_moment
        master[at] = new_weight
        copy[at] = new_weight.astype(low_type)

    every = slice(None)
    for chunk, (begin, end) in enumerate(CHUNKS):
        for tile in range(begin, end):
            for kind in range(3):
                place = (2 * (tile - begin) + kind) if kind < 2 else (2 * (end - begin) + tile - begin)
                lanes = slice(place * LANES, (place + 1) * LANES)
                mine = [own[chunk * REPLICA_GROUPS + k][:, lanes] for k in range(REPLICA_GROUPS)]
                theirs = [other[chunk * REPLICA_GROUPS + k][:, lanes] for k in range(REPLICA_GROUPS)]
                for side in range(2):
                    grads = [
                        (jnp.where(near, a, b) if side == 0 else jnp.where(near, b, a)).astype(f32)
                        for a, b in zip(mine, theirs)
                    ]
                    at = slice(side * half + tile * LANES, side * half + (tile + 1) * LANES)
                    if kind < 2:
                        for k, grad in enumerate(grads):
                            gate_grads[k, :, kind, at] = grad
                    else:
                        update(
                            grads,
                            (every, at),
                            down_first,
                            down_second,
                            down_weight,
                            down_moment,
                            (down_first_new, down_second_new, down_delta, down_moment_new, down_master, down_copy),
                            inner_rates[4],
                            inner_decays[4],
                        )

    def some_rows(step, _):
        at = (pl.ds(step * PAIR_ROWS, PAIR_ROWS),)
        update(
            [gate_grads[(k,) + at] for k in range(REPLICA_GROUPS)],
            at,
            gate_first,
            gate_second,
            gate_weight,
            gate_moment,
            (gate_first_new, gate_second_new, gate_delta, gate_moment_new, gate_master, gate_copy),
            inner_rates[3],
            inner_decays[3],
        )
        return 0

    lax.fori_loop(0, down_weight.shape[0] // PAIR_ROWS, some_rows, 0)


def feed_update(place, own, other, gating, down):
    rows, _, hidden = gating[2].shape
    size = 32 if rows % 32 == 0 else 16
    steps = rows // size
    own_list = [value for chunk in own for value in chunk]
    other_list = [value for chunk in other for value in chunk]
    plane = pl.BlockSpec((size, hidden), lambda i, p: (i, 0))
    pair = pl.BlockSpec((size, 2, hidden), lambda i, p: (i, 0, 0))
    stack = pl.BlockSpec((REPLICA_GROUPS, size, hidden), lambda i, p: (0, i, 0))
    stack_pair = pl.BlockSpec((REPLICA_GROUPS, size, 2, hidden), lambda i, p: (0, i, 0, 0))
    shape = lambda value, dtype=f32: jax.ShapeDtypeStruct(value.shape, dtype)
    return pl.pallas_call(
        feed_update_kernel,
        grid_spec=pltpu.PrefetchScalarGridSpec(
            num_scalar_prefetch=1,
            grid=(steps,),
            in_specs=[
                pl.BlockSpec((size, value.shape[1]), lambda i, p: (i, 0)) for value in own_list + other_list
            ]
            + [stack_pair, stack_pair, pair, pair, stack, stack, plane, plane],
            out_specs=[stack_pair, stack_pair, pair, pair, pair, pair, stack, stack, plane, plane, plane, plane],
            scratch_shapes=[pltpu.VMEM((REPLICA_GROUPS, size, 2, hidden), f32)],
        ),
        out_shape=[
            shape(gating[0]),
            shape(gating[1]),
            shape(gating[2]),
            shape(gating[2]),
            shape(gating[2]),
            shape(gating[2], low_type),
            shape(down[0]),
            shape(down[1]),
            shape(down[2]),
            shape(down[2]),
            shape(down[2]),
            shape(down[2], low_type),
        ],
        compiler_params=params(),
        cost_estimate=cost(0, rows * hidden * 3 * 90),
        name="feed_update",
    )(place, *own_list, *other_list, *gating, *down)


def optimize(weight, grad, first, second, moment, rate, decay):
    first_new, second_new, step = adam_step(grad, first, second, lambda value: 1.0 / value)
    delta = mean_step(jnp.sum(step, axis=0), weight, rate, decay)
    moment_new, weight_new = outer_step(weight, delta, moment)
    return (first_new, second_new, delta, moment_new, weight_new, weight_new.astype(low_type))


def doc_layout(lengths, token_length):
    ends = jnp.cumsum(lengths)
    starts = ends - lengths
    places = jnp.arange(token_length, dtype=jnp.int32)
    segment = jnp.sum((places[:, None] >= ends[None, :]).astype(jnp.int32), axis=1)
    member = (segment[:, None] == jnp.arange(lengths.shape[0], dtype=jnp.int32)[None, :]).astype(
        jnp.int32
    )
    offset = jnp.sum(member * starts[None, :], axis=1)
    return offset, places - offset


def rope_tables(position):
    half = HEAD_WIDTH // 2
    frequency = rope_base ** (-2.0 * jnp.arange(half, dtype=f32) / HEAD_WIDTH)
    angle = position.astype(f32)[:, None] * frequency[None, :]
    cosine, sine = jnp.cos(angle), jnp.sin(angle)
    gap = jnp.zeros((angle.shape[0], HALF - half), f32)
    return (
        jnp.concatenate([cosine, gap, cosine, gap], axis=1),
        jnp.concatenate([-sine, gap, sine, gap], axis=1),
    )


def norm_inverse(value):
    return lax.rsqrt(jnp.mean(value * value, axis=-1, keepdims=True) + epsilon)


def norm_backward(value, inverse, gain, grad_normed):
    scaled = gain * grad_normed
    return inverse * scaled - value * inverse**3 * jnp.mean(scaled * value, axis=-1, keepdims=True)


def per_device(
    tokens,
    cotangent,
    doc_lengths,
    query_weight,
    keyvalue_weight_full,
    output_weight,
    gating_weight,
    down_weight,
    norm_gains,
    first_query,
    keyvalue_first_moment,
    first_output,
    first_gating,
    first_down,
    first_gains,
    second_query,
    keyvalue_second_moment,
    second_output,
    second_gating,
    second_down,
    second_gains,
    moment_query,
    keyvalue_outer_momentum,
    moment_output,
    moment_gating,
    moment_down,
    moment_gains,
):
    ring = lax.axis_size("ring")
    spot = lax.axis_index("ring")
    side = lax.axis_index("pair")
    near = side == 0
    rows = query_weight.shape[0]
    width = tokens.shape[1]
    local_rows = tokens.shape[0]
    sequence = local_rows * lax.axis_size("tensor")
    plane = ("pair", "tensor")
    per_group = ring // REPLICA_GROUPS
    direct = per_group == 1 and (2 * rows) % LANES == 0
    zero = jnp.zeros_like(spot)
    mine = side * lax.axis_size("tensor") + lax.axis_index("tensor")
    place = jnp.stack([spot if direct else zero, side, spot if direct else zero, mine])
    blocks = ring if direct else 1
    hops = [1, 3, 2]

    def swap(value):
        return lax.ppermute(value, "pair", [(0, 1), (1, 0)])

    def across(value, bit):
        count = lax.axis_size("tensor")
        return lax.ppermute(value, "tensor", [(i, i ^ bit) for i in range(count)])

    def add(left, right):
        return (left.astype(f32) + right.astype(f32)).astype(low_type)

    def core_stage(kept, sent):
        shape = (2, 2, local_rows, width)
        kept, other = kept.reshape(shape), across(sent, 1).reshape(shape)
        cut = local_rows // 2
        spans = [
            (slice(None), 0, slice(None, cut)),
            (slice(None), 1, slice(None, cut)),
            (0, slice(None), slice(cut, None)),
            (1, slice(None), slice(cut, None)),
        ]
        return [add(kept[span], other[span]) for span in spans]

    def chip_stage(parts, *earlier):
        by_x, by_y = after((across(parts[1], 2), swap(parts[3])), *earlier)
        return add(parts[0], by_x), add(parts[2], by_y)

    def last_stage(parts, *earlier):
        one, two = parts
        by_y, by_x = after((swap(one[1]), across(two[1], 2)), *earlier)
        return jnp.concatenate(
            [one[0].astype(f32) + by_y.astype(f32), two[0].astype(f32) + by_x.astype(f32)], axis=0
        )

    def hop(value, step):
        return lax.ppermute(value, "ring", [(i, (i + step) % ring) for i in range(ring)])

    def halves(kept, sent):
        other = swap(sent)
        return jnp.concatenate([jnp.where(near, kept, other), jnp.where(near, other, kept)], axis=0)

    def gather(shard):
        return lax.all_gather(shard, "ring", axis=0, tiled=True)

    def gather_hops(shard):
        if not direct:
            return [gather(shard)]
        found = [shard] + [None] * (ring - 1)
        for step in hops:
            found[step] = hop(shard, step)
        return found

    def relay(found):
        if not direct:
            return [gather(found[0])] if len(found) == 1 and found[0].shape[0] == 2 * rows else found
        return found + [hop(found[-1], 1)]

    def gather_first(value):
        cut = local_rows // 2
        return value, across(value[:cut], 2), swap(value[cut:])

    def gather_second(parts):
        value, by_x, by_y = parts
        cut = local_rows // 2
        one = jnp.stack([value[:cut], by_x])
        two = jnp.stack([value[cut:], by_y])
        return one, two, swap(one), across(two, 2)

    def gather_last(parts):
        one, two, one_y, two_x = parts
        ones = [one[0], one[1], one_y[0], one_y[1]]
        twos = [two[0], two_x[0], two[1], two_x[1]]
        mine = jnp.concatenate([half for pair in zip(ones, twos) for half in pair], axis=0)
        other = across(mine, 1)
        found = []
        for start in range(0, mine.shape[0], local_rows):
            found += [mine[start : start + local_rows], other[start : start + local_rows]]
        return jnp.concatenate(found, axis=0)

    def sides(grads):
        if direct:
            return grads[1::2], grads[0::2]
        whole = grads[0].reshape(ring, 2, rows, -1)
        return (lax.dynamic_index_in_dim(whole, 1 - side, 1, False), lax.dynamic_index_in_dim(whole, side, 1, False))

    def deliver(grads):
        if not direct:
            whole = lax.all_to_all(grads, "ring", split_axis=0, concat_axis=0, tiled=True).astype(f32)
            whole = whole.reshape((REPLICA_GROUPS, per_group) + whole.shape[1:])
            whole = jnp.sum(whole, axis=1).astype(low_type)
            return [whole[k] for k in range(REPLICA_GROUPS)]
        found = [grads[0]] + [None] * (ring - 1)
        for step in hops:
            found[step] = hop(grads[step], -step)
        return found

    def plane_sum(value):
        count = lax.axis_size("tensor")
        bit = 1
        while bit < count:
            value = value + across(value, bit)
            bit *= 2
        return value + swap(value)

    tokens_all = lax.all_gather(tokens, plane, axis=0, tiled=True)

    flat = HEADS * HEAD_WIDTH
    query_halves = [query_weight[:, :flat], query_weight[:, flat:]]
    pair_halves = [
        keyvalue_weight_full[:, :, :HEAD_WIDTH].reshape(rows, 2 * HEAD_WIDTH),
        keyvalue_weight_full[:, :, HEAD_WIDTH:].reshape(rows, 2 * HEAD_WIDTH),
    ]
    gain_columns = jnp.concatenate(
        [norm_gains.T, jnp.zeros((rows, PACK - flat - 2 * HEAD_WIDTH - 2), f32)], axis=1
    )
    packed = [
        jnp.concatenate([q, p, gain_columns, o], axis=1).astype(low_type)
        for q, p, o in zip(query_halves, pair_halves, [output_weight[:, :flat], output_weight[:, flat:]])
    ]
    kept, sent = (jnp.where(near, packed[0], packed[1]), jnp.where(near, packed[1], packed[0]))
    attention_shard = halves(kept, sent)
    attention_blocks = gather_hops(attention_shard)

    feed_parts = pack_feed(after(place, attention_shard), gating_weight, down_weight)
    kept, sent = feed_parts[: len(CHUNKS)], feed_parts[len(CHUNKS) :]
    feed_shards = []
    last = tokens_all
    for a, b in zip(kept, sent):
        last = halves(a, after(b, last))
        feed_shards.append(last)
    one = relay([after(feed_shards[0], attention_blocks)])
    cotangent_parts = gather_first(after(cotangent, tokens_all))

    other_lengths = swap(doc_lengths)
    lengths = [jnp.where(near, doc_lengths[0], other_lengths[0]), jnp.where(near, other_lengths[0], doc_lengths[0])]
    layouts = [doc_layout(value, sequence) for value in lengths]
    starts = jnp.broadcast_to(
        jnp.concatenate([value[0] for value in layouts])[None, :], (8, 2 * sequence)
    ).astype(jnp.int32)
    cosine, sine = rope_tables(jnp.concatenate([value[1] for value in layouts]))

    tokens_late = after(tokens_all, feed_parts)
    normed_one, heads, gains, wide = project(place, tokens_late, attention_blocks, cosine, sine)
    gain_one, gain_two = gains[0], gains[1]
    heads = after(heads, cotangent_parts, feed_shards[0])
    mixed, totals, *partial = attend(place, heads, starts, attention_blocks, sequence)
    cotangent_parts = gather_second(cotangent_parts)
    partial = after(partial, cotangent_parts, feed_shards[1:], one)
    parts = core_stage(*partial)
    one = relay(one)
    cotangent_all = gather_last(after(cotangent_parts, parts))
    parts = chip_stage(parts, cotangent_all, one)
    one = relay(one)
    attention = last_stage(parts, one)

    hidden = tokens.astype(f32)
    inverse_one = norm_inverse(hidden)
    hidden_one = hidden + attention
    inverse_two = norm_inverse(hidden_one)
    normed_two = (hidden_one * inverse_two * gain_two).astype(low_type)
    two = relay([after(feed_shards[1], one)])
    normed_parts = gather_second(after(gather_first(normed_two)))
    normed_two_all = gather_last(after(normed_parts, two))
    hid, grad_pair = feed(place, normed_two_all, cotangent_all, one)
    two = relay(two)
    grad_pair = after(grad_pair, two)
    two = relay(two)
    theirs, mine = sides(weight_grad(place, blocks, [(normed_two_all, grad_pair), (cotangent_all, hid)]))
    theirs_one = deliver(theirs)
    others_one = [swap(theirs_one[0])]
    normed_late = after(normed_two_all, theirs[0])
    hid_two, grad_pair_two = feed(place, normed_late, cotangent_all, two)
    partial = spread(place, after([grad_pair, grad_pair_two], others_one), [one, two], 0)
    partial = after(partial, theirs_one)
    others_one += [swap(after(value, partial)) for value in theirs_one[1:]]
    mine_one = deliver(after(mine, theirs_one))
    parts = core_stage(*partial)
    theirs, mine = sides(
        weight_grad(place, blocks, [(normed_two_all, after(grad_pair_two, *parts)), (cotangent_all, hid_two)])
    )
    parts = chip_stage(parts, theirs[0], mine_one[1::2])
    theirs_two = deliver(after(theirs, mine_one[1:]))
    feed_partial = spread(place, after([hid, hid_two], *parts), [one, two], 2)
    grad_normed_two = last_stage(parts, *feed_partial)
    grad_normed_two = after(grad_normed_two, mine_one, others_one[1])

    grad_hidden_one = cotangent.astype(f32) + norm_backward(
        hidden_one, inverse_two, gain_two, grad_normed_two
    )
    grad_gain_two = jnp.sum(grad_normed_two * hidden_one * inverse_two, axis=0)
    grad_hidden_all = lax.all_gather(grad_hidden_one.astype(low_type), plane, axis=0, tiled=True)
    grad_hidden_all = after(grad_hidden_all, theirs_two, others_one)
    mine_two = deliver(after(mine, grad_hidden_all))
    others_two = [swap(after(value, grad_hidden_all)) for value in theirs_two]

    grad_query, grad_pair = attend_grad(
        place, grad_hidden_all, heads, totals, starts, cosine, sine, attention_blocks, sequence
    )
    *partial, gain_sums = project_grad(place, grad_query, grad_pair, tokens_all, wide)
    partial = after(partial, others_two[:3], mine_two)
    parts = core_stage(*partial)
    project_theirs, project_mine = sides(
        weight_grad(
            place,
            blocks,
            [(normed_one, after(grad_query, *parts)), (normed_one, grad_pair)],
            projection_selector(),
        )
    )
    parts = chip_stage(parts, project_theirs[0])
    project_theirs = deliver(project_theirs)
    project_mine = deliver(project_mine)
    output_theirs, output_mine = sides(
        weight_grad(place, blocks, [(grad_hidden_all, after(mixed, *parts))], output_selector())
    )
    feed_parts = core_stage(*after(feed_partial, output_theirs[0]))
    grad_normed_one = last_stage(parts, output_theirs[0], feed_parts)
    output_theirs, output_mine = deliver(output_theirs), deliver(output_mine)

    token_grad = (
        grad_hidden_one + norm_backward(hidden, inverse_one, gain_one, grad_normed_one)
    ).astype(low_type)

    grad_gains = jnp.stack([jnp.sum(gain_sums, axis=0), grad_gain_two], axis=0)
    grad_gains = plane_sum(grad_gains)
    start = (2 * spot + side) * rows
    if direct:
        found = [grad_gains] + [hop(grad_gains, -step) for step in range(1, ring)]
        found = [lax.dynamic_slice_in_dim(value, start, rows, 1) for value in found]
        gains_total = jnp.roll(jnp.stack(found), spot, axis=0)
    else:
        gains_all = lax.all_gather(grad_gains, "ring", axis=0, tiled=False)
        gains_all = jnp.sum(gains_all.reshape(REPLICA_GROUPS, per_group, 2, width), axis=1)
        gains_total = lax.dynamic_slice_in_dim(gains_all, start, rows, 2)

    updated = feed_update(
        after(place, grad_normed_one, project_theirs, gains_total, others_two),
        [mine_one, mine_two],
        [others_one, others_two],
        (first_gating, second_gating, gating_weight, moment_gating),
        (first_down, second_down, down_weight, moment_down),
    )
    project_other = [swap(value) for value in project_theirs]
    output_other = [swap(after(value, updated[0])) for value in output_theirs]
    feed_parts = chip_stage(feed_parts, updated[0])
    feed_out = last_stage(feed_parts)
    block_output = (hidden_one + feed_out).astype(low_type)

    def slots_to_groups(own, other):
        both = [jnp.stack(own), jnp.stack(other)]
        both = [jnp.where(near, both[0], both[1]), jnp.where(near, both[1], both[0])]
        if direct:
            both = [jnp.roll(value, spot, axis=0) for value in both]
        return [value.astype(f32) for value in both]

    project_totals = slots_to_groups(project_mine, project_other)
    output_totals = slots_to_groups(output_mine, output_other)
    query_total = jnp.concatenate([value[..., :flat] for value in project_totals], axis=-1)
    pair_total = jnp.concatenate(
        [
            value[..., flat : flat + 2 * HEAD_WIDTH].reshape(REPLICA_GROUPS, rows, 2, HEAD_WIDTH)
            for value in project_totals
        ],
        axis=-1,
    )
    output_total = jnp.concatenate(output_totals, axis=-1)

    qry = optimize(
        query_weight, query_total, first_query, second_query, moment_query, inner_rates[0], inner_decays[0]
    )
    kvl = optimize(
        keyvalue_weight_full,
        pair_total,
        keyvalue_first_moment,
        keyvalue_second_moment,
        keyvalue_outer_momentum,
        inner_rates[1],
        inner_decays[1],
    )
    out = optimize(
        output_weight, output_total, first_output, second_output, moment_output, inner_rates[2], inner_decays[2]
    )
    gns = optimize(
        norm_gains, gains_total, first_gains, second_gains, moment_gains, inner_rates[5], inner_decays[5]
    )
    gat = updated[:6]
    dwn = updated[6:]
    return (block_output, token_grad, *qry, *kvl, *out, *gat, *dwn, *gns)


def solution(mesh):
    shape = (mesh.shape["dp"] // 2, 2, mesh.shape["tensor"])
    mesh = Mesh(mesh.devices.reshape(shape), ("ring", "pair", "tensor"))
    dp = ("ring", "pair")
    matrix = P(dp, "tensor")
    pair = P(dp, None, "tensor")
    stack = P(None, dp, "tensor")
    stack_pair = P(None, dp, None, "tensor")
    tokens = P(("ring", "pair", "tensor"), None)
    gains = P(None, dp)
    stack_gains = P(None, None, dp)
    weights = (matrix, pair, matrix, pair, matrix, gains)
    states = (stack, stack_pair, stack, stack_pair, stack, stack_gains)
    outs = []
    for weight, state in zip(weights, states):
        outs += [state, state, weight, weight, weight, weight]
    return jax.shard_map(
        per_device,
        mesh=mesh,
        in_specs=(tokens, tokens, P(dp, None), *weights, *states, *states, *weights),
        out_specs=(tokens, tokens, *outs),
        check_vma=False,
    )
```

time: 2260 us -> 1150 us (0.51)
  waiting for transfers between devices: 1410 us -> 449 us
  Pallas kernels: 0 us -> 367 us
  matrix products: 277 us -> 0 us
  local copies, waits for them, and re-layouts: 256 us -> 54.5 us
  starting transfers between devices: 30.5 us -> 169 us
  other arithmetic: 209 us -> 83.7 us
  blocking collectives: 38.7 us -> 0 us
    all_gather x9 -> x2, waiting for transfers between devices: 673 us -> 0.01 us  [the longest x1 0.01 us: per_device(): tokens_all = lax.all_gather(tokens, plane, axis=0, tiled=True)]
    all_to_all x6 -> x0, waiting for transfers between devices: 627 us -> none  [the longest x1 312 us: per_device(): lax.all_to_all(to_sources(grad_gating, pieces).astype(jnp.bfloat16), 'dp'...]
    ppermute x0 -> x89, waiting for transfers between devices: none -> 449 us  [the longest x36 237 us: hop(): lax.ppermute(value, 'ring', [(i, (i + step) % ring) for i in range(ring)])]
    pallas_call x0 -> x14, Pallas kernels: none -> 367 us  [the longest x4 87.3 us: weight_grad(): pl.pallas_call(functools.partial(weight_grad_kernel, len(pairs), len(extr...]
    dot_general x29 -> x0, matrix products: 277 us -> none  [the longest x5 65.6 us: matmul_plain(): return jnp.dot(left, right, preferred_element_type=jnp.float32)]
    ppermute x0 -> x89, starting transfers between devices: none -> 169 us  [the longest x36 109 us: hop(): lax.ppermute(value, 'ring', [(i, (i + step) % ring) for i in range(ring)])]
    reduce_scatter x4 -> x0, waiting for transfers between devices: 112 us -> none  [the longest x1 49.5 us: per_device(): lax.psum_scatter(matmul_right_t(grad_gating_flat, gating_flat).astype(jnp...]
    reduce_sum x16 -> x6, other arithmetic: 117 us -> 16.3 us  [the longest x4 14.5 us: optimize(): delta = mean_step(jnp.sum(step, axis=0), weight, rate, decay)]
  transfers between devices with their start and end apart: 19 -> 91, of which waited for: 17 -> 42; matrix products, arithmetic and copies ran while one was open for 13% -> 10% of each run, Pallas kernels for 0% -> 32%
where the time goes in v1:
time: 1150 us; the launch traced here: 1140 us
  waiting for transfers between devices  449 us (39%)
  Pallas kernels  367 us (32%)
  starting transfers between devices  169 us (15%)
  other arithmetic  83.7 us (7%)
  local copies, waits for them, and re-layouts  54.5 us (5%)
  between operations  15.8 us (1%)
    ppermute x36, waiting for transfers between devices, hop(): lax.ppermute(value, 'ring', [(i, (i + step) % ring) for i in range(ring)])  237 us
    ppermute x33, waiting for transfers between devices, swap(): return lax.ppermute(value, 'pair', [(0, 1), (1, 0)])  129 us
    ppermute x36, starting transfers between devices, hop(): lax.ppermute(value, 'ring', [(i, (i + step) % ring) for i in range(ring)])  109 us
    pallas_call x4, Pallas kernels, weight_grad(): pl.pallas_call(functools.partial(weight_grad_kernel, len(pairs), len(extr...  87.3 us
    ppermute x20, waiting for transfers between devices, across(): return lax.ppermute(value, 'tensor', [(i, i ^ bit) for i in range(count)])  82.3 us
    pallas_call x1, Pallas kernels, feed_update(): pl.pallas_call(feed_update_kernel, grid_spec=pltpu.PrefetchScalarGridSpec...  62.8 us
    pallas_call x2, Pallas kernels, spread(): pl.pallas_call(functools.partial(spread_kernel, tuple((len(blocks) for bl...  47.7 us
    pallas_call x2, Pallas kernels, feed(): pl.pallas_call(functools.partial(feed_kernel, len(blocks), tiles), grid_s...  45.5 us
  transfers between devices with their start and end apart: 91, of which 42 were waited for; matrix products, arithmetic and copies ran while one was open for 10% of the time, Pallas kernels for 32%

profile of v1, /device:TPU:0, one launch (start us, length us, event | category | flops | bytes accessed | tf_op | source)
XLA Modules:
  0.0 1140.1 jit_solution(1268314656648135471)
XLA Ops:
  11.0 3.0 collective-permute-start
  14.8 17.0 %collective-permute-done.4 = s32[1,4]{1,0:T(1,128)S(1)} collective-permute-done((s32[1,4]{1,0:T(1,128)S(1)}, s32[1,4]{1,0:T(1,128)S(1)}, u32[]{:S(2)}, u32[]{:S(2)}) %collective-permute-start.4) | collective-permute-done | bytes 48 | tf_op jit(solution)/shard_map/ppermute | solution.py:900
  39.9 3.7 fusion.35
  46.2 10.1 pack_feed.1
  56.3 6.8 collective-permute-done.1
  65.5 39.0 %collective-permute-done.2 = bf16[640,832]{0,1:T(8,128)(2,1)} collective-permute-done((bf16[640,832]{0,1:T(8,128)(2,1)}, bf16[640,832]{0,1:T(8,128)(2,1)}, u32[]{:S(2)}, u32[]{:S(2)}) %collective-permute-start.2) | collective-permute-done | bytes 1064992 | tf_op jit(solution)/shard_map/ppermute | solution.py:933
  113.7 21.2 %projection.1 = (bf16[2048,2560]{1,0:T(8,128)(2,1)}, bf16[2048,768]{1,0:T(8,128)(2,1)}, f32[8,2560]{1,0:T(8,128)}, bf16[2560,768]{1,0:T(8,128)(2,1)}) custom-call(s32[4]{0:T(128)} %pad_add_fusion.1.place_ref, bf16[2048,2560]{1,0:T(8,128)(2,1)} %all-gather.3.cloned.1.call-done.tokens, bf16[640,832]{1,0:T(8,128)(2,1)} %copy-done.16, ...), custom_call_target="tpu_custom_call" | custom-call | flops 8053063680 | bytes 32768000 | tf_op jit(solution)/shard_map/projection/pallas_call | solution.py:158
  137.8 7.3 collective-permute-done.7
  147.5 21.4 %collective-permute-start.11 = (bf16[640,1152]{1,0:T(8,128)(2,1)S(1)}, bf16[640,1152]{1,0:T(8,128)(2,1)S(1)}, u32[]{:S(2)}, u32[]{:S(2)}) collective-permute-start(bf16[640,1152]{1,0:T(8,128)(2,1)S(1)} %pad_maximum_fusion.10.refs_0_.refs_2_), channel_id=1, source_target_pairs={{0,8},{8,16},{16,24},{24,0},{1,9},{9,17},{17,25},{25,1},{2,10},{10... | collective-permute-start | bytes 4423688 | tf_op jit(solution)/shard_map/ppermute | solution.py:933
  169.6 32.4 %attention.1 = (bf16[2048,512]{1,0:T(8,128)(2,1)}, f32[8,2048]{1,0:T(8,128)}, bf16[1024,2560]{1,0:T(8,128)(2,1)}, bf16[1024,2560]{1,0:T(8,128)(2,1)}) custom-call(s32[4]{0:T(128)} %pad_add_fusion.1.place_ref, bf16[2048,768]{1,0:T(8,128)(2,1)} %get-tuple-element.196.query.key.value, bf16[2048,768]{1,0:T(8,128)(2,1)} %get-tuple-element.196.query.key.value, ...), custom_call_target="tpu_custom_call" | custom-call | flops 20000000000 | bytes 20971520 | tf_op jit(solution)/shard_map/attention/pallas_call | solution.py:253
  204.1 8.9 collective-permute-done.12
  219.3 12.2 %collective-permute-start.16 = (bf16[640,1152]{1,0:T(8,128)(2,1)S(1)}, bf16[640,1152]{1,0:T(8,128)(2,1)S(1)}, u32[]{:S(2)}, u32[]{:S(2)}) collective-permute-start(bf16[640,1152]{1,0:T(8,128)(2,1)S(1)} %collective-permute-done.11.refs_1_.refs_3_), channel_id=1, source_target_pairs={{0,8},{8,16},{16,24},{24,0},{1,9},{9,17},{17,25},{25,1},{2,10},{10... | collective-permute-start | bytes 4423688 | tf_op jit(solution)/shard_map/ppermute | solution.py:933
  231.5 32.1 %collective-permute-done.16.refs_2_.refs_4_ = bf16[640,1152]{1,0:T(8,128)(2,1)S(1)} collective-permute-done((bf16[640,1152]{1,0:T(8,128)(2,1)S(1)}, bf16[640,1152]{1,0:T(8,128)(2,1)S(1)}, u32[]{:S(2)}, u32[]{:S(2)}) %collective-permute-start.16) | collective-permute-done | bytes 1474592 | tf_op jit(solution)/shard_map/ppermute | solution.py:933
  263.5 2.9 collective-permute-start.19
  273.7 22.7 %collective-permute-done.13 = bf16[2,128,2560]{2,1,0:T(8,128)(2,1)S(1)} collective-permute-done((bf16[2,128,2560]{2,1,0:T(8,128)(2,1)S(1)}, bf16[2,128,2560]{2,1,0:T(8,128)(2,1)S(1)}, u32[]{:S(2)}, u32[]{:S(2)}) %collective-permute-start.13) | collective-permute-done | bytes 1310752 | tf_op jit(solution)/shard_map/ppermute | solution.py:904
  302.3 9.5 collective-permute-done.17
  317.8 11.1 collective-permute-done.20
  332.6 27.2 %collective-permute-done.24.refs_1_.refs_7_ = bf16[640,1536]{1,0:T(8,128)(2,1)S(1)} collective-permute-done((bf16[640,1536]{1,0:T(8,128)(2,1)S(1)}, bf16[640,1536]{1,0:T(8,128)(2,1)S(1)}, u32[]{:S(2)}, u32[]{:S(2)}) %collective-permute-start.24) | collective-permute-done | bytes 1966112 | tf_op jit(solution)/shard_map/ppermute | solution.py:933
  362.3 46.9 %collective-permute-done.26.refs_2_.refs_8_ = bf16[640,1536]{1,0:T(8,128)(2,1)S(1)} collective-permute-done((bf16[640,1536]{1,0:T(8,128)(2,1)S(1)}, bf16[640,1536]{1,0:T(8,128)(2,1)S(1)}, u32[]{:S(2)}, u32[]{:S(2)}) %collective-permute-start.26) | collective-permute-done | bytes 1966112 | tf_op jit(solution)/shard_map/ppermute | solution.py:933
  419.2 20.8 %feed.2 = (bf16[2048,384]{1,0:T(8,128)(2,1)}, bf16[2048,768]{1,0:T(8,128)(2,1)}) custom-call(s32[4]{0:T(128)} %pad_add_fusion.1.place_ref, bf16[2048,2560]{1,0:T(8,128)(2,1)} %slice_dynamic-update-slice_fusion.normed.refs_0_, bf16[2048,2560]{1,0:T(8,128)(2,1)} %copy-done.39, bf16[640,1152]{1,0:T(8,128)(2,1)} %copy-done.3, bf16[640,1152]{1,0:T(8,128)(2,1)} %copy-done.7, ...), custom_call_target="tpu_custom_call" | custom-call | flops 12079595520 | bytes 26869760 | tf_op jit(solution)/shard_map/feed/pallas_call | solution.py:514
  440.0 23.3 %weight_grad.4 = (bf16[320,1152]{1,0:T(8,128)(2,1)}, bf16[320,1152]{1,0:T(8,128)(2,1)}, bf16[320,1152]{1,0:T(8,128)(2,1)}, bf16[320,1152]{1,0:T(8,128)(2,1)}, bf...) custom-call(s32[4]{0:T(128)} %pad_add_fusion.1.place_ref, ...), custom_call_target="tpu_custom_call" | custom-call | flops 12079595520 | bytes 25690112 | tf_op jit(solution)/shard_map/weight_grad/pallas_call | solution.py:635
  465.0 3.8 collective-permute-start.29
  469.4 24.7 %feed.3 = (bf16[2048,512]{1,0:T(8,128)(2,1)}, bf16[2048,1024]{1,0:T(8,128)(2,1)}) custom-call(s32[4]{0:T(128)} %pad_add_fusion.1.place_ref, bf16[2048,2560]{1,0:T(8,128)(2,1)} %slice_dynamic-update-slice_fusion.normed.refs_0_, bf16[2048,2560]{1,0:T(8,128)(2,1)} %copy-done.39, bf16[640,1536]{1,0:T(8,128)(2,1)} %copy-done.2, bf16[640,1536]{1,0:T(8,128)(2,1)} %copy-done.5, ...), custom_call_target="tpu_custom_call" | custom-call | flops 16106127360 | bytes 28835840 | tf_op jit(solution)/shard_map/feed/pallas_call | solution.py:514
  494.1 28.7 %spread.2 = (bf16[1024,2560]{1,0:T(8,128)(2,1)}, bf16[1024,2560]{1,0:T(8,128)(2,1)}) custom-call(s32[4]{0:T(128)} %pad_add_fusion.1.place_ref, bf16[2048,768]{1,0:T(8,128)(2,1)} %get-tuple-element.227.refs_2_.refs_0_, bf16[2048,1024]{1,0:T(8,128)(2,1)} %get-tuple-element.236.refs_1_.refs_2_, bf16[640,1152]{1,0:T(8,128)(2,1)} %copy-done.3, ...), custom_call_target="tpu_custom_call" | custom-call | flops 1 | bytes 1 | tf_op jit(solution)/shard_map/spread/pallas_call | solution.py:557
  522.8 5.8 collective-permute-done.30
  528.6 19.3 %collective-permute-start.36 = (bf16[320,1152]{1,0:T(8,128)(2,1)}, bf16[320,1152]{1,0:T(8,128)(2,1)}, u32[]{:S(2)}, u32[]{:S(2)}) collective-permute-start(bf16[320,1152]{1,0:T(8,128)(2,1)} %get-tuple-element.243), channel_id=1, source_target_pairs={{0,8},{8,16},{16,24},{24,0},{1,9},{9,17},{17,25},{25,1},{2,10},{10... | collective-permute-start | bytes 2211848 | tf_op jit(solution)/shard_map/ppermute | solution.py:933
  549.6 3.9 fusion.18
  556.2 27.6 %weight_grad.5 = (bf16[320,1536]{1,0:T(8,128)(2,1)}, bf16[320,1536]{1,0:T(8,128)(2,1)}, bf16[320,1536]{1,0:T(8,128)(2,1)}, bf16[320,1536]{1,0:T(8,128)(2,1)}, bf...) custom-call(s32[4]{0:T(128)} %pad_add_fusion.1.place_ref, ...), custom_call_target="tpu_custom_call" | custom-call | flops 16106127360 | bytes 27262976 | tf_op jit(solution)/shard_map/weight_grad/pallas_call | solution.py:635
  593.6 10.7 collective-permute-start.39
  605.9 19.0 %spread.3 = (bf16[1024,2560]{1,0:T(8,128)(2,1)}, bf16[1024,2560]{1,0:T(8,128)(2,1)}) custom-call(s32[4]{0:T(128)} %pad_add_fusion.1.place_ref, bf16[2048,384]{1,0:T(8,128)(2,1)} %get-tuple-element.246.refs_3_.refs_0_, bf16[2048,512]{1,0:T(8,128)(2,1)} %get-tuple-element.247.refs_3_.refs_1_, bf16[640,1152]{1,0:T(8,128)(2,1)} %copy-done.3, ...), custom_call_target="tpu_custom_call" | custom-call | flops 1 | bytes 1 | tf_op jit(solution)/shard_map/spread/pallas_call | solution.py:557
  627.6 7.8 collective-permute-done.39.refs_2_
  636.4 2.9 fusion.58
  643.4 30.8 %collective-permute-done.44.refs_10_ = bf16[320,1152]{1,0:T(8,128)(2,1)} collective-permute-done((bf16[320,1152]{1,0:T(8,128)(2,1)}, bf16[320,1152]{1,0:T(8,128)(2,1)}, u32[]{:S(2)}, u32[]{:S(2)}) %collective-permute-start.44) | collective-permute-done | bytes 737312 | tf_op jit(solution)/shard_map/ppermute | solution.py:900
  674.2 22.1 %collective-permute-done.45.refs_11_ = bf16[320,1152]{1,0:T(8,128)(2,1)} collective-permute-done((bf16[320,1152]{1,0:T(8,128)(2,1)}, bf16[320,1152]{1,0:T(8,128)(2,1)}, u32[]{:S(2)}, u32[]{:S(2)}) %collective-permute-start.45) | collective-permute-done | bytes 737312 | tf_op jit(solution)/shard_map/ppermute | solution.py:900
  696.3 28.0 %collective-permute-done.42 = bf16[320,1536]{1,0:T(8,128)(2,1)} collective-permute-done((bf16[320,1536]{1,0:T(8,128)(2,1)}, bf16[320,1536]{1,0:T(8,128)(2,1)}, u32[]{:S(2)}, u32[]{:S(2)}) %collective-permute-start.42) | collective-permute-done | bytes 983072 | tf_op jit(solution)/shard_map/ppermute | solution.py:933
  727.9 3.3 collective-permute-start.50
  731.2 18.1 %collective-permute-done.46.refs_12_ = bf16[320,1536]{1,0:T(8,128)(2,1)} collective-permute-done((bf16[320,1536]{1,0:T(8,128)(2,1)}, bf16[320,1536]{1,0:T(8,128)(2,1)}, u32[]{:S(2)}, u32[]{:S(2)}) %collective-permute-start.46) | collective-permute-done | bytes 983072 | tf_op jit(solution)/shard_map/ppermute | solution.py:900
  750.6 37.3 %attention_grad.1 = (bf16[2048,512]{1,0:T(8,128)(2,1)}, bf16[2048,256]{1,0:T(8,128)(2,1)}) custom-call(s32[4]{0:T(128)} %pad_add_fusion.1.place_ref, bf16[2048,2560]{1,0:T(8,128)(2,1)} %all-gather.5.cloned.1.call-done.grad_hidden.refs_0_, bf16[2048,768]{1,0:T(8,128)(2,1)} %get-tuple-element.196.query.key.value, ...), custom_call_target="tpu_custom_call" | custom-call | flops 30000001024 | bytes 20971520 | tf_op jit(solution)/shard_map/attention_grad/pallas_call | solution.py:350
  787.9 23.1 %projection_grad.1 = (bf16[1024,2560]{1,0:T(8,128)(2,1)}, bf16[1024,2560]{1,0:T(8,128)(2,1)}, f32[8,2560]{1,0:T(8,128)}) custom-call(s32[4]{0:T(128)} %pad_add_fusion.1.place_ref, bf16[2048,512]{1,0:T(8,128)(2,1)} %get-tuple-element.287.grad_query.refs_2_, bf16[2048,256]{1,0:T(8,128)(2,1)} %get-tuple-element.269.grad_pair.refs_3_, ...), custom_call_target="tpu_custom_call" | custom-call | flops 1 | bytes 1 | tf_op jit(solution)/shard_map/projection_grad/pallas_call | solution.py:421
  811.1 4.8 collective-permute-done.50.refs_6_
  817.4 7.1 collective-permute-done.63
  825.3 3.2 collective-permute-done.64
  841.4 3.1 fusion.20
  844.5 4.2 fusion.22
  851.6 23.8 %weight_grad.6 = (bf16[320,512]{1,0:T(8,128)(2,1)}, bf16[320,512]{1,0:T(8,128)(2,1)}, bf16[320,512]{1,0:T(8,128)(2,1)}, bf16[320,512]{1,0:T(8,128)(2,1)}, bf16[3...) custom-call(s32[4]{0:T(128)} %pad_add_fusion.1.place_ref, ...), custom_call_target="tpu_custom_call" | custom-call | flops 8053063680 | bytes 24117248 | tf_op jit(solution)/shard_map/weight_grad/pallas_call | solution.py:635
  887.5 12.5 %weight_grad.7 = (bf16[320,320]{1,0:T(8,128)(2,1)}, bf16[320,320]{1,0:T(8,128)(2,1)}, bf16[320,320]{1,0:T(8,128)(2,1)}, bf16[320,320]{1,0:T(8,128)(2,1)}, bf16[3...) custom-call(s32[4]{0:T(128)} %pad_add_fusion.1.place_ref, ...), custom_call_target="tpu_custom_call" | custom-call | flops 5368709120 | bytes 12582912 | tf_op jit(solution)/shard_map/weight_grad/pallas_call | solution.py:635
  901.5 12.3 %collective-permute-done.61 = bf16[320,512]{1,0:T(8,128)(2,1)} collective-permute-done((bf16[320,512]{1,0:T(8,128)(2,1)}, bf16[320,512]{1,0:T(8,128)(2,1)}, u32[]{:S(2)}, u32[]{:S(2)}) %collective-permute-start.61) | collective-permute-done | bytes 327712 | tf_op jit(solution)/shard_map/ppermute | solution.py:933
  916.2 5.6 collective-permute-start.78
  927.5 62.8 %feed_update.1 = (f32[4,320,2,1792]{3,2,1,0:T(2,128)}, f32[4,320,2,1792]{3,2,1,0:T(2,128)}, f32[320,2,1792]{2,1,0:T(2,128)}, f32[320,2,1792]{2,1,0:T(2,128)}, f3...) custom-call(s32[4]{0:T(128)} %pad_add_fusion.1.place_ref, ...), custom_call_target="tpu_custom_call" | custom-call | bytes 154828800 | tf_op jit(solution)/shard_map/feed_update/pallas_call | solution.py:781
  1004.1 6.9 multiply_reduce_fusion.1
  1014.3 3.0 multiply_reduce_fusion.5
  1017.3 5.6 collective-permute-start.87
  1022.9 3.3 collective-permute-start.85
  1028.0 4.6 collective-permute-done.87
  1032.6 5.0 collective-permute-start.81
  1037.6 10.3 collective-permute-done.85
  1048.0 5.4 collective-permute-start.79
  1053.4 3.2 collective-permute-start.88
  1056.7 4.4 collective-permute-done.80
  1065.4 4.6 collective-permute-done.84
  1074.6 4.2 collective-permute-start.56
  1079.6 3.9 multiply_reduce_fusion
  1085.3 24.0 %collective-permute-done.56 = bf16[2,128,2560]{2,1,0:T(8,128)(2,1)S(1)} collective-permute-done((bf16[2,128,2560]{2,1,0:T(8,128)(2,1)S(1)}, bf16[2,128,2560]{2,1,0:T(8,128)(2,1)S(1)}, u32[]{:S(2)}, u32[]{:S(2)}) %collective-permute-start.56) | collective-permute-done | bytes 1310752 | tf_op jit(solution)/shard_map/ppermute | solution.py:904
  1119.9 9.8 collective-permute-done.70
  (424 shorter events, 190.5 us)
Async XLA Ops:
  7.3 102.1 %all-gather.3.cloned.1.call-start = ((), (), s32[]{:S(2)}) async-start(), calls=%async_computation | async-start | bytes 11796480 | tf_op jit(solution)/shard_map/all_gather | solution.py:1002
  8.0 716.3 %all-gather.5.cloned.1.call-start = ((), (), s32[]{:S(2)}) async-start(), calls=%async_computation.1 | async-start | bytes 11796480 | tf_op jit(solution)/shard_map/all_gather | solution.py:1088
  34.4 28.7 %collective-permute-start.1 = (bf16[640,832]{0,1:T(8,128)(2,1)}, bf16[640,832]{0,1:T(8,128)(2,1)}, u32[]{:S(2)}, u32[]{:S(2)}) collective-permute-start(bf16[640,832]{0,1:T(8,128)(2,1)} %copy.150), channel_id=1, source_target_pairs={{0,8},{8,16},{16,24},{24,0},{1,9},{9,17},{17,25},{25,1},{2,10},{10... | collective-permute-start | bytes 3194888 | tf_op jit(solution)/shard_map/ppermute | solution.py:933
  35.9 68.7 %collective-permute-start.2 = (bf16[640,832]{0,1:T(8,128)(2,1)}, bf16[640,832]{0,1:T(8,128)(2,1)}, u32[]{:S(2)}, u32[]{:S(2)}) collective-permute-start(bf16[640,832]{0,1:T(8,128)(2,1)} %copy.150), channel_id=1, source_target_pairs={{0,16},{8,24},{16,0},{24,8},{1,17},{9,25},{17,1},{25,9},{2,18},{10... | collective-permute-start | bytes 3194888 | tf_op jit(solution)/shard_map/ppermute | solution.py:933
  38.6 68.3 %collective-permute-start.3 = (bf16[640,832]{0,1:T(8,128)(2,1)}, bf16[640,832]{0,1:T(8,128)(2,1)}, u32[]{:S(2)}, u32[]{:S(2)}) collective-permute-start(bf16[640,832]{0,1:T(8,128)(2,1)} %copy.150), channel_id=1, source_target_pairs={{0,24},{8,0},{16,8},{24,16},{1,25},{9,1},{17,9},{25,17},{2,26},{10... | collective-permute-start | bytes 3194888 | tf_op jit(solution)/shard_map/ppermute | solution.py:933
  109.6 25.3 %collective-permute-start.5 = (bf16[128,2560]{1,0:T(8,128)(2,1)S(1)}, bf16[128,2560]{1,0:T(8,128)(2,1)S(1)}, u32[]{:S(2)}, u32[]{:S(2)}) collective-permute-start(bf16[128,2560]{1,0:T(8,128)(2,1)S(1)} %get-tuple-element.410), channel_id=1, source_target_pairs={{0,2},{1,3},{2,0},{3,1},{4,6},{5,7},{6,4},{7,5},{8,10},{9,11},{10,... | collective-permute-start | bytes 1966088 | tf_op jit(solution)/shard_map/ppermute | solution.py:904
  111.2 25.9 %collective-permute-start.6 = (bf16[128,2560]{1,0:T(8,128)(2,1)S(1)}, bf16[128,2560]{1,0:T(8,128)(2,1)S(1)}, u32[]{:S(2)}, u32[]{:S(2)}) collective-permute-start(bf16[128,2560]{1,0:T(8,128)(2,1)S(1)} %get-tuple-element.409), channel_id=1, source_target_pairs={{0,4},{4,0},{1,5},{5,1},{2,6},{6,2},{3,7},{7,3},{8,12},{12,8},{9,1... | collective-permute-start | bytes 1966088 | tf_op jit(solution)/shard_map/ppermute | solution.py:900
  113.6 31.4 %collective-permute-start.7 = (bf16[320,1152]{1,0:T(8,128)(2,1)}, bf16[320,1152]{1,0:T(8,128)(2,1)S(1)}, u32[]{:S(2)}, u32[]{:S(2)}) collective-permute-start(bf16[320,1152]{1,0:T(8,128)(2,1)} %get-tuple-element.195), channel_id=1, source_target_pairs={{0,4},{4,0},{1,5},{5,1},{2,6},{6,2},{3,7},{7,3},{8,12},{12,8},{9,1... | collective-permute-start | bytes 2211848 | tf_op jit(solution)/shard_map/ppermute | solution.py:900
  135.0 69.0 %collective-permute-start.8 = (bf16[2,128,2560]{2,1,0:T(8,128)(2,1)S(1)}, bf16[2,128,2560]{2,1,0:T(8,128)(2,1)}, u32[]{:S(2)}, u32[]{:S(2)}) collective-permute-start(bf16[2,128,2560]{2,1,0:T(8,128)(2,1)S(1)} %pad_maximum_fusion.11), channel_id=1, source_target_pairs={{0,4},{4,0},{1,5},{5,1},{2,6},{6,2},{3,7},{7,3},{8,12},{12,8},{9,1... | collective-permute-start | bytes 3932168 | tf_op jit(solution)/shard_map/ppermute | solution.py:900
  137.2 66.8 %collective-permute-start.9 = (bf16[2,128,2560]{2,1,0:T(8,128)(2,1)S(1)}, bf16[2,128,2560]{2,1,0:T(8,128)(2,1)}, u32[]{:S(2)}, u32[]{:S(2)}) collective-permute-start(bf16[2,128,2560]{2,1,0:T(8,128)(2,1)S(1)} %pad_maximum_fusion.12), channel_id=1, source_target_pairs={{0,2},{1,3},{2,0},{3,1},{4,6},{5,7},{6,4},{7,5},{8,10},{9,11},{10,... | collective-permute-start | bytes 3932168 | tf_op jit(solution)/shard_map/ppermute | solution.py:904
  145.4 56.6 %collective-permute-start.10 = (bf16[320,1536]{1,0:T(8,128)(2,1)}, bf16[320,1536]{1,0:T(8,128)(2,1)}, u32[]{:S(2)}, u32[]{:S(2)}) collective-permute-start(bf16[320,1536]{1,0:T(8,128)(2,1)} %get-tuple-element.199), channel_id=1, source_target_pairs={{0,4},{4,0},{1,5},{5,1},{2,6},{6,2},{3,7},{7,3},{8,12},{12,8},{9,1... | collective-permute-start | bytes 2949128 | tf_op jit(solution)/shard_map/ppermute | solution.py:900
  147.5 56.5 %collective-permute-start.11 = (bf16[640,1152]{1,0:T(8,128)(2,1)S(1)}, bf16[640,1152]{1,0:T(8,128)(2,1)S(1)}, u32[]{:S(2)}, u32[]{:S(2)}) collective-permute-start(bf16[640,1152]{1,0:T(8,128)(2,1)S(1)} %pad_maximum_fusion.10.refs_0_.refs_2_), channel_id=1, source_target_pairs={{0,8},{8,16},{16,24},{24,0},{1,9},{9,17},{17,25},{25,1},{2,10},{10... | collective-permute-start | bytes 4423688 | tf_op jit(solution)/shard_map/ppermute | solution.py:933
  219.1 49.6 %collective-permute-start.15 = (bf16[1024,2560]{1,0:T(8,128)(2,1)S(1)}, bf16[1024,2560]{1,0:T(8,128)(2,1)S(1)}, u32[]{:S(2)}, u32[]{:S(2)}) collective-permute-start(bf16[1024,2560]{1,0:T(8,128)(2,1)S(1)} %bitcast_dynamic-update-slice_fusion.17), channel_id=1, source_target_pairs={{0,1},{1,0},{2,3},{3,2},{4,5},{5,4},{6,7},{7,6},{8,9},{9,8},{10,11... | collective-permute-start | bytes 15728648 | tf_op jit(solution)/shard_map/ppermute | solution.py:904
  219.3 44.3 %collective-permute-start.16 = (bf16[640,1152]{1,0:T(8,128)(2,1)S(1)}, bf16[640,1152]{1,0:T(8,128)(2,1)S(1)}, u32[]{:S(2)}, u32[]{:S(2)}) collective-permute-start(bf16[640,1152]{1,0:T(8,128)(2,1)S(1)} %collective-permute-done.11.refs_1_.refs_3_), channel_id=1, source_target_pairs={{0,8},{8,16},{16,24},{24,0},{1,9},{9,17},{17,25},{25,1},{2,10},{10... | collective-permute-start | bytes 4423688 | tf_op jit(solution)/shard_map/ppermute | solution.py:933
  263.5 38.8 %collective-permute-start.19 = (bf16[640,1152]{1,0:T(8,128)(2,1)S(1)}, bf16[640,1152]{1,0:T(8,128)(2,1)S(1)}, u32[]{:S(2)}, u32[]{:S(2)}) collective-permute-start(bf16[640,1152]{1,0:T(8,128)(2,1)S(1)} %collective-permute-done.16.refs_2_.refs_4_), channel_id=1, source_target_pairs={{0,8},{8,16},{16,24},{24,0},{1,9},{9,17},{17,25},{25,1},{2,10},{10... | collective-permute-start | bytes 4423688 | tf_op jit(solution)/shard_map/ppermute | solution.py:933
  266.4 30.0 %collective-permute-start.13 = (bf16[2,128,2560]{2,1,0:T(8,128)(2,1)S(1)}, bf16[2,128,2560]{2,1,0:T(8,128)(2,1)S(1)}, u32[]{:S(2)}, u32[]{:S(2)}) collective-permute-start(bf16[2,128,2560]{2,1,0:T(8,128)(2,1)S(1)} %fusion.12), channel_id=1, source_target_pairs={{0,2},{1,3},{2,0},{3,1},{4,6},{5,7},{6,4},{7,5},{8,10},{9,11},{10,... | collective-permute-start | bytes 3932168 | tf_op jit(solution)/shard_map/ppermute | solution.py:904
  266.9 29.7 %collective-permute-start.14 = (bf16[2,128,2560]{2,1,0:T(8,128)(2,1)S(1)}, bf16[2,128,2560]{2,1,0:T(8,128)(2,1)S(1)}, u32[]{:S(2)}, u32[]{:S(2)}) collective-permute-start(bf16[2,128,2560]{2,1,0:T(8,128)(2,1)S(1)} %get-tuple-element.384), channel_id=1, source_target_pairs={{0,4},{4,0},{1,5},{5,1},{2,6},{6,2},{3,7},{7,3},{8,12},{12,8},{9,1... | collective-permute-start | bytes 3932168 | tf_op jit(solution)/shard_map/ppermute | solution.py:900
  317.0 42.8 %collective-permute-start.24 = (bf16[640,1536]{1,0:T(8,128)(2,1)S(1)}, bf16[640,1536]{1,0:T(8,128)(2,1)S(1)}, u32[]{:S(2)}, u32[]{:S(2)}) collective-permute-start(bf16[640,1536]{1,0:T(8,128)(2,1)S(1)} %pad_maximum_fusion.3.refs_0_.refs_6_), channel_id=1, source_target_pairs={{0,8},{8,16},{16,24},{24,0},{1,9},{9,17},{17,25},{25,1},{2,10},{10... | collective-permute-start | bytes 5898248 | tf_op jit(solution)/shard_map/ppermute | solution.py:933
  331.5 28.3 %collective-permute-start.22 = (bf16[2,128,2560]{2,1,0:T(8,128)(2,1)S(1)}, bf16[2,128,2560]{2,1,0:T(8,128)(2,1)S(1)}, u32[]{:S(2)}, u32[]{:S(2)}) collective-permute-start(bf16[2,128,2560]{2,1,0:T(8,128)(2,1)S(1)} %pad_maximum_fusion.13), channel_id=1, source_target_pairs={{0,4},{4,0},{1,5},{5,1},{2,6},{6,2},{3,7},{7,3},{8,12},{12,8},{9,1... | collective-permute-start | bytes 3932168 | tf_op jit(solution)/shard_map/ppermute | solution.py:900
  332.0 27.8 %collective-permute-start.23 = (bf16[2,128,2560]{2,1,0:T(8,128)(2,1)S(1)}, bf16[2,128,2560]{2,1,0:T(8,128)(2,1)S(1)}, u32[]{:S(2)}, u32[]{:S(2)}) collective-permute-start(bf16[2,128,2560]{2,1,0:T(8,128)(2,1)S(1)} %pad_maximum_fusion.14), channel_id=1, source_target_pairs={{0,2},{1,3},{2,0},{3,1},{4,6},{5,7},{6,4},{7,5},{8,10},{9,11},{10,... | collective-permute-start | bytes 3932168 | tf_op jit(solution)/shard_map/ppermute | solution.py:904
  362.2 47.1 %collective-permute-start.25 = (bf16[1024,2560]{1,0:T(8,128)(2,1)S(1)}, bf16[1024,2560]{1,0:T(8,128)(2,1)S(1)}, u32[]{:S(2)}, u32[]{:S(2)}) collective-permute-start(bf16[1024,2560]{1,0:T(8,128)(2,1)S(1)} %bitcast_dynamic-update-slice_fusion.1), channel_id=1, source_target_pairs={{0,1},{1,0},{2,3},{3,2},{4,5},{5,4},{6,7},{7,6},{8,9},{9,8},{10,11... | collective-permute-start | bytes 15728648 | tf_op jit(solution)/shard_map/ppermute | solution.py:904
  362.2 47.0 %collective-permute-start.26 = (bf16[640,1536]{1,0:T(8,128)(2,1)S(1)}, bf16[640,1536]{1,0:T(8,128)(2,1)S(1)}, u32[]{:S(2)}, u32[]{:S(2)}) collective-permute-start(bf16[640,1536]{1,0:T(8,128)(2,1)S(1)} %collective-permute-done.24.refs_1_.refs_7_), channel_id=1, source_target_pairs={{0,8},{8,16},{16,24},{24,0},{1,9},{9,17},{17,25},{25,1},{2,10},{10... | collective-permute-start | bytes 5898248 | tf_op jit(solution)/shard_map/ppermute | solution.py:933
  409.3 60.1 %collective-permute-start.27 = (bf16[640,1536]{1,0:T(8,128)(2,1)S(1)}, bf16[640,1536]{1,0:T(8,128)(2,1)}, u32[]{:S(2)}, u32[]{:S(2)}) collective-permute-start(bf16[640,1536]{1,0:T(8,128)(2,1)S(1)} %collective-permute-done.26.refs_2_.refs_8_), channel_id=1, source_target_pairs={{0,8},{8,16},{16,24},{24,0},{1,9},{9,17},{17,25},{25,1},{2,10},{10... | collective-permute-start | bytes 5898248 | tf_op jit(solution)/shard_map/ppermute | solution.py:933
  463.3 30.8 %collective-permute-start.28 = (bf16[320,1152]{1,0:T(8,128)(2,1)}, bf16[320,1152]{1,0:T(8,128)(2,1)S(1)}, u32[]{:S(2)}, u32[]{:S(2)}) collective-permute-start(bf16[320,1152]{1,0:T(8,128)(2,1)} %get-tuple-element.223), channel_id=1, source_target_pairs={{0,4},{4,0},{1,5},{5,1},{2,6},{6,2},{3,7},{7,3},{8,12},{12,8},{9,1... | collective-permute-start | bytes 2211848 | tf_op jit(solution)/shard_map/ppermute | solution.py:900
  465.0 57.8 %collective-permute-start.29 = (bf16[320,1152]{1,0:T(8,128)(2,1)}, bf16[320,1152]{1,0:T(8,128)(2,1)}, u32[]{:S(2)}, u32[]{:S(2)}) collective-permute-start(bf16[320,1152]{1,0:T(8,128)(2,1)} %get-tuple-element.231), channel_id=1, source_target_pairs={{0,24},{8,0},{16,8},{24,16},{1,25},{9,1},{17,9},{25,17},{2,26},{10... | collective-permute-start | bytes 2211848 | tf_op jit(solution)/shard_map/ppermute | solution.py:933
  468.8 59.8 %collective-permute-start.30 = (bf16[320,1152]{1,0:T(8,128)(2,1)}, bf16[320,1152]{1,0:T(8,128)(2,1)}, u32[]{:S(2)}, u32[]{:S(2)}) collective-permute-start(bf16[320,1152]{1,0:T(8,128)(2,1)} %get-tuple-element.232), channel_id=1, source_target_pairs={{0,16},{8,24},{16,0},{24,8},{1,17},{9,25},{17,1},{25,9},{2,18},{10... | collective-permute-start | bytes 2211848 | tf_op jit(solution)/shard_map/ppermute | solution.py:933
  468.8 59.8 %collective-permute-start.31 = (bf16[320,1152]{1,0:T(8,128)(2,1)}, bf16[320,1152]{1,0:T(8,128)(2,1)}, u32[]{:S(2)}, u32[]{:S(2)}) collective-permute-start(bf16[320,1152]{1,0:T(8,128)(2,1)} %get-tuple-element.233), channel_id=1, source_target_pairs={{0,8},{8,16},{16,24},{24,0},{1,9},{9,17},{17,25},{25,1},{2,10},{10... | collective-permute-start | bytes 2211848 | tf_op jit(solution)/shard_map/ppermute | solution.py:933
  528.6 55.2 %collective-permute-start.35 = (bf16[320,1152]{1,0:T(8,128)(2,1)}, bf16[320,1152]{1,0:T(8,128)(2,1)S(1)}, u32[]{:S(2)}, u32[]{:S(2)}) collective-permute-start(bf16[320,1152]{1,0:T(8,128)(2,1)} %get-tuple-element.242), channel_id=1, source_target_pairs={{0,24},{8,0},{16,8},{24,16},{1,25},{9,1},{17,9},{25,17},{2,26},{10... | collective-permute-start | bytes 2211848 | tf_op jit(solution)/shard_map/ppermute | solution.py:933
  528.6 55.7 %collective-permute-start.36 = (bf16[320,1152]{1,0:T(8,128)(2,1)}, bf16[320,1152]{1,0:T(8,128)(2,1)}, u32[]{:S(2)}, u32[]{:S(2)}) collective-permute-start(bf16[320,1152]{1,0:T(8,128)(2,1)} %get-tuple-element.243), channel_id=1, source_target_pairs={{0,8},{8,16},{16,24},{24,0},{1,9},{9,17},{17,25},{25,1},{2,10},{10... | collective-permute-start | bytes 2211848 | tf_op jit(solution)/shard_map/ppermute | solution.py:933
  555.1 31.1 %collective-permute-start.33 = (bf16[2,128,2560]{2,1,0:T(8,128)(2,1)S(1)}, bf16[2,128,2560]{2,1,0:T(8,128)(2,1)}, u32[]{:S(2)}, u32[]{:S(2)}) collective-permute-start(bf16[2,128,2560]{2,1,0:T(8,128)(2,1)S(1)} %fusion.16), channel_id=1, source_target_pairs={{0,2},{1,3},{2,0},{3,1},{4,6},{5,7},{6,4},{7,5},{8,10},{9,11},{10,... | collective-permute-start | bytes 3932168 | tf_op jit(solution)/shard_map/ppermute | solution.py:904
  555.7 30.9 %collective-permute-start.34 = (bf16[2,128,2560]{2,1,0:T(8,128)(2,1)}, bf16[2,128,2560]{2,1,0:T(8,128)(2,1)}, u32[]{:S(2)}, u32[]{:S(2)}) collective-permute-start(bf16[2,128,2560]{2,1,0:T(8,128)(2,1)} %get-tuple-element.382), channel_id=1, source_target_pairs={{0,4},{4,0},{1,5},{5,1},{2,6},{6,2},{3,7},{7,3},{8,12},{12,8},{9,1... | collective-permute-start | bytes 3932168 | tf_op jit(solution)/shard_map/ppermute | solution.py:900
  590.9 34.0 %collective-permute-start.37 = (bf16[128,2560]{1,0:T(8,128)(2,1)}, bf16[128,2560]{1,0:T(8,128)(2,1)}, u32[]{:S(2)}, u32[]{:S(2)}) collective-permute-start(bf16[128,2560]{1,0:T(8,128)(2,1)} %slice_bitcast_fusion.18), channel_id=1, source_target_pairs={{0,4},{4,0},{1,5},{5,1},{2,6},{6,2},{3,7},{7,3},{8,12},{12,8},{9,1... | collective-permute-start | bytes 1966088 | tf_op jit(solution)/shard_map/ppermute | solution.py:900
  592.2 32.7 %collective-permute-start.38 = (bf16[128,2560]{1,0:T(8,128)(2,1)}, bf16[128,2560]{1,0:T(8,128)(2,1)}, u32[]{:S(2)}, u32[]{:S(2)}) collective-permute-start(bf16[128,2560]{1,0:T(8,128)(2,1)} %slice_bitcast_fusion.17), channel_id=1, source_target_pairs={{0,2},{1,3},{2,0},{3,1},{4,6},{5,7},{6,4},{7,5},{8,10},{9,11},{10,... | collective-permute-start | bytes 1966088 | tf_op jit(solution)/shard_map/ppermute | solution.py:904
  593.6 41.8 %collective-permute-start.39 = (bf16[320,1152]{1,0:T(8,128)(2,1)}, bf16[320,1152]{1,0:T(8,128)(2,1)S(1)}, u32[]{:S(2)}, u32[]{:S(2)}) collective-permute-start(bf16[320,1152]{1,0:T(8,128)(2,1)} %get-tuple-element.253), channel_id=1, source_target_pairs={{0,16},{8,24},{16,0},{24,8},{1,17},{9,25},{17,1},{25,9},{2,18},{10... | collective-permute-start | bytes 2211848 | tf_op jit(solution)/shard_map/ppermute | solution.py:933
  604.3 31.1 %collective-permute-start.40 = (bf16[320,1152]{1,0:T(8,128)(2,1)}, bf16[320,1152]{1,0:T(8,128)(2,1)}, u32[]{:S(2)}, u32[]{:S(2)}) collective-permute-start(bf16[320,1152]{1,0:T(8,128)(2,1)} %collective-permute-done.29), channel_id=1, source_target_pairs={{0,4},{4,0},{1,5},{5,1},{2,6},{6,2},{3,7},{7,3},{8,12},{12,8},{9,1... | collective-permute-start | bytes 2211848 | tf_op jit(solution)/shard_map/ppermute | solution.py:900
  639.3 57.0 %collective-permute-start.41 = (bf16[320,1536]{1,0:T(8,128)(2,1)}, bf16[320,1536]{1,0:T(8,128)(2,1)}, u32[]{:S(2)}, u32[]{:S(2)}) collective-permute-start(bf16[320,1536]{1,0:T(8,128)(2,1)} %get-tuple-element.260), channel_id=1, source_target_pairs={{0,24},{8,0},{16,8},{24,16},{1,25},{9,1},{17,9},{25,17},{2,26},{10... | collective-permute-start | bytes 2949128 | tf_op jit(solution)/shard_map/ppermute | solution.py:933
  639.8 84.5 %collective-permute-start.42 = (bf16[320,1536]{1,0:T(8,128)(2,1)}, bf16[320,1536]{1,0:T(8,128)(2,1)}, u32[]{:S(2)}, u32[]{:S(2)}) collective-permute-start(bf16[320,1536]{1,0:T(8,128)(2,1)} %get-tuple-element.261), channel_id=1, source_target_pairs={{0,16},{8,24},{16,0},{24,8},{1,17},{9,25},{17,1},{25,9},{2,18},{10... | collective-permute-start | bytes 2949128 | tf_op jit(solution)/shard_map/ppermute | solution.py:933
  639.8 84.5 %collective-permute-start.43 = (bf16[320,1536]{1,0:T(8,128)(2,1)}, bf16[320,1536]{1,0:T(8,128)(2,1)}, u32[]{:S(2)}, u32[]{:S(2)}) collective-permute-start(bf16[320,1536]{1,0:T(8,128)(2,1)} %get-tuple-element.262), channel_id=1, source_target_pairs={{0,8},{8,16},{16,24},{24,0},{1,9},{9,17},{17,25},{25,1},{2,10},{10... | collective-permute-start | bytes 2949128 | tf_op jit(solution)/shard_map/ppermute | solution.py:933
  641.4 32.8 %collective-permute-start.44 = (bf16[320,1152]{1,0:T(8,128)(2,1)}, bf16[320,1152]{1,0:T(8,128)(2,1)}, u32[]{:S(2)}, u32[]{:S(2)}) collective-permute-start(bf16[320,1152]{1,0:T(8,128)(2,1)} %collective-permute-done.30), channel_id=1, source_target_pairs={{0,4},{4,0},{1,5},{5,1},{2,6},{6,2},{3,7},{7,3},{8,12},{12,8},{9,1... | collective-permute-start | bytes 2211848 | tf_op jit(solution)/shard_map/ppermute | solution.py:900
  643.0 53.3 %collective-permute-start.45 = (bf16[320,1152]{1,0:T(8,128)(2,1)}, bf16[320,1152]{1,0:T(8,128)(2,1)}, u32[]{:S(2)}, u32[]{:S(2)}) collective-permute-start(bf16[320,1152]{1,0:T(8,128)(2,1)} %collective-permute-done.31), channel_id=1, source_target_pairs={{0,4},{4,0},{1,5},{5,1},{2,6},{6,2},{3,7},{7,3},{8,12},{12,8},{9,1... | collective-permute-start | bytes 2211848 | tf_op jit(solution)/shard_map/ppermute | solution.py:900
  724.3 25.0 %collective-permute-start.46 = (bf16[320,1536]{1,0:T(8,128)(2,1)}, bf16[320,1536]{1,0:T(8,128)(2,1)}, u32[]{:S(2)}, u32[]{:S(2)}) collective-permute-start(bf16[320,1536]{1,0:T(8,128)(2,1)} %get-tuple-element.273), channel_id=1, source_target_pairs={{0,4},{4,0},{1,5},{5,1},{2,6},{6,2},{3,7},{7,3},{8,12},{12,8},{9,1... | collective-permute-start | bytes 2949128 | tf_op jit(solution)/shard_map/ppermute | solution.py:900
  725.9 85.2 %collective-permute-start.47 = (bf16[320,1536]{1,0:T(8,128)(2,1)}, bf16[320,1536]{1,0:T(8,128)(2,1)}, u32[]{:S(2)}, u32[]{:S(2)}) collective-permute-start(bf16[320,1536]{1,0:T(8,128)(2,1)} %collective-permute-done.41), channel_id=1, source_target_pairs={{0,4},{4,0},{1,5},{5,1},{2,6},{6,2},{3,7},{7,3},{8,12},{12,8},{9,1... | collective-permute-start | bytes 2949128 | tf_op jit(solution)/shard_map/ppermute | solution.py:900
  726.3 84.8 %collective-permute-start.48 = (bf16[320,1536]{1,0:T(8,128)(2,1)}, bf16[320,1536]{1,0:T(8,128)(2,1)}, u32[]{:S(2)}, u32[]{:S(2)}) collective-permute-start(bf16[320,1536]{1,0:T(8,128)(2,1)} %collective-permute-done.42), channel_id=1, source_target_pairs={{0,4},{4,0},{1,5},{5,1},{2,6},{6,2},{3,7},{7,3},{8,12},{12,8},{9,1... | collective-permute-start | bytes 2949128 | tf_op jit(solution)/shard_map/ppermute | solution.py:900
  727.9 83.1 %collective-permute-start.49 = (bf16[320,1536]{1,0:T(8,128)(2,1)}, bf16[320,1536]{1,0:T(8,128)(2,1)}, u32[]{:S(2)}, u32[]{:S(2)}) collective-permute-start(bf16[320,1536]{1,0:T(8,128)(2,1)} %get-tuple-element.281), channel_id=1, source_target_pairs={{0,24},{8,0},{16,8},{24,16},{1,25},{9,1},{17,9},{25,17},{2,26},{10... | collective-permute-start | bytes 2949128 | tf_op jit(solution)/shard_map/ppermute | solution.py:933
  727.9 87.9 %collective-permute-start.50 = (bf16[320,1536]{1,0:T(8,128)(2,1)}, bf16[320,1536]{1,0:T(8,128)(2,1)}, u32[]{:S(2)}, u32[]{:S(2)}) collective-permute-start(bf16[320,1536]{1,0:T(8,128)(2,1)} %get-tuple-element.282), channel_id=1, source_target_pairs={{0,16},{8,24},{16,0},{24,8},{1,17},{9,25},{17,1},{25,9},{2,18},{10... | collective-permute-start | bytes 2949128 | tf_op jit(solution)/shard_map/ppermute | solution.py:933
  749.3 66.6 %collective-permute-start.51 = (bf16[320,1536]{1,0:T(8,128)(2,1)}, bf16[320,1536]{1,0:T(8,128)(2,1)}, u32[]{:S(2)}, u32[]{:S(2)}) collective-permute-start(bf16[320,1536]{1,0:T(8,128)(2,1)} %get-tuple-element.283), channel_id=1, source_target_pairs={{0,8},{8,16},{16,24},{24,0},{1,9},{9,17},{17,25},{25,1},{2,10},{10... | collective-permute-start | bytes 2949128 | tf_op jit(solution)/shard_map/ppermute | solution.py:933
  815.9 25.5 %collective-permute-start.52 = (bf16[1024,2560]{1,0:T(8,128)(2,1)}, bf16[1024,2560]{1,0:T(8,128)(2,1)}, u32[]{:S(2)}, u32[]{:S(2)}) collective-permute-start(bf16[1024,2560]{1,0:T(8,128)(2,1)} %get-tuple-element.285), channel_id=1, source_target_pairs={{0,1},{1,0},{2,3},{3,2},{4,5},{5,4},{6,7},{7,6},{8,9},{9,8},{10,11... | collective-permute-start | bytes 15728648 | tf_op jit(solution)/shard_map/ppermute | solution.py:904
  829.5 70.5 %collective-permute-start.69 = (bf16[320,1536]{1,0:T(8,128)(2,1)}, bf16[320,1536]{1,0:T(8,128)(2,1)S(1)}, u32[]{:S(2)}, u32[]{:S(2)}) collective-permute-start(bf16[320,1536]{1,0:T(8,128)(2,1)} %collective-permute-done.43), channel_id=1, source_target_pairs={{0,4},{4,0},{1,5},{5,1},{2,6},{6,2},{3,7},{7,3},{8,12},{12,8},{9,1... | collective-permute-start | bytes 2949128 | tf_op jit(solution)/shard_map/ppermute | solution.py:900
  848.7 28.7 %collective-permute-start.53 = (bf16[2,128,2560]{2,1,0:T(8,128)(2,1)}, bf16[2,128,2560]{2,1,0:T(8,128)(2,1)}, u32[]{:S(2)}, u32[]{:S(2)}) collective-permute-start(bf16[2,128,2560]{2,1,0:T(8,128)(2,1)} %fusion.20), channel_id=1, source_target_pairs={{0,2},{1,3},{2,0},{3,1},{4,6},{5,7},{6,4},{7,5},{8,10},{9,11},{10,... | collective-permute-start | bytes 3932168 | tf_op jit(solution)/shard_map/ppermute | solution.py:904
  849.3 31.2 %collective-permute-start.54 = (bf16[2,128,2560]{2,1,0:T(8,128)(2,1)}, bf16[2,128,2560]{2,1,0:T(8,128)(2,1)}, u32[]{:S(2)}, u32[]{:S(2)}) collective-permute-start(bf16[2,128,2560]{2,1,0:T(8,128)(2,1)} %get-tuple-element.380), channel_id=1, source_target_pairs={{0,4},{4,0},{1,5},{5,1},{2,6},{6,2},{3,7},{7,3},{8,12},{12,8},{9,1... | collective-permute-start | bytes 3932168 | tf_op jit(solution)/shard_map/ppermute | solution.py:900
  877.1 36.7 %collective-permute-start.61 = (bf16[320,512]{1,0:T(8,128)(2,1)}, bf16[320,512]{1,0:T(8,128)(2,1)}, u32[]{:S(2)}, u32[]{:S(2)}) collective-permute-start(bf16[320,512]{1,0:T(8,128)(2,1)} %get-tuple-element.298), channel_id=1, source_target_pairs={{0,16},{8,24},{16,0},{24,8},{1,17},{9,25},{17,1},{25,9},{2,18},{10... | collective-permute-start | bytes 983048 | tf_op jit(solution)/shard_map/ppermute | solution.py:933
  877.4 38.7 %collective-permute-start.62 = (bf16[320,512]{1,0:T(8,128)(2,1)}, bf16[320,512]{1,0:T(8,128)(2,1)}, u32[]{:S(2)}, u32[]{:S(2)}) collective-permute-start(bf16[320,512]{1,0:T(8,128)(2,1)} %get-tuple-element.299), channel_id=1, source_target_pairs={{0,8},{8,16},{16,24},{24,0},{1,9},{9,17},{17,25},{25,1},{2,10},{10... | collective-permute-start | bytes 983048 | tf_op jit(solution)/shard_map/ppermute | solution.py:933
  880.5 35.6 %collective-permute-start.75 = (bf16[320,512]{1,0:T(8,128)(2,1)}, bf16[320,512]{1,0:T(8,128)(2,1)}, u32[]{:S(2)}, u32[]{:S(2)}) collective-permute-start(bf16[320,512]{1,0:T(8,128)(2,1)} %get-tuple-element.288), channel_id=1, source_target_pairs={{0,4},{4,0},{1,5},{5,1},{2,6},{6,2},{3,7},{7,3},{8,12},{12,8},{9,1... | collective-permute-start | bytes 983048 | tf_op jit(solution)/shard_map/ppermute | solution.py:900
  913.9 157.1 %collective-permute-start.55 = (bf16[1024,2560]{1,0:T(8,128)(2,1)}, bf16[1024,2560]{1,0:T(8,128)(2,1)}, u32[]{:S(2)}, u32[]{:S(2)}) collective-permute-start(bf16[1024,2560]{1,0:T(8,128)(2,1)} %get-tuple-element.294), channel_id=1, source_target_pairs={{0,1},{1,0},{2,3},{3,2},{4,5},{5,4},{6,7},{7,6},{8,9},{9,8},{10,11... | collective-permute-start | bytes 15728648 | tf_op jit(solution)/shard_map/ppermute | solution.py:904
  916.2 74.2 %collective-permute-start.72 = (bf16[320,512]{1,0:T(8,128)(2,1)}, bf16[320,512]{1,0:T(8,128)(2,1)S(1)}, u32[]{:S(2)}, u32[]{:S(2)}) collective-permute-start(bf16[320,512]{1,0:T(8,128)(2,1)} %get-tuple-element.309), channel_id=1, source_target_pairs={{0,24},{8,0},{16,8},{24,16},{1,25},{9,1},{17,9},{25,17},{2,26},{10... | collective-permute-start | bytes 983048 | tf_op jit(solution)/shard_map/ppermute | solution.py:933
  916.2 74.2 %collective-permute-start.78 = (bf16[320,512]{1,0:T(8,128)(2,1)}, bf16[320,512]{1,0:T(8,128)(2,1)S(1)}, u32[]{:S(2)}, u32[]{:S(2)}) collective-permute-start(bf16[320,512]{1,0:T(8,128)(2,1)} %collective-permute-done.62), channel_id=1, source_target_pairs={{0,4},{4,0},{1,5},{5,1},{2,6},{6,2},{3,7},{7,3},{8,12},{12,8},{9,1... | collective-permute-start | bytes 983048 | tf_op jit(solution)/shard_map/ppermute | solution.py:900
  921.8 68.6 %collective-permute-start.77 = (bf16[320,512]{1,0:T(8,128)(2,1)}, bf16[320,512]{1,0:T(8,128)(2,1)S(1)}, u32[]{:S(2)}, u32[]{:S(2)}) collective-permute-start(bf16[320,512]{1,0:T(8,128)(2,1)} %collective-permute-done.61), channel_id=1, source_target_pairs={{0,4},{4,0},{1,5},{5,1},{2,6},{6,2},{3,7},{7,3},{8,12},{12,8},{9,1... | collective-permute-start | bytes 983048 | tf_op jit(solution)/shard_map/ppermute | solution.py:900
  923.7 66.7 %collective-permute-start.76 = (bf16[320,512]{1,0:T(8,128)(2,1)}, bf16[320,512]{1,0:T(8,128)(2,1)S(1)}, u32[]{:S(2)}, u32[]{:S(2)}) collective-permute-start(bf16[320,512]{1,0:T(8,128)(2,1)} %collective-permute-done.60), channel_id=1, source_target_pairs={{0,4},{4,0},{1,5},{5,1},{2,6},{6,2},{3,7},{7,3},{8,12},{12,8},{9,1... | collective-permute-start | bytes 983048 | tf_op jit(solution)/shard_map/ppermute | solution.py:900
  1022.9 25.1 %collective-permute-start.85 = (bf16[320,320]{1,0:T(8,128)(2,1)S(1)}, bf16[320,320]{1,0:T(8,128)(2,1)S(1)}, u32[]{:S(2)}, u32[]{:S(2)}) collective-permute-start(bf16[320,320]{1,0:T(8,128)(2,1)S(1)} %copy-done.58), channel_id=1, source_target_pairs={{0,16},{8,24},{16,0},{24,8},{1,17},{9,25},{17,1},{25,9},{2,18},{10... | collective-permute-start | bytes 614408 | tf_op jit(solution)/shard_map/ppermute | solution.py:933
  1027.6 25.8 %collective-permute-start.82 = (bf16[320,320]{1,0:T(8,128)(2,1)S(1)}, bf16[320,320]{1,0:T(8,128)(2,1)S(1)}, u32[]{:S(2)}, u32[]{:S(2)}) collective-permute-start(bf16[320,320]{1,0:T(8,128)(2,1)S(1)} %copy-done.56), channel_id=1, source_target_pairs={{0,4},{4,0},{1,5},{5,1},{2,6},{6,2},{3,7},{7,3},{8,12},{12,8},{9,1... | collective-permute-start | bytes 614408 | tf_op jit(solution)/shard_map/ppermute | solution.py:900
  1063.7 52.1 %collective-permute-start.58 = (bf16[128,2560]{1,0:T(8,128)(2,1)S(1)}, bf16[128,2560]{1,0:T(8,128)(2,1)S(1)}, u32[]{:S(2)}, u32[]{:S(2)}) collective-permute-start(bf16[128,2560]{1,0:T(8,128)(2,1)S(1)} %slice_bitcast_fusion.14), channel_id=1, source_target_pairs={{0,4},{4,0},{1,5},{5,1},{2,6},{6,2},{3,7},{7,3},{8,12},{12,8},{9,1... | collective-permute-start | bytes 1966088 | tf_op jit(solution)/shard_map/ppermute | solution.py:900
  1065.4 50.5 %collective-permute-start.59 = (bf16[128,2560]{1,0:T(8,128)(2,1)S(1)}, bf16[128,2560]{1,0:T(8,128)(2,1)S(1)}, u32[]{:S(2)}, u32[]{:S(2)}) collective-permute-start(bf16[128,2560]{1,0:T(8,128)(2,1)S(1)} %slice_bitcast_fusion.13), channel_id=1, source_target_pairs={{0,2},{1,3},{2,0},{3,1},{4,6},{5,7},{6,4},{7,5},{8,10},{9,11},{10,... | collective-permute-start | bytes 1966088 | tf_op jit(solution)/shard_map/ppermute | solution.py:904
  1074.6 34.8 %collective-permute-start.56 = (bf16[2,128,2560]{2,1,0:T(8,128)(2,1)S(1)}, bf16[2,128,2560]{2,1,0:T(8,128)(2,1)S(1)}, u32[]{:S(2)}, u32[]{:S(2)}) collective-permute-start(bf16[2,128,2560]{2,1,0:T(8,128)(2,1)S(1)} %fusion.24), channel_id=1, source_target_pairs={{0,2},{1,3},{2,0},{3,1},{4,6},{5,7},{6,4},{7,5},{8,10},{9,11},{10,... | collective-permute-start | bytes 3932168 | tf_op jit(solution)/shard_map/ppermute | solution.py:904
  1078.8 32.2 %collective-permute-start.57 = (bf16[2,128,2560]{2,1,0:T(8,128)(2,1)S(1)}, bf16[2,128,2560]{2,1,0:T(8,128)(2,1)S(1)}, u32[]{:S(2)}, u32[]{:S(2)}) collective-permute-start(bf16[2,128,2560]{2,1,0:T(8,128)(2,1)S(1)} %fusion.25), channel_id=1, source_target_pairs={{0,4},{4,0},{1,5},{5,1},{2,6},{6,2},{3,7},{7,3},{8,12},{12,8},{9,1... | collective-permute-start | bytes 3932168 | tf_op jit(solution)/shard_map/ppermute | solution.py:900
  (89 other events, 1498.6 us)
Sparse Core Ops, SparseCore 0:
  10.0 70.4 all-gather.2
  639.4 79.9 all-gather.4

commit v2 on v1

--- a/solution.py
+++ b/solution.py
@@ -54,8 +54,13 @@
     return pltpu.CompilerParams(vmem_limit_bytes=VMEM_BYTES, **kwargs)
 
 
+COST_SHARE = 1.0
+
+
 def cost(flops, size):
-    return pl.CostEstimate(flops=int(flops), bytes_accessed=int(size), transcendentals=0)
+    return pl.CostEstimate(
+        flops=int(COST_SHARE * flops), bytes_accessed=int(COST_SHARE * size), transcendentals=0
+    )
 
 
 SHORT = pl.CostEstimate(flops=1, bytes_accessed=1, transcendentals=0)
@@ -83,6 +88,16 @@
         for place in range(HEAD_WIDTH):
             table[head * HEAD_WIDTH + place, head * LANES + place] = 1.0
     return table
+
+
+OUTPUT_PACK = 384
+
+
+def gradient_selectors():
+    project, output = projection_selector(), output_selector()
+    padded = np.zeros((OUTPUT_PACK, HEADS * LANES), np.float32)
+    padded[: output.shape[0]] = output
+    return ((0, project[:, : HEADS * LANES]), (0, project[:, HEADS * LANES :]), (0, None), (1, padded))
 
 
 def gains_selector():
@@ -161,7 +176,7 @@
             num_scalar_prefetch=1,
             grid=(total // TILE,),
             in_specs=[tile(width)]
-            + [resident((block.shape[0], PACK)) for block in blocks]
+            + [resident(block.shape) for block in blocks]
             + [
                 resident((PACK, WIDE)),
                 resident((8, PACK)),
@@ -211,8 +226,7 @@
         rows = blocks[0].shape[0]
         for step, block in enumerate(blocks):
             start = first_row(place_ref[0], step, len(blocks), rows)
-            value = block[:, PACK:]
-            wide[pl.ds(start, rows), :] = dot(value, select[...]).astype(low_type)
+            wide[pl.ds(start, rows), :] = dot(block[...], select[...]).astype(low_type)
 
 
 def attention_kernel(count, blocks_per, place_ref, query, key, value, starts, *refs):
@@ -580,15 +594,11 @@
 ROW_TILE = 640
 
 
-def weight_grad_kernel(parts, select_count, split, place_ref, *refs):
+def weight_grad_kernel(spans, selected, split, place_ref, *refs):
+    parts = len(spans)
     lefts, rights, rest = refs[:parts], refs[parts : 2 * parts], refs[2 * parts :]
-    select, outs = rest[:select_count], rest[select_count:]
-
-    def compute(left, right, offset):
-        value = dot(left[...], right[...], TN).astype(low_type)
-        if select_count:
-            return dot(value, select[0][:, offset : offset + right.shape[1]], NT)
-        return value
+    outs = rest[sum(selected) :]
+    selects = [rest[sum(selected[:place])] if chosen else None for place, chosen in enumerate(selected)]
 
     def write(targets, value, columns, again):
         size = targets[0].shape[0]
@@ -603,12 +613,12 @@
 
         @pl.when(pl.program_id(0) == block)
         def _(targets=targets):
-            offset = 0
-            for left, right in zip(lefts, rights):
-                value = compute(left, right, offset)
-                columns = slice(None) if select_count else slice(offset, offset + right.shape[1])
-                again = select_count and offset
-                offset += right.shape[1]
+            for place, (left, right) in enumerate(zip(lefts, rights)):
+                value = dot(left[...], right[...], TN).astype(low_type)
+                if selects[place] is not None:
+                    value = dot(value, selects[place][...], NT)
+                columns = slice(*spans[place])
+                again = place and spans[place] == spans[place - 1]
                 if split == 1:
                     write(targets, value, columns, again)
                     continue
@@ -622,29 +632,38 @@
                     write(targets[::-1], value, columns, again)
 
 
-def weight_grad(place, blocks, pairs, select=None):
+def weight_grad(place, blocks, pairs, selects=()):
     total, width = pairs[0][0].shape
     rows = width // blocks
     split = 1 if blocks == 1 else 2
     row_tile = math.gcd(rows, ROW_TILE)
     row_tiles = rows // row_tile
-    columns = sum(right.shape[1] for _, right in pairs)
-    out_columns = columns if select is None else select.shape[0]
+    spans, end = [], 0
+    for index, (_, right) in enumerate(pairs):
+        if selects and index and selects[index][0] == selects[index - 1][0]:
+            spans.append(spans[-1])
+            continue
+        size = selects[index][1].shape[0] if selects else right.shape[1]
+        spans.append((end, end + size))
+        end += size
     first = lambda b, r, p: lax.rem(p[0] - b + blocks, blocks) * row_tiles + r
-    extra = [] if select is None else [jnp.asarray(select, low_type)]
+    selected = [table is not None for _, table in selects] or [False] * len(pairs)
+    extra = [jnp.asarray(table, low_type) for _, table in selects if table is not None]
     return pl.pallas_call(
-        functools.partial(weight_grad_kernel, len(pairs), len(extra), split),
+        functools.partial(weight_grad_kernel, spans, selected, split),
         grid_spec=pltpu.PrefetchScalarGridSpec(
             num_scalar_prefetch=1,
             grid=(blocks, row_tiles),
-            in_specs=[pl.BlockSpec((total, row_tile), lambda b, r, p: (0, first(b, r, p))) for _ in pairs]
+            in_specs=[
+                pl.BlockSpec((left.shape[0], row_tile), lambda b, r, p: (0, first(b, r, p))) for left, _ in pairs
+            ]
             + [resident(right.shape) for _, right in pairs]
             + [resident(value.shape) for value in extra],
-            out_specs=[pl.BlockSpec((row_tile // split, out_columns), lambda b, r, p: (r, 0))] * (blocks * split),
+            out_specs=[pl.BlockSpec((row_tile // split, end), lambda b, r, p: (r, 0))] * (blocks * split),
         ),
-        out_shape=[jax.ShapeDtypeStruct((rows // split, out_columns), low_type)] * (blocks * split),
+        out_shape=[jax.ShapeDtypeStruct((rows // split, end), low_type)] * (blocks * split),
         compiler_params=params(),
-        cost_estimate=cost(2 * total * width * columns, 2 * total * (columns + width * len(pairs))),
+        cost_estimate=cost(2 * total * width * end, 2 * total * (end + width * len(pairs))),
         name="weight_grad",
     )(place, *[left for left, _ in pairs], *[right for _, right in pairs], *extra)
 
@@ -808,6 +827,68 @@
         cost_estimate=cost(0, rows * hidden * 3 * 90),
         name="feed_update",
     )(place, *own_list, *other_list, *gating, *down)
+
+
+def attention_update_kernel(place_ref, *refs):
+    own, other, rest = refs[:REPLICA_GROUPS], refs[REPLICA_GROUPS : 2 * REPLICA_GROUPS], refs[2 * REPLICA_GROUPS :]
+    left, right, states, outs = rest[0], rest[1], rest[2:10], rest[10:]
+    near = place_ref[1] == 0
+    flat = HEADS * HEAD_WIDTH
+    for kind, (start, size) in enumerate(((0, PACK), (PACK, OUTPUT_PACK))):
+        first, second, weight, moment = states[4 * kind : 4 * kind + 4]
+        first_new, second_new, delta_out, moment_new, master, copy = outs[6 * kind : 6 * kind + 6]
+        value = weight[...]
+        total = None
+        for slot in range(REPLICA_GROUPS):
+            group = lax.rem(place_ref[2] + slot, REPLICA_GROUPS)
+            mine, theirs = own[slot][:, start : start + size], other[slot][:, start : start + size]
+            low, high = jnp.where(near, mine, theirs), jnp.where(near, theirs, mine)
+            grad = dot(low, left[:size, :]) + dot(high, right[:size, :])
+            one, two, step = adam_step(
+                grad, first[group], second[group], lambda item: pl.reciprocal(item, approx=True)
+            )
+            first_new[group] = one
+            second_new[group] = two
+            total = step if total is None else total + step
+        delta = mean_step(total, value, inner_rates[2 * kind], inner_decays[2 * kind])
+        new_moment, new_weight = outer_step(value, delta, moment[...])
+        delta_out[...] = delta
+        moment_new[...] = new_moment
+        master[...] = new_weight
+        copy[...] = new_weight.astype(low_type)
+
+
+def attention_update(place, own, other, query, output):
+    rows, columns = query[2].shape
+    flat = HEADS * HEAD_WIDTH
+    size = math.gcd(rows, 160)
+    table = np.zeros((2, PACK, columns), np.float32)
+    for place_of in range(flat):
+        table[0, place_of, place_of] = 1.0
+        table[1, place_of, flat + place_of] = 1.0
+    plane = pl.BlockSpec((size, columns), lambda i, p: (i, 0))
+    stack = pl.BlockSpec((REPLICA_GROUPS, size, columns), lambda i, p: (0, i, 0))
+    shape = lambda value, dtype=f32: jax.ShapeDtypeStruct(value.shape, dtype)
+    shapes = []
+    for state in (query, output):
+        shapes += [shape(state[0]), shape(state[1])] + [shape(state[2])] * 3 + [shape(state[2], low_type)]
+    return pl.pallas_call(
+        attention_update_kernel,
+        grid_spec=pltpu.PrefetchScalarGridSpec(
+            num_scalar_prefetch=1,
+            grid=(rows // size,),
+            in_specs=[
+                pl.BlockSpec((size, value.shape[1]), lambda i, p: (i, 0)) for value in (*own, *other)
+            ]
+            + [resident((PACK, columns))] * 2
+            + [stack, stack, plane, plane] * 2,
+            out_specs=[stack, stack, plane, plane, plane, plane] * 2,
+        ),
+        out_shape=shapes,
+        compiler_params=params(),
+        cost_estimate=cost(0, rows * columns * 2 * 90),
+        name="attention_update",
+    )(place, *own, *other, jnp.asarray(table[0], low_type), jnp.asarray(table[1], low_type), *query, *output)
 
 
 def optimize(weight, grad, first, second, moment, rate, decay):
@@ -918,13 +999,19 @@
         ]
         return [add(kept[span], other[span]) for span in spans]
 
-    def chip_stage(parts, *earlier):
-        by_x, by_y = after((across(parts[1], 2), swap(parts[3])), *earlier)
+    def chip_send(parts):
+        return across(parts[1], 2), swap(parts[3])
+
+    def chip_stage(parts, *earlier, came=None):
+        by_x, by_y = after(came or chip_send(parts), *earlier)
         return add(parts[0], by_x), add(parts[2], by_y)
 
-    def last_stage(parts, *earlier):
+    def last_send(parts):
+        return swap(parts[0][1]), across(parts[1][1], 2)
+
+    def last_stage(parts, *earlier, came=None):
         one, two = parts
-        by_y, by_x = after((swap(one[1]), across(two[1], 2)), *earlier)
+        by_y, by_x = after(came or last_send(parts), *earlier)
         return jnp.concatenate(
             [one[0].astype(f32) + by_y.astype(f32), two[0].astype(f32) + by_x.astype(f32)], axis=0
         )
@@ -932,8 +1019,8 @@
     def hop(value, step):
         return lax.ppermute(value, "ring", [(i, (i + step) % ring) for i in range(ring)])
 
-    def halves(kept, sent):
-        other = swap(sent)
+    def halves(kept, sent, other=None):
+        other = swap(sent) if other is None else other
         return jnp.concatenate([jnp.where(near, kept, other), jnp.where(near, other, kept)], axis=0)
 
     def gather(shard):
@@ -949,7 +1036,7 @@
 
     def relay(found):
         if not direct:
-            return [gather(found[0])] if len(found) == 1 and found[0].shape[0] == 2 * rows else found
+            return [gather(found[0])] if found[0].shape[0] == 2 * rows else found
         return found + [hop(found[-1], 1)]
 
     def gather_first(value):
@@ -991,13 +1078,13 @@
             found[step] = hop(grads[step], -step)
         return found
 
-    def plane_sum(value):
+    def tensor_sum(value):
         count = lax.axis_size("tensor")
         bit = 1
         while bit < count:
             value = value + across(value, bit)
             bit *= 2
-        return value + swap(value)
+        return value
 
     tokens_all = lax.all_gather(tokens, plane, axis=0, tiled=True)
 
@@ -1011,19 +1098,26 @@
         [norm_gains.T, jnp.zeros((rows, PACK - flat - 2 * HEAD_WIDTH - 2), f32)], axis=1
     )
     packed = [
-        jnp.concatenate([q, p, gain_columns, o], axis=1).astype(low_type)
-        for q, p, o in zip(query_halves, pair_halves, [output_weight[:, :flat], output_weight[:, flat:]])
+        jnp.concatenate([q, p, gain_columns], axis=1).astype(low_type)
+        for q, p in zip(query_halves, pair_halves)
     ]
-    kept, sent = (jnp.where(near, packed[0], packed[1]), jnp.where(near, packed[1], packed[0]))
-    attention_shard = halves(kept, sent)
+    output_low = output_weight.astype(low_type)
+    output_parts = [output_low[:, :flat], output_low[:, flat:]]
+    pick = lambda parts: (jnp.where(near, parts[0], parts[1]), jnp.where(near, parts[1], parts[0]))
+    attention_shard = halves(*pick(packed))
     attention_blocks = gather_hops(attention_shard)
+    output_kept, output_sent = pick(output_parts)
+    output_shard = halves(output_kept, after(output_sent, attention_shard))
+    output_blocks = gather_hops(after(output_shard, attention_blocks[1:2]))
 
     feed_parts = pack_feed(after(place, attention_shard), gating_weight, down_weight)
+    tokens_all = after(tokens_all, feed_parts)
     kept, sent = feed_parts[: len(CHUNKS)], feed_parts[len(CHUNKS) :]
-    feed_shards = []
-    last = tokens_all
+    feed_shards, came = [], []
+    last = attention_shard
     for a, b in zip(kept, sent):
-        last = halves(a, after(b, last))
+        came.append(swap(after(b, last)))
+        last = halves(a, b, came[-1])
         feed_shards.append(last)
     one = relay([after(feed_shards[0], attention_blocks)])
     cotangent_parts = gather_first(after(cotangent, tokens_all))
@@ -1036,32 +1130,31 @@
     ).astype(jnp.int32)
     cosine, sine = rope_tables(jnp.concatenate([value[1] for value in layouts]))
 
-    tokens_late = after(tokens_all, feed_parts)
-    normed_one, heads, gains, wide = project(place, tokens_late, attention_blocks, cosine, sine)
+    cosine = after(cosine, came[0])
+    normed_one, heads, gains, wide = project(place, tokens_all, attention_blocks, cosine, sine)
     gain_one, gain_two = gains[0], gains[1]
-    heads = after(heads, cotangent_parts, feed_shards[0])
-    mixed, totals, *partial = attend(place, heads, starts, attention_blocks, sequence)
+    heads = after(heads, cotangent_parts)
+    mixed, totals, *partial = attend(place, heads, starts, output_blocks, sequence)
     cotangent_parts = gather_second(cotangent_parts)
-    partial = after(partial, cotangent_parts, feed_shards[1:], one)
-    parts = core_stage(*partial)
+    partial = after(partial, cotangent_parts, one)
+    one = relay(one)
+    parts = after(core_stage(*partial), one)
     one = relay(one)
     cotangent_all = gather_last(after(cotangent_parts, parts))
-    parts = chip_stage(parts, cotangent_all, one)
-    one = relay(one)
-    attention = last_stage(parts, one)
+    parts = after(chip_stage(parts, one), cotangent_all)
+    two = relay([after(feed_shards[1], one)])
+    attention = last_stage(parts, two)
 
     hidden = tokens.astype(f32)
     inverse_one = norm_inverse(hidden)
     hidden_one = hidden + attention
     inverse_two = norm_inverse(hidden_one)
     normed_two = (hidden_one * inverse_two * gain_two).astype(low_type)
-    two = relay([after(feed_shards[1], one)])
-    normed_parts = gather_second(after(gather_first(normed_two)))
-    normed_two_all = gather_last(after(normed_parts, two))
+    two = relay(two)
+    normed_parts = after(gather_second(gather_first(normed_two)), two)
+    two = relay(two)
+    normed_two_all = gather_last(normed_parts)
     hid, grad_pair = feed(place, normed_two_all, cotangent_all, one)
-    two = relay(two)
-    grad_pair = after(grad_pair, two)
-    two = relay(two)
     theirs, mine = sides(weight_grad(place, blocks, [(normed_two_all, grad_pair), (cotangent_all, hid)]))
     theirs_one = deliver(theirs)
     others_one = [swap(theirs_one[0])]
@@ -1069,102 +1162,94 @@
     hid_two, grad_pair_two = feed(place, normed_late, cotangent_all, two)
     partial = spread(place, after([grad_pair, grad_pair_two], others_one), [one, two], 0)
     partial = after(partial, theirs_one)
-    others_one += [swap(after(value, partial)) for value in theirs_one[1:]]
-    mine_one = deliver(after(mine, theirs_one))
+    others_one += [swap(after(value, partial)) for value in theirs_one[1:3]]
     parts = core_stage(*partial)
-    theirs, mine = sides(
+    mine_one = deliver(after(mine, partial))
+    theirs, mine_later = sides(
         weight_grad(place, blocks, [(normed_two_all, after(grad_pair_two, *parts)), (cotangent_all, hid_two)])
     )
-    parts = chip_stage(parts, theirs[0], mine_one[1::2])
-    theirs_two = deliver(after(theirs, mine_one[1:]))
+    parts = after(chip_stage(parts, theirs[0]), others_one, mine_one[1:2])
+    theirs_two = deliver(theirs)
     feed_partial = spread(place, after([hid, hid_two], *parts), [one, two], 2)
-    grad_normed_two = last_stage(parts, *feed_partial)
-    grad_normed_two = after(grad_normed_two, mine_one, others_one[1])
+    grad_normed_two = last_stage(parts, *feed_partial, theirs_two[1:2], theirs_two[3:])
 
     grad_hidden_one = cotangent.astype(f32) + norm_backward(
         hidden_one, inverse_two, gain_two, grad_normed_two
     )
     grad_gain_two = jnp.sum(grad_normed_two * hidden_one * inverse_two, axis=0)
     grad_hidden_all = lax.all_gather(grad_hidden_one.astype(low_type), plane, axis=0, tiled=True)
-    grad_hidden_all = after(grad_hidden_all, theirs_two, others_one)
-    mine_two = deliver(after(mine, grad_hidden_all))
-    others_two = [swap(after(value, grad_hidden_all)) for value in theirs_two]
+    feed_parts = chip_stage(core_stage(*after(feed_partial, grad_hidden_one)))
+    feed_came = last_send(feed_parts)
+    grad_hidden_all = after(grad_hidden_all, theirs_two, mine_one[3:], feed_came)
+    mine_two = deliver(after(mine_later, grad_hidden_all))
+    others_one.append(swap(after(theirs_one[3], grad_hidden_all)))
+    others_two = [swap(after(value, grad_hidden_all)) for value in theirs_two[:2]]
 
     grad_query, grad_pair = attend_grad(
-        place, grad_hidden_all, heads, totals, starts, cosine, sine, attention_blocks, sequence
+        place, grad_hidden_all, heads, totals, starts, cosine, sine, output_blocks, sequence
     )
     *partial, gain_sums = project_grad(place, grad_query, grad_pair, tokens_all, wide)
-    partial = after(partial, others_two[:3], mine_two)
+    grad_gains = jnp.stack([jnp.sum(gain_sums, axis=0), grad_gain_two], axis=0)
+    grad_gains = jnp.concatenate([grad_gains, jnp.zeros((6, width), f32)], axis=0).astype(low_type)
+    partial = after(partial, mine_one, others_one, others_two, mine_two[1:2])
     parts = core_stage(*partial)
-    project_theirs, project_mine = sides(
+    others_two += [swap(after(value, partial)) for value in theirs_two[2:]]
+    theirs, mine = sides(
         weight_grad(
             place,
             blocks,
-            [(normed_one, after(grad_query, *parts)), (normed_one, grad_pair)],
-            projection_selector(),
+            [
+                (normed_one, after(grad_query, *parts)),
+                (normed_one, grad_pair),
+                (grad_gains, jnp.asarray(gains_selector(), low_type)),
+                (grad_hidden_all, mixed),
+            ],
+            gradient_selectors(),
         )
     )
-    parts = chip_stage(parts, project_theirs[0])
-    project_theirs = deliver(project_theirs)
-    project_mine = deliver(project_mine)
-    output_theirs, output_mine = sides(
-        weight_grad(place, blocks, [(grad_hidden_all, after(mixed, *parts))], output_selector())
-    )
-    feed_parts = core_stage(*after(feed_partial, output_theirs[0]))
-    grad_normed_one = last_stage(parts, output_theirs[0], feed_parts)
-    output_theirs, output_mine = deliver(output_theirs), deliver(output_mine)
+    parts = after(chip_stage(parts, theirs[0]), mine_two, others_two[:3])
+    theirs_last = deliver(theirs)
+    came = last_send(parts)
+    grad_normed_one = last_stage(parts, came=came)
+    mine_one, others_one, mine_two, others_two, theirs_last = after(
+        (mine_one, others_one, mine_two, others_two, theirs_last), came
+    )
+    mine_last = deliver(after(mine, theirs_last))
+    others_last = [swap(theirs_last[0]), swap(jnp.stack(theirs_last[1:]))]
+    block_output = (hidden_one + last_stage(feed_parts, came=feed_came)).astype(low_type)
 
     token_grad = (
         grad_hidden_one + norm_backward(hidden, inverse_one, gain_one, grad_normed_one)
     ).astype(low_type)
 
-    grad_gains = jnp.stack([jnp.sum(gain_sums, axis=0), grad_gain_two], axis=0)
-    grad_gains = plane_sum(grad_gains)
-    start = (2 * spot + side) * rows
-    if direct:
-        found = [grad_gains] + [hop(grad_gains, -step) for step in range(1, ring)]
-        found = [lax.dynamic_slice_in_dim(value, start, rows, 1) for value in found]
-        gains_total = jnp.roll(jnp.stack(found), spot, axis=0)
-    else:
-        gains_all = lax.all_gather(grad_gains, "ring", axis=0, tiled=False)
-        gains_all = jnp.sum(gains_all.reshape(REPLICA_GROUPS, per_group, 2, width), axis=1)
-        gains_total = lax.dynamic_slice_in_dim(gains_all, start, rows, 2)
-
     updated = feed_update(
-        after(place, grad_normed_one, project_theirs, gains_total, others_two),
+        place,
         [mine_one, mine_two],
         [others_one, others_two],
         (first_gating, second_gating, gating_weight, moment_gating),
         (first_down, second_down, down_weight, moment_down),
     )
-    project_other = [swap(value) for value in project_theirs]
-    output_other = [swap(after(value, updated[0])) for value in output_theirs]
-    feed_parts = chip_stage(feed_parts, updated[0])
-    feed_out = last_stage(feed_parts)
-    block_output = (hidden_one + feed_out).astype(low_type)
-
-    def slots_to_groups(own, other):
-        both = [jnp.stack(own), jnp.stack(other)]
-        both = [jnp.where(near, both[0], both[1]), jnp.where(near, both[1], both[0])]
-        if direct:
-            both = [jnp.roll(value, spot, axis=0) for value in both]
-        return [value.astype(f32) for value in both]
-
-    project_totals = slots_to_groups(project_mine, project_other)
-    output_totals = slots_to_groups(output_mine, output_other)
-    query_total = jnp.concatenate([value[..., :flat] for value in project_totals], axis=-1)
+    mine_last = after(mine_last, updated[0])
+    others_last = [others_last[0]] + [others_last[1][k] for k in range(REPLICA_GROUPS - 1)]
+    attention_updated = attention_update(
+        place,
+        mine_last,
+        others_last,
+        (first_query, second_query, query_weight, moment_query),
+        (first_output, second_output, output_weight, moment_output),
+    )
+    qry, out = attention_updated[:6], attention_updated[6:]
+    columns = slice(flat, flat + 2 * HEAD_WIDTH + 2)
+    both = [jnp.stack([value[:, columns] for value in part]) for part in (mine_last, others_last)]
+    both = [jnp.where(near, both[0], both[1]), jnp.where(near, both[1], both[0])]
+    if direct:
+        both = [jnp.roll(value, spot, axis=0) for value in both]
+    both = [value.astype(f32) for value in both]
     pair_total = jnp.concatenate(
-        [
-            value[..., flat : flat + 2 * HEAD_WIDTH].reshape(REPLICA_GROUPS, rows, 2, HEAD_WIDTH)
-            for value in project_totals
-        ],
-        axis=-1,
-    )
-    output_total = jnp.concatenate(output_totals, axis=-1)
-
-    qry = optimize(
-        query_weight, query_total, first_query, second_query, moment_query, inner_rates[0], inner_decays[0]
-    )
+        [value[..., : 2 * HEAD_WIDTH].reshape(REPLICA_GROUPS, rows, 2, HEAD_WIDTH) for value in both], axis=-1
+    )
+    gains_total = jnp.swapaxes(both[0][..., 2 * HEAD_WIDTH :] + both[1][..., 2 * HEAD_WIDTH :], 1, 2)
+    gains_total = tensor_sum(gains_total)
     kvl = optimize(
         keyvalue_weight_full,
         pair_total,
@@ -1173,9 +1258,6 @@
         keyvalue_outer_momentum,
         inner_rates[1],
         inner_decays[1],
-    )
-    out = optimize(
-        output_weight, output_total, first_output, second_output, moment_output, inner_rates[2], inner_decays[2]
     )
     gns = optimize(
         norm_gains, gains_total, first_gains, second_gains, moment_gains, inner_rates[5], inner_decays[5]

time: 1150 us -> 1010 us (0.88)
  waiting for transfers between devices: 449 us -> 364 us
  starting transfers between devices: 169 us -> 114 us
  Pallas kernels: 367 us -> 380 us
    ppermute x36 -> x30, waiting for transfers between devices: 237 us -> 153 us  [hop(): lax.ppermute(value, 'ring', [(i, (i + step) % ring) for i in range(ring)])]
    ppermute x36 -> x30, starting transfers between devices: 109 us -> 71.4 us  [hop(): lax.ppermute(value, 'ring', [(i, (i + step) % ring) for i in range(ring)])]
    ppermute x33 -> x27, starting transfers between devices: 45.2 us -> 27.8 us  [swap(): return lax.ppermute(value, 'pair', [(0, 1), (1, 0)])]
    pallas_call x4, Pallas kernels: 87.3 us -> 104 us  [the longest x3 87.8 us: weight_grad(): pl.pallas_call(functools.partial(weight_grad_kernel, spans, selected, spl...]
    ppermute x33 -> x27, waiting for transfers between devices: 129 us -> 119 us  [swap(): return lax.ppermute(value, 'pair', [(0, 1), (1, 0)])]
    unnamed x163 -> x152, local copies, waits for them, and re-layouts: 24.8 us -> 27.1 us
  transfers between devices with their start and end apart: 91 -> 79, of which waited for: 42 -> 27; matrix products, arithmetic and copies ran while one was open for 10% -> 10% of each run, Pallas kernels for 32% -> 38%
where the time goes in v2:
time: 1010 us; the launch traced here: 1000 us
  Pallas kernels  380 us (38%)
  waiting for transfers between devices  364 us (36%)
  starting transfers between devices  114 us (11%)
  other arithmetic  81.8 us (8%)
  local copies, waits for them, and re-layouts  47.2 us (5%)
  between operations  16 us (2%)
    ppermute x30, waiting for transfers between devices, hop(): lax.ppermute(value, 'ring', [(i, (i + step) % ring) for i in range(ring)])  153 us
    ppermute x27, waiting for transfers between devices, swap(): return lax.ppermute(value, 'pair', [(0, 1), (1, 0)])  119 us
    pallas_call x3, Pallas kernels, weight_grad(): pl.pallas_call(functools.partial(weight_grad_kernel, spans, selected, spl...  87.8 us
    ppermute x20, waiting for transfers between devices, across(): return lax.ppermute(value, 'tensor', [(i, i ^ bit) for i in range(count)])  85.2 us
    ppermute x30, starting transfers between devices, hop(): lax.ppermute(value, 'ring', [(i, (i + step) % ring) for i in range(ring)])  71.4 us
    pallas_call x1, Pallas kernels, feed_update(): pl.pallas_call(feed_update_kernel, grid_spec=pltpu.PrefetchScalarGridSpec...  62.4 us
    pallas_call x2, Pallas kernels, spread(): pl.pallas_call(functools.partial(spread_kernel, tuple((len(blocks) for bl...  47.6 us
    pallas_call x2, Pallas kernels, feed(): pl.pallas_call(functools.partial(feed_kernel, len(blocks), tiles), grid_s...  45.5 us
  transfers between devices with their start and end apart: 79, of which 27 were waited for; matrix products, arithmetic and copies ran while one was open for 10% of the time, Pallas kernels for 38%

profile of v2, /device:TPU:0, one launch (start us, length us, event | category | flops | bytes accessed | tf_op | source)
XLA Modules:
  0.0 1002.3 jit_solution(247669188574869872)
XLA Ops:
  10.9 3.0 collective-permute-start
  15.5 6.2 collective-permute-done.4
  22.4 3.7 fusion.34
  26.6 2.1 collective-permute-start.1
  28.6 9.1 pack_feed.1
  39.8 2.5 pad_maximum_fusion.4
  42.3 2.6 collective-permute-start.2
  46.3 31.0 %collective-permute-done.8 = bf16[320,320]{1,0:T(8,128)(2,1)S(1)} collective-permute-done((bf16[320,320]{1,0:T(8,128)(2,1)S(1)}, bf16[320,320]{1,0:T(8,128)(2,1)S(1)}, u32[]{:S(2)}, u32[]{:S(2)}) %collective-permute-start.8) | collective-permute-done | bytes 204832 | tf_op jit(solution)/shard_map/ppermute | solution.py:981
  80.8 2.9 collective-permute-start.11
  84.8 5.7 all-gather.3.cloned.1.call-done.tokens
  94.7 20.2 %projection.1 = (bf16[2048,2560]{1,0:T(8,128)(2,1)}, bf16[2048,768]{1,0:T(8,128)(2,1)}, f32[8,2560]{1,0:T(8,128)}, bf16[2560,768]{1,0:T(8,128)(2,1)}) custom-call(s32[4]{0:T(128)} %pad_add_fusion.1.place_ref, bf16[2048,2560]{1,0:T(8,128)(2,1)} %all-gather.3.cloned.1.call-done.tokens, bf16[640,512]{1,0:T(8,128)(2,1)} %copy-done.39, ...), custom_call_target="tpu_custom_call" | custom-call | flops 8053063680 | bytes 32768000 | tf_op jit(solution)/shard_map/projection/pallas_call | solution.py:173
  114.9 18.8 %collective-permute-start.14 = (bf16[640,1152]{1,0:T(8,128)(2,1)S(1)}, bf16[640,1152]{1,0:T(8,128)(2,1)S(1)}, u32[]{:S(2)}, u32[]{:S(2)}) collective-permute-start(bf16[640,1152]{1,0:T(8,128)(2,1)S(1)} %pad_maximum_fusion.8.refs_0_.refs_2_), channel_id=1, source_target_pairs={{0,8},{8,16},{16,24},{24,0},{1,9},{9,17},{17,25},{25,1},{2,10},{10... | collective-permute-start | bytes 4423688 | tf_op jit(solution)/shard_map/ppermute | solution.py:1020
  138.3 31.4 %attention.1 = (bf16[2048,512]{1,0:T(8,128)(2,1)}, f32[8,2048]{1,0:T(8,128)}, bf16[1024,2560]{1,0:T(8,128)(2,1)}, bf16[1024,2560]{1,0:T(8,128)(2,1)}) custom-call(s32[4]{0:T(128)} %pad_add_fusion.1.place_ref, bf16[2048,768]{1,0:T(8,128)(2,1)} %get-tuple-element.226.query.key.value, bf16[2048,768]{1,0:T(8,128)(2,1)} %get-tuple-element.226.query.key.value, ...), custom_call_target="tpu_custom_call" | custom-call | flops 20000000000 | bytes 20971520 | tf_op jit(solution)/shard_map/attention/pallas_call | solution.py:267
  169.9 23.4 %collective-permute-start.16 = (bf16[640,1152]{1,0:T(8,128)(2,1)S(1)}, bf16[640,1152]{1,0:T(8,128)(2,1)S(1)}, u32[]{:S(2)}, u32[]{:S(2)}) collective-permute-start(bf16[640,1152]{1,0:T(8,128)(2,1)S(1)} %collective-permute-done.14.refs_1_.refs_3_), channel_id=1, source_target_pairs={{0,8},{8,16},{16,24},{24,0},{1,9},{9,17},{17,25},{25,1},{2,10},{10... | collective-permute-start | bytes 4423688 | tf_op jit(solution)/shard_map/ppermute | solution.py:1020
  197.6 27.9 %collective-permute-done.16.refs_2_.refs_4_ = bf16[640,1152]{1,0:T(8,128)(2,1)S(1)} collective-permute-done((bf16[640,1152]{1,0:T(8,128)(2,1)S(1)}, bf16[640,1152]{1,0:T(8,128)(2,1)S(1)}, u32[]{:S(2)}, u32[]{:S(2)}) %collective-permute-start.16) | collective-permute-done | bytes 1474592 | tf_op jit(solution)/shard_map/ppermute | solution.py:1020
  232.4 2.5 collective-permute-start.19
  236.9 18.6 %collective-permute-done.23 = bf16[320,1536]{1,0:T(8,128)(2,1)S(1)} collective-permute-done((bf16[320,1536]{1,0:T(8,128)(2,1)S(1)}, bf16[320,1536]{1,0:T(8,128)(2,1)S(1)}, u32[]{:S(2)}, u32[]{:S(2)}) %collective-permute-start.23) | collective-permute-done | bytes 983072 | tf_op jit(solution)/shard_map/ppermute | solution.py:981
  255.8 12.9 %collective-permute-done.19.refs_3_.refs_5_ = bf16[640,1152]{1,0:T(8,128)(2,1)} collective-permute-done((bf16[640,1152]{1,0:T(8,128)(2,1)S(1)}, bf16[640,1152]{1,0:T(8,128)(2,1)}, u32[]{:S(2)}, u32[]{:S(2)}) %collective-permute-start.19) | collective-permute-done | bytes 1474592 | tf_op jit(solution)/shard_map/ppermute | solution.py:1020
  269.5 13.6 %collective-permute-done.18 = bf16[2,128,2560]{2,1,0:T(8,128)(2,1)S(1)} collective-permute-done((bf16[2,128,2560]{2,1,0:T(8,128)(2,1)S(1)}, bf16[2,128,2560]{2,1,0:T(8,128)(2,1)S(1)}, u32[]{:S(2)}, u32[]{:S(2)}) %collective-permute-start.18) | collective-permute-done | bytes 1310752 | tf_op jit(solution)/shard_map/ppermute | solution.py:981
  293.9 20.8 %collective-permute-done.24.refs_1_.refs_7_ = bf16[640,1536]{1,0:T(8,128)(2,1)S(1)} collective-permute-done((bf16[640,1536]{1,0:T(8,128)(2,1)S(1)}, bf16[640,1536]{1,0:T(8,128)(2,1)S(1)}, u32[]{:S(2)}, u32[]{:S(2)}) %collective-permute-start.24) | collective-permute-done | bytes 1966112 | tf_op jit(solution)/shard_map/ppermute | solution.py:1020
  318.3 13.1 %collective-permute-done.25 = bf16[128,2560]{1,0:T(8,128)(2,1)S(1)} collective-permute-done((bf16[128,2560]{1,0:T(8,128)(2,1)S(1)}, bf16[128,2560]{1,0:T(8,128)(2,1)S(1)}, u32[]{:S(2)}, u32[]{:S(2)}) %collective-permute-start.25) | collective-permute-done | bytes 655392 | tf_op jit(solution)/shard_map/ppermute | solution.py:985
  333.7 28.9 %collective-permute-done.29.refs_2_.refs_8_ = bf16[640,1536]{1,0:T(8,128)(2,1)S(1)} collective-permute-done((bf16[640,1536]{1,0:T(8,128)(2,1)S(1)}, bf16[640,1536]{1,0:T(8,128)(2,1)S(1)}, u32[]{:S(2)}, u32[]{:S(2)}) %collective-permute-start.29) | collective-permute-done | bytes 1966112 | tf_op jit(solution)/shard_map/ppermute | solution.py:1020
  365.1 8.6 collective-permute-done.30
  383.5 20.8 %feed.2 = (bf16[2048,384]{1,0:T(8,128)(2,1)}, bf16[2048,768]{1,0:T(8,128)(2,1)}) custom-call(s32[4]{0:T(128)} %pad_add_fusion.1.place_ref, bf16[2048,2560]{1,0:T(8,128)(2,1)} %slice_dynamic-update-slice_fusion.normed.refs_0_, bf16[2048,2560]{1,0:T(8,128)(2,1)} %copy-done.44, bf16[640,1152]{1,0:T(8,128)(2,1)} %copy-done.3, bf16[640,1152]{1,0:T(8,128)(2,1)} %copy-done.8, ...), custom_call_target="tpu_custom_call" | custom-call | flops 12079595520 | bytes 26869760 | tf_op jit(solution)/shard_map/feed/pallas_call | solution.py:528
  404.3 23.5 %weight_grad.3 = (bf16[320,1152]{1,0:T(8,128)(2,1)}, bf16[320,1152]{1,0:T(8,128)(2,1)}, bf16[320,1152]{1,0:T(8,128)(2,1)}, bf16[320,1152]{1,0:T(8,128)(2,1)}, bf...) custom-call(s32[4]{0:T(128)} %pad_add_fusion.1.place_ref, ...), custom_call_target="tpu_custom_call" | custom-call | flops 12079595520 | bytes 25690112 | tf_op jit(solution)/shard_map/weight_grad/pallas_call | solution.py:652
  429.3 2.0 collective-permute-start.35
  431.3 24.7 %feed.3 = (bf16[2048,512]{1,0:T(8,128)(2,1)}, bf16[2048,1024]{1,0:T(8,128)(2,1)}) custom-call(s32[4]{0:T(128)} %pad_add_fusion.1.place_ref, bf16[2048,2560]{1,0:T(8,128)(2,1)} %slice_dynamic-update-slice_fusion.normed.refs_0_, bf16[2048,2560]{1,0:T(8,128)(2,1)} %copy-done.44, bf16[640,1536]{1,0:T(8,128)(2,1)} %copy-done.2, bf16[640,1536]{1,0:T(8,128)(2,1)} %copy-done.6, ...), custom_call_target="tpu_custom_call" | custom-call | flops 16106127360 | bytes 28835840 | tf_op jit(solution)/shard_map/feed/pallas_call | solution.py:528
  456.0 28.7 %spread.2 = (bf16[1024,2560]{1,0:T(8,128)(2,1)}, bf16[1024,2560]{1,0:T(8,128)(2,1)}) custom-call(s32[4]{0:T(128)} %pad_add_fusion.1.place_ref, bf16[2048,768]{1,0:T(8,128)(2,1)} %get-tuple-element.261.refs_2_.refs_0_, bf16[2048,1024]{1,0:T(8,128)(2,1)} %get-tuple-element.270.refs_1_.refs_2_, bf16[640,1152]{1,0:T(8,128)(2,1)} %copy-done.3, ...), custom_call_target="tpu_custom_call" | custom-call | flops 1 | bytes 1 | tf_op jit(solution)/shard_map/spread/pallas_call | solution.py:571
  484.7 8.5 collective-permute-done.34
  495.2 6.8 collective-permute-done.36
  502.1 2.7 fusion.15
  504.8 3.8 fusion.17
  511.4 27.5 %weight_grad.4 = (bf16[320,1536]{1,0:T(8,128)(2,1)}, bf16[320,1536]{1,0:T(8,128)(2,1)}, bf16[320,1536]{1,0:T(8,128)(2,1)}, bf16[320,1536]{1,0:T(8,128)(2,1)}, bf...) custom-call(s32[4]{0:T(128)} %pad_add_fusion.1.place_ref, ...), custom_call_target="tpu_custom_call" | custom-call | flops 16106127360 | bytes 27262976 | tf_op jit(solution)/shard_map/weight_grad/pallas_call | solution.py:652
  538.9 2.4 collective-permute-done.37
  541.3 15.0 %collective-permute-done.38 = bf16[2,128,2560]{2,1,0:T(8,128)(2,1)} collective-permute-done((bf16[2,128,2560]{2,1,0:T(8,128)(2,1)}, bf16[2,128,2560]{2,1,0:T(8,128)(2,1)}, u32[]{:S(2)}, u32[]{:S(2)}) %collective-permute-start.38) | collective-permute-done | bytes 1310752 | tf_op jit(solution)/shard_map/ppermute | solution.py:981
  564.1 18.9 %spread.3 = (bf16[1024,2560]{1,0:T(8,128)(2,1)}, bf16[1024,2560]{1,0:T(8,128)(2,1)}) custom-call(s32[4]{0:T(128)} %pad_add_fusion.1.place_ref, bf16[2048,384]{1,0:T(8,128)(2,1)} %get-tuple-element.283.refs_3_.refs_0_, bf16[2048,512]{1,0:T(8,128)(2,1)} %get-tuple-element.284.refs_3_.refs_1_, bf16[640,1152]{1,0:T(8,128)(2,1)} %copy-done.3, ...), custom_call_target="tpu_custom_call" | custom-call | flops 1 | bytes 1 | tf_op jit(solution)/shard_map/spread/pallas_call | solution.py:571
  583.1 5.5 collective-permute-done.45
  592.4 2.9 fusion.45
  595.3 8.9 collective-permute-done.46
  609.3 45.5 %collective-permute-done.47 = bf16[2,128,2560]{2,1,0:T(8,128)(2,1)S(1)} collective-permute-done((bf16[2,128,2560]{2,1,0:T(8,128)(2,1)S(1)}, bf16[2,128,2560]{2,1,0:T(8,128)(2,1)S(1)}, u32[]{:S(2)}, u32[]{:S(2)}) %collective-permute-start.47) | collective-permute-done | bytes 1310752 | tf_op jit(solution)/shard_map/ppermute | solution.py:985
  656.0 2.7 fusion.7
  662.0 2.4 collective-permute-start.53
  664.4 22.4 %collective-permute-done.51 = bf16[320,1536]{1,0:T(8,128)(2,1)S(1)} collective-permute-done((bf16[320,1536]{1,0:T(8,128)(2,1)S(1)}, bf16[320,1536]{1,0:T(8,128)(2,1)S(1)}, u32[]{:S(2)}, u32[]{:S(2)}) %collective-permute-start.51) | collective-permute-done | bytes 983072 | tf_op jit(solution)/shard_map/ppermute | solution.py:1020
  691.2 2.5 collective-permute-start.57
  693.8 36.7 %attention_grad.1 = (bf16[2048,512]{1,0:T(8,128)(2,1)}, bf16[2048,256]{1,0:T(8,128)(2,1)}) custom-call(s32[4]{0:T(128)} %pad_add_fusion.1.place_ref, bf16[2048,2560]{1,0:T(8,128)(2,1)} %all-gather.5.cloned.1.call-done.grad_hidden.refs_3_, bf16[2048,768]{1,0:T(8,128)(2,1)} %get-tuple-element.226.query.key.value, ...), custom_call_target="tpu_custom_call" | custom-call | flops 30000001024 | bytes 20971520 | tf_op jit(solution)/shard_map/attention_grad/pallas_call | solution.py:364
  730.5 23.3 %projection_grad.1 = (bf16[1024,2560]{1,0:T(8,128)(2,1)}, bf16[1024,2560]{1,0:T(8,128)(2,1)}, f32[8,2560]{1,0:T(8,128)}) custom-call(s32[4]{0:T(128)} %pad_add_fusion.1.place_ref, bf16[2048,512]{1,0:T(8,128)(2,1)} %get-tuple-element.320.grad_query.refs_4_, bf16[2048,256]{1,0:T(8,128)(2,1)} %get-tuple-element.302.grad_pair.refs_5_, ...), custom_call_target="tpu_custom_call" | custom-call | flops 1 | bytes 1 | tf_op jit(solution)/shard_map/projection_grad/pallas_call | solution.py:435
  756.3 2.6 convert_add_fusion.5
  758.9 2.3 convert_add_fusion.6
  764.3 3.1 fusion.23
  767.4 4.2 fusion.25
  773.6 2.0 fusion.22
  775.6 36.8 %weight_grad.5 = (bf16[320,896]{1,0:T(8,128)(2,1)}, bf16[320,896]{1,0:T(8,128)(2,1)}, bf16[320,896]{1,0:T(8,128)(2,1)}, bf16[320,896]{1,0:T(8,128)(2,1)}, bf16[3...) custom-call(s32[4]{0:T(128)} %pad_add_fusion.1.place_ref, ...), custom_call_target="tpu_custom_call" | custom-call | flops 9395240960 | bytes 45613056 | tf_op jit(solution)/shard_map/weight_grad/pallas_call | solution.py:652
  812.5 2.6 collective-permute-done.60
  818.6 9.2 collective-permute-done.61.refs_6_
  833.4 12.1 %collective-permute-done.64 = bf16[128,2560]{1,0:T(8,128)(2,1)S(1)} collective-permute-done((bf16[128,2560]{1,0:T(8,128)(2,1)S(1)}, bf16[128,2560]{1,0:T(8,128)(2,1)S(1)}, u32[]{:S(2)}, u32[]{:S(2)}) %collective-permute-start.64) | collective-permute-done | bytes 655392 | tf_op jit(solution)/shard_map/ppermute | solution.py:981
  848.5 17.1 %collective-permute-done.66.refs_15_ = bf16[320,1536]{1,0:T(8,128)(2,1)S(1)} collective-permute-done((bf16[320,1536]{1,0:T(8,128)(2,1)}, bf16[320,1536]{1,0:T(8,128)(2,1)S(1)}, u32[]{:S(2)}, u32[]{:S(2)}) %collective-permute-start.66) | collective-permute-done | bytes 983072 | tf_op jit(solution)/shard_map/ppermute | solution.py:981
  865.7 16.5 %collective-permute-done.68 = bf16[320,896]{1,0:T(8,128)(2,1)S(1)} collective-permute-done((bf16[320,896]{1,0:T(8,128)(2,1)S(1)}, bf16[320,896]{1,0:T(8,128)(2,1)S(1)}, u32[]{:S(2)}, u32[]{:S(2)}) %collective-permute-start.68) | collective-permute-done | bytes 573472 | tf_op jit(solution)/shard_map/ppermute | solution.py:1020
  883.7 2.0 collective-permute-start.71
  885.6 2.0 collective-permute-start.72
  890.6 62.4 %feed_update.1 = (f32[4,320,2,1792]{3,2,1,0:T(2,128)}, f32[4,320,2,1792]{3,2,1,0:T(2,128)}, f32[320,2,1792]{2,1,0:T(2,128)}, f32[320,2,1792]{2,1,0:T(2,128)}, f3...) custom-call(s32[4]{0:T(128)} %pad_add_fusion.1.place_ref, ...), custom_call_target="tpu_custom_call" | custom-call | bytes 154828800 | tf_op jit(solution)/shard_map/feed_update/pallas_call | solution.py:800
  953.0 3.6 fusion.4
  966.2 5.4 multiply_reduce_fusion.3
  974.1 16.0 %attention_update.1 = (f32[4,320,640]{2,1,0:T(8,128)}, f32[4,320,640]{2,1,0:T(8,128)}, f32[320,640]{1,0:T(8,128)}, f32[320,640]{1,0:T(8,128)}, f32[320,640]{1,0:...) custom-call(s32[4]{0:T(128)} %pad_add_fusion.1.place_ref, ...), custom_call_target="tpu_custom_call" | custom-call | bytes 36864000 | tf_op jit(solution)/shard_map/attention_update/pallas_call | solution.py:875
  991.5 1.9 copy.200
  (392 shorter events, 137.0 us)
Async XLA Ops:
  7.2 83.2 %all-gather.3.cloned.1.call-start = ((), (), s32[]{:S(2)}) async-start(), calls=%async_computation | async-start | bytes 11796480 | tf_op jit(solution)/shard_map/all_gather | solution.py:1089
  8.0 679.8 %all-gather.5.cloned.1.call-start = ((), (), s32[]{:S(2)}) async-start(), calls=%async_computation.1 | async-start | bytes 11796480 | tf_op jit(solution)/shard_map/all_gather | solution.py:1180
  26.6 51.6 %collective-permute-start.1 = (bf16[640,512]{1,0:T(8,128)(2,1)S(1)}, bf16[640,512]{1,0:T(8,128)(2,1)S(1)}, u32[]{:S(2)}, u32[]{:S(2)}) collective-permute-start(bf16[640,512]{1,0:T(8,128)(2,1)S(1)} %pad_maximum_fusion.13.refs_0_), channel_id=1, source_target_pairs={{0,8},{8,16},{16,24},{24,0},{1,9},{9,17},{17,25},{25,1},{2,10},{10... | collective-permute-start | bytes 1966088 | tf_op jit(solution)/shard_map/ppermute | solution.py:1020
  37.7 43.1 %collective-permute-start.5 = (bf16[320,1152]{1,0:T(8,128)(2,1)}, bf16[320,1152]{1,0:T(8,128)(2,1)S(1)}, u32[]{:S(2)}, u32[]{:S(2)}) collective-permute-start(bf16[320,1152]{1,0:T(8,128)(2,1)} %get-tuple-element.222), channel_id=1, source_target_pairs={{0,4},{4,0},{1,5},{5,1},{2,6},{6,2},{3,7},{7,3},{8,12},{12,8},{9,1... | collective-permute-start | bytes 2211848 | tf_op jit(solution)/shard_map/ppermute | solution.py:981
  39.3 38.0 %collective-permute-start.8 = (bf16[320,320]{1,0:T(8,128)(2,1)S(1)}, bf16[320,320]{1,0:T(8,128)(2,1)S(1)}, u32[]{:S(2)}, u32[]{:S(2)}) collective-permute-start(bf16[320,320]{1,0:T(8,128)(2,1)S(1)} %copy-done.41), channel_id=1, source_target_pairs={{0,4},{4,0},{1,5},{5,1},{2,6},{6,2},{3,7},{7,3},{8,12},{12,8},{9,1... | collective-permute-start | bytes 614408 | tf_op jit(solution)/shard_map/ppermute | solution.py:981
  42.3 41.6 %collective-permute-start.2 = (bf16[640,512]{1,0:T(8,128)(2,1)S(1)}, bf16[640,512]{1,0:T(8,128)(2,1)S(1)}, u32[]{:S(2)}, u32[]{:S(2)}) collective-permute-start(bf16[640,512]{1,0:T(8,128)(2,1)S(1)} %pad_maximum_fusion.13.refs_0_), channel_id=1, source_target_pairs={{0,16},{8,24},{16,0},{24,8},{1,17},{9,25},{17,1},{25,9},{2,18},{10... | collective-permute-start | bytes 1966088 | tf_op jit(solution)/shard_map/ppermute | solution.py:1020
  44.9 39.9 %collective-permute-start.3 = (bf16[640,512]{1,0:T(8,128)(2,1)S(1)}, bf16[640,512]{1,0:T(8,128)(2,1)}, u32[]{:S(2)}, u32[]{:S(2)}) collective-permute-start(bf16[640,512]{1,0:T(8,128)(2,1)S(1)} %pad_maximum_fusion.13.refs_0_), channel_id=1, source_target_pairs={{0,24},{8,0},{16,8},{24,16},{1,25},{9,1},{17,9},{25,17},{2,26},{10... | collective-permute-start | bytes 1966088 | tf_op jit(solution)/shard_map/ppermute | solution.py:1020
  78.2 58.8 %collective-permute-start.9 = (bf16[640,320]{1,0:T(8,128)(2,1)}, bf16[640,320]{1,0:T(8,128)(2,1)}, u32[]{:S(2)}, u32[]{:S(2)}) collective-permute-start(bf16[640,320]{1,0:T(8,128)(2,1)} %pad_maximum_fusion.16.refs_0_), channel_id=1, source_target_pairs={{0,8},{8,16},{16,24},{24,0},{1,9},{9,17},{17,25},{25,1},{2,10},{10... | collective-permute-start | bytes 1228808 | tf_op jit(solution)/shard_map/ppermute | solution.py:1020
  79.6 58.0 %collective-permute-start.10 = (bf16[640,320]{1,0:T(8,128)(2,1)}, bf16[640,320]{1,0:T(8,128)(2,1)}, u32[]{:S(2)}, u32[]{:S(2)}) collective-permute-start(bf16[640,320]{1,0:T(8,128)(2,1)} %pad_maximum_fusion.16.refs_0_), channel_id=1, source_target_pairs={{0,16},{8,24},{16,0},{24,8},{1,17},{9,25},{17,1},{25,9},{2,18},{10... | collective-permute-start | bytes 1228808 | tf_op jit(solution)/shard_map/ppermute | solution.py:1020
  80.8 56.9 %collective-permute-start.11 = (bf16[640,320]{1,0:T(8,128)(2,1)}, bf16[640,320]{1,0:T(8,128)(2,1)}, u32[]{:S(2)}, u32[]{:S(2)}) collective-permute-start(bf16[640,320]{1,0:T(8,128)(2,1)} %pad_maximum_fusion.16.refs_0_), channel_id=1, source_target_pairs={{0,24},{8,0},{16,8},{24,16},{1,25},{9,1},{17,9},{25,17},{2,26},{10... | collective-permute-start | bytes 1228808 | tf_op jit(solution)/shard_map/ppermute | solution.py:1020
  93.2 41.8 %collective-permute-start.7 = (bf16[128,2560]{1,0:T(8,128)(2,1)}, bf16[128,2560]{1,0:T(8,128)(2,1)S(1)}, u32[]{:S(2)}, u32[]{:S(2)}) collective-permute-start(bf16[128,2560]{1,0:T(8,128)(2,1)} %get-tuple-element.638), channel_id=1, source_target_pairs={{0,4},{4,0},{1,5},{5,1},{2,6},{6,2},{3,7},{7,3},{8,12},{12,8},{9,1... | collective-permute-start | bytes 1966088 | tf_op jit(solution)/shard_map/ppermute | solution.py:981
  114.9 54.8 %collective-permute-start.14 = (bf16[640,1152]{1,0:T(8,128)(2,1)S(1)}, bf16[640,1152]{1,0:T(8,128)(2,1)S(1)}, u32[]{:S(2)}, u32[]{:S(2)}) collective-permute-start(bf16[640,1152]{1,0:T(8,128)(2,1)S(1)} %pad_maximum_fusion.8.refs_0_.refs_2_), channel_id=1, source_target_pairs={{0,8},{8,16},{16,24},{24,0},{1,9},{9,17},{17,25},{25,1},{2,10},{10... | collective-permute-start | bytes 4423688 | tf_op jit(solution)/shard_map/ppermute | solution.py:1020
  135.0 34.8 %collective-permute-start.12 = (bf16[2,128,2560]{2,1,0:T(8,128)(2,1)S(1)}, bf16[2,128,2560]{2,1,0:T(8,128)(2,1)}, u32[]{:S(2)}, u32[]{:S(2)}) collective-permute-start(bf16[2,128,2560]{2,1,0:T(8,128)(2,1)S(1)} %pad_maximum_fusion.9), channel_id=1, source_target_pairs={{0,4},{4,0},{1,5},{5,1},{2,6},{6,2},{3,7},{7,3},{8,12},{12,8},{9,1... | collective-permute-start | bytes 3932168 | tf_op jit(solution)/shard_map/ppermute | solution.py:981
  137.0 32.7 %collective-permute-start.13 = (bf16[2,128,2560]{2,1,0:T(8,128)(2,1)S(1)}, bf16[2,128,2560]{2,1,0:T(8,128)(2,1)}, u32[]{:S(2)}, u32[]{:S(2)}) collective-permute-start(bf16[2,128,2560]{2,1,0:T(8,128)(2,1)S(1)} %pad_maximum_fusion.10), channel_id=1, source_target_pairs={{0,2},{1,3},{2,0},{3,1},{4,6},{5,7},{6,4},{7,5},{8,10},{9,11},{10,... | collective-permute-start | bytes 3932168 | tf_op jit(solution)/shard_map/ppermute | solution.py:985
  169.9 55.6 %collective-permute-start.16 = (bf16[640,1152]{1,0:T(8,128)(2,1)S(1)}, bf16[640,1152]{1,0:T(8,128)(2,1)S(1)}, u32[]{:S(2)}, u32[]{:S(2)}) collective-permute-start(bf16[640,1152]{1,0:T(8,128)(2,1)S(1)} %collective-permute-done.14.refs_1_.refs_3_), channel_id=1, source_target_pairs={{0,8},{8,16},{16,24},{24,0},{1,9},{9,17},{17,25},{25,1},{2,10},{10... | collective-permute-start | bytes 4423688 | tf_op jit(solution)/shard_map/ppermute | solution.py:1020
  230.8 53.0 %collective-permute-start.20 = (bf16[1024,2560]{1,0:T(8,128)(2,1)S(1)}, bf16[1024,2560]{1,0:T(8,128)(2,1)S(1)}, u32[]{:S(2)}, u32[]{:S(2)}) collective-permute-start(bf16[1024,2560]{1,0:T(8,128)(2,1)S(1)} %bitcast_dynamic-update-slice_fusion.17), channel_id=1, source_target_pairs={{0,1},{1,0},{2,3},{3,2},{4,5},{5,4},{6,7},{7,6},{8,9},{9,8},{10,11... | collective-permute-start | bytes 15728648 | tf_op jit(solution)/shard_map/ppermute | solution.py:985
  230.9 24.6 %collective-permute-start.23 = (bf16[320,1536]{1,0:T(8,128)(2,1)S(1)}, bf16[320,1536]{1,0:T(8,128)(2,1)S(1)}, u32[]{:S(2)}, u32[]{:S(2)}) collective-permute-start(bf16[320,1536]{1,0:T(8,128)(2,1)S(1)} %copy-done.51), channel_id=1, source_target_pairs={{0,4},{4,0},{1,5},{5,1},{2,6},{6,2},{3,7},{7,3},{8,12},{12,8},{9,1... | collective-permute-start | bytes 2949128 | tf_op jit(solution)/shard_map/ppermute | solution.py:981
  232.4 36.3 %collective-permute-start.19 = (bf16[640,1152]{1,0:T(8,128)(2,1)S(1)}, bf16[640,1152]{1,0:T(8,128)(2,1)}, u32[]{:S(2)}, u32[]{:S(2)}) collective-permute-start(bf16[640,1152]{1,0:T(8,128)(2,1)S(1)} %collective-permute-done.16.refs_2_.refs_4_), channel_id=1, source_target_pairs={{0,8},{8,16},{16,24},{24,0},{1,9},{9,17},{17,25},{25,1},{2,10},{10... | collective-permute-start | bytes 4423688 | tf_op jit(solution)/shard_map/ppermute | solution.py:1020
  234.9 34.6 %collective-permute-start.17 = (bf16[2,128,2560]{2,1,0:T(8,128)(2,1)S(1)}, bf16[2,128,2560]{2,1,0:T(8,128)(2,1)S(1)}, u32[]{:S(2)}, u32[]{:S(2)}) collective-permute-start(bf16[2,128,2560]{2,1,0:T(8,128)(2,1)S(1)} %fusion.11), channel_id=1, source_target_pairs={{0,2},{1,3},{2,0},{3,1},{4,6},{5,7},{6,4},{7,5},{8,10},{9,11},{10,... | collective-permute-start | bytes 3932168 | tf_op jit(solution)/shard_map/ppermute | solution.py:985
  236.4 46.7 %collective-permute-start.18 = (bf16[2,128,2560]{2,1,0:T(8,128)(2,1)S(1)}, bf16[2,128,2560]{2,1,0:T(8,128)(2,1)S(1)}, u32[]{:S(2)}, u32[]{:S(2)}) collective-permute-start(bf16[2,128,2560]{2,1,0:T(8,128)(2,1)S(1)} %get-tuple-element.236), channel_id=1, source_target_pairs={{0,4},{4,0},{1,5},{5,1},{2,6},{6,2},{3,7},{7,3},{8,12},{12,8},{9,1... | collective-permute-start | bytes 3932168 | tf_op jit(solution)/shard_map/ppermute | solution.py:981
  268.7 46.0 %collective-permute-start.24 = (bf16[640,1536]{1,0:T(8,128)(2,1)S(1)}, bf16[640,1536]{1,0:T(8,128)(2,1)S(1)}, u32[]{:S(2)}, u32[]{:S(2)}) collective-permute-start(bf16[640,1536]{1,0:T(8,128)(2,1)S(1)} %pad_maximum_fusion.1.refs_0_.refs_6_), channel_id=1, source_target_pairs={{0,8},{8,16},{16,24},{24,0},{1,9},{9,17},{17,25},{25,1},{2,10},{10... | collective-permute-start | bytes 5898248 | tf_op jit(solution)/shard_map/ppermute | solution.py:1020
  289.0 25.7 %collective-permute-start.21 = (bf16[128,2560]{1,0:T(8,128)(2,1)S(1)}, bf16[128,2560]{1,0:T(8,128)(2,1)S(1)}, u32[]{:S(2)}, u32[]{:S(2)}) collective-permute-start(bf16[128,2560]{1,0:T(8,128)(2,1)S(1)} %slice_bitcast_fusion.17), channel_id=1, source_target_pairs={{0,4},{4,0},{1,5},{5,1},{2,6},{6,2},{3,7},{7,3},{8,12},{12,8},{9,1... | collective-permute-start | bytes 1966088 | tf_op jit(solution)/shard_map/ppermute | solution.py:981
  318.3 44.4 %collective-permute-start.29 = (bf16[640,1536]{1,0:T(8,128)(2,1)S(1)}, bf16[640,1536]{1,0:T(8,128)(2,1)S(1)}, u32[]{:S(2)}, u32[]{:S(2)}) collective-permute-start(bf16[640,1536]{1,0:T(8,128)(2,1)S(1)} %collective-permute-done.24.refs_1_.refs_7_), channel_id=1, source_target_pairs={{0,8},{8,16},{16,24},{24,0},{1,9},{9,17},{17,25},{25,1},{2,10},{10... | collective-permute-start | bytes 5898248 | tf_op jit(solution)/shard_map/ppermute | solution.py:1020
  331.4 31.2 %collective-permute-start.27 = (bf16[2,128,2560]{2,1,0:T(8,128)(2,1)S(1)}, bf16[2,128,2560]{2,1,0:T(8,128)(2,1)S(1)}, u32[]{:S(2)}, u32[]{:S(2)}) collective-permute-start(bf16[2,128,2560]{2,1,0:T(8,128)(2,1)S(1)} %pad_maximum_fusion.11), channel_id=1, source_target_pairs={{0,4},{4,0},{1,5},{5,1},{2,6},{6,2},{3,7},{7,3},{8,12},{12,8},{9,1... | collective-permute-start | bytes 3932168 | tf_op jit(solution)/shard_map/ppermute | solution.py:981
  333.5 29.1 %collective-permute-start.28 = (bf16[2,128,2560]{2,1,0:T(8,128)(2,1)S(1)}, bf16[2,128,2560]{2,1,0:T(8,128)(2,1)S(1)}, u32[]{:S(2)}, u32[]{:S(2)}) collective-permute-start(bf16[2,128,2560]{2,1,0:T(8,128)(2,1)S(1)} %pad_maximum_fusion.12), channel_id=1, source_target_pairs={{0,2},{1,3},{2,0},{3,1},{4,6},{5,7},{6,4},{7,5},{8,10},{9,11},{10,... | collective-permute-start | bytes 3932168 | tf_op jit(solution)/shard_map/ppermute | solution.py:985
  365.0 66.3 %collective-permute-start.31 = (bf16[640,1536]{1,0:T(8,128)(2,1)S(1)}, bf16[640,1536]{1,0:T(8,128)(2,1)}, u32[]{:S(2)}, u32[]{:S(2)}) collective-permute-start(bf16[640,1536]{1,0:T(8,128)(2,1)S(1)} %collective-permute-done.29.refs_2_.refs_8_), channel_id=1, source_target_pairs={{0,8},{8,16},{16,24},{24,0},{1,9},{9,17},{17,25},{25,1},{2,10},{10... | collective-permute-start | bytes 5898248 | tf_op jit(solution)/shard_map/ppermute | solution.py:1020
  427.8 28.2 %collective-permute-start.32 = (bf16[320,1152]{1,0:T(8,128)(2,1)}, bf16[320,1152]{1,0:T(8,128)(2,1)S(1)}, u32[]{:S(2)}, u32[]{:S(2)}) collective-permute-start(bf16[320,1152]{1,0:T(8,128)(2,1)} %get-tuple-element.257), channel_id=1, source_target_pairs={{0,4},{4,0},{1,5},{5,1},{2,6},{6,2},{3,7},{7,3},{8,12},{12,8},{9,1... | collective-permute-start | bytes 2211848 | tf_op jit(solution)/shard_map/ppermute | solution.py:981
  429.3 55.4 %collective-permute-start.33 = (bf16[320,1152]{1,0:T(8,128)(2,1)}, bf16[320,1152]{1,0:T(8,128)(2,1)}, u32[]{:S(2)}, u32[]{:S(2)}) collective-permute-start(bf16[320,1152]{1,0:T(8,128)(2,1)} %get-tuple-element.265), channel_id=1, source_target_pairs={{0,24},{8,0},{16,8},{24,16},{1,25},{9,1},{17,9},{25,17},{2,26},{10... | collective-permute-start | bytes 2211848 | tf_op jit(solution)/shard_map/ppermute | solution.py:1020
  429.3 63.9 %collective-permute-start.34 = (bf16[320,1152]{1,0:T(8,128)(2,1)}, bf16[320,1152]{1,0:T(8,128)(2,1)}, u32[]{:S(2)}, u32[]{:S(2)}) collective-permute-start(bf16[320,1152]{1,0:T(8,128)(2,1)} %get-tuple-element.266), channel_id=1, source_target_pairs={{0,16},{8,24},{16,0},{24,8},{1,17},{9,25},{17,1},{25,9},{2,18},{10... | collective-permute-start | bytes 2211848 | tf_op jit(solution)/shard_map/ppermute | solution.py:1020
  429.3 63.9 %collective-permute-start.35 = (bf16[320,1152]{1,0:T(8,128)(2,1)}, bf16[320,1152]{1,0:T(8,128)(2,1)}, u32[]{:S(2)}, u32[]{:S(2)}) collective-permute-start(bf16[320,1152]{1,0:T(8,128)(2,1)} %get-tuple-element.267), channel_id=1, source_target_pairs={{0,8},{8,16},{16,24},{24,0},{1,9},{9,17},{17,25},{25,1},{2,10},{10... | collective-permute-start | bytes 2211848 | tf_op jit(solution)/shard_map/ppermute | solution.py:1020
  493.2 67.8 %collective-permute-start.39 = (bf16[320,1152]{1,0:T(8,128)(2,1)}, bf16[320,1152]{1,0:T(8,128)(2,1)S(1)}, u32[]{:S(2)}, u32[]{:S(2)}) collective-permute-start(bf16[320,1152]{1,0:T(8,128)(2,1)} %collective-permute-done.33), channel_id=1, source_target_pairs={{0,4},{4,0},{1,5},{5,1},{2,6},{6,2},{3,7},{7,3},{8,12},{12,8},{9,1... | collective-permute-start | bytes 2211848 | tf_op jit(solution)/shard_map/ppermute | solution.py:981
  493.8 67.3 %collective-permute-start.40 = (bf16[320,1152]{1,0:T(8,128)(2,1)}, bf16[320,1152]{1,0:T(8,128)(2,1)}, u32[]{:S(2)}, u32[]{:S(2)}) collective-permute-start(bf16[320,1152]{1,0:T(8,128)(2,1)} %collective-permute-done.34), channel_id=1, source_target_pairs={{0,4},{4,0},{1,5},{5,1},{2,6},{6,2},{3,7},{7,3},{8,12},{12,8},{9,1... | collective-permute-start | bytes 2211848 | tf_op jit(solution)/shard_map/ppermute | solution.py:981
  495.2 65.8 %collective-permute-start.41 = (bf16[320,1152]{1,0:T(8,128)(2,1)}, bf16[320,1152]{1,0:T(8,128)(2,1)}, u32[]{:S(2)}, u32[]{:S(2)}) collective-permute-start(bf16[320,1152]{1,0:T(8,128)(2,1)} %get-tuple-element.280), channel_id=1, source_target_pairs={{0,24},{8,0},{16,8},{24,16},{1,25},{9,1},{17,9},{25,17},{2,26},{10... | collective-permute-start | bytes 2211848 | tf_op jit(solution)/shard_map/ppermute | solution.py:1020
  510.2 31.1 %collective-permute-start.37 = (bf16[2,128,2560]{2,1,0:T(8,128)(2,1)}, bf16[2,128,2560]{2,1,0:T(8,128)(2,1)S(1)}, u32[]{:S(2)}, u32[]{:S(2)}) collective-permute-start(bf16[2,128,2560]{2,1,0:T(8,128)(2,1)} %fusion.15), channel_id=1, source_target_pairs={{0,2},{1,3},{2,0},{3,1},{4,6},{5,7},{6,4},{7,5},{8,10},{9,11},{10,... | collective-permute-start | bytes 3932168 | tf_op jit(solution)/shard_map/ppermute | solution.py:985
  510.8 45.5 %collective-permute-start.38 = (bf16[2,128,2560]{2,1,0:T(8,128)(2,1)}, bf16[2,128,2560]{2,1,0:T(8,128)(2,1)}, u32[]{:S(2)}, u32[]{:S(2)}) collective-permute-start(bf16[2,128,2560]{2,1,0:T(8,128)(2,1)} %get-tuple-element.612), channel_id=1, source_target_pairs={{0,4},{4,0},{1,5},{5,1},{2,6},{6,2},{3,7},{7,3},{8,12},{12,8},{9,1... | collective-permute-start | bytes 3932168 | tf_op jit(solution)/shard_map/ppermute | solution.py:981
  541.3 41.7 %collective-permute-start.44 = (bf16[320,1536]{1,0:T(8,128)(2,1)}, bf16[320,1536]{1,0:T(8,128)(2,1)}, u32[]{:S(2)}, u32[]{:S(2)}) collective-permute-start(bf16[320,1536]{1,0:T(8,128)(2,1)} %get-tuple-element.287), channel_id=1, source_target_pairs={{0,24},{8,0},{16,8},{24,16},{1,25},{9,1},{17,9},{25,17},{2,26},{10... | collective-permute-start | bytes 2949128 | tf_op jit(solution)/shard_map/ppermute | solution.py:1020
  556.3 32.2 %collective-permute-start.45 = (bf16[320,1536]{1,0:T(8,128)(2,1)}, bf16[320,1536]{1,0:T(8,128)(2,1)}, u32[]{:S(2)}, u32[]{:S(2)}) collective-permute-start(bf16[320,1536]{1,0:T(8,128)(2,1)} %get-tuple-element.288), channel_id=1, source_target_pairs={{0,8},{8,16},{16,24},{24,0},{1,9},{9,17},{17,25},{25,1},{2,10},{10... | collective-permute-start | bytes 2949128 | tf_op jit(solution)/shard_map/ppermute | solution.py:1020
  562.1 26.4 %collective-permute-start.42 = (bf16[128,2560]{1,0:T(8,128)(2,1)}, bf16[128,2560]{1,0:T(8,128)(2,1)}, u32[]{:S(2)}, u32[]{:S(2)}) collective-permute-start(bf16[128,2560]{1,0:T(8,128)(2,1)} %slice_bitcast_fusion.15), channel_id=1, source_target_pairs={{0,4},{4,0},{1,5},{5,1},{2,6},{6,2},{3,7},{7,3},{8,12},{12,8},{9,1... | collective-permute-start | bytes 1966088 | tf_op jit(solution)/shard_map/ppermute | solution.py:981
  563.5 25.0 %collective-permute-start.43 = (bf16[128,2560]{1,0:T(8,128)(2,1)}, bf16[128,2560]{1,0:T(8,128)(2,1)}, u32[]{:S(2)}, u32[]{:S(2)}) collective-permute-start(bf16[128,2560]{1,0:T(8,128)(2,1)} %slice_bitcast_fusion.14), channel_id=1, source_target_pairs={{0,2},{1,3},{2,0},{3,1},{4,6},{5,7},{6,4},{7,5},{8,10},{9,11},{10,... | collective-permute-start | bytes 1966088 | tf_op jit(solution)/shard_map/ppermute | solution.py:985
  607.8 47.0 %collective-permute-start.47 = (bf16[2,128,2560]{2,1,0:T(8,128)(2,1)S(1)}, bf16[2,128,2560]{2,1,0:T(8,128)(2,1)S(1)}, u32[]{:S(2)}, u32[]{:S(2)}) collective-permute-start(bf16[2,128,2560]{2,1,0:T(8,128)(2,1)S(1)} %fusion.19), channel_id=1, source_target_pairs={{0,2},{1,3},{2,0},{3,1},{4,6},{5,7},{6,4},{7,5},{8,10},{9,11},{10,... | collective-permute-start | bytes 3932168 | tf_op jit(solution)/shard_map/ppermute | solution.py:985
  608.4 47.6 %collective-permute-start.48 = (bf16[2,128,2560]{2,1,0:T(8,128)(2,1)S(1)}, bf16[2,128,2560]{2,1,0:T(8,128)(2,1)S(1)}, u32[]{:S(2)}, u32[]{:S(2)}) collective-permute-start(bf16[2,128,2560]{2,1,0:T(8,128)(2,1)S(1)} %fusion.20), channel_id=1, source_target_pairs={{0,4},{4,0},{1,5},{5,1},{2,6},{6,2},{3,7},{7,3},{8,12},{12,8},{9,1... | collective-permute-start | bytes 3932168 | tf_op jit(solution)/shard_map/ppermute | solution.py:981
  609.0 55.5 %collective-permute-start.52 = (bf16[320,1152]{1,0:T(8,128)(2,1)S(1)}, bf16[320,1152]{1,0:T(8,128)(2,1)}, u32[]{:S(2)}, u32[]{:S(2)}) collective-permute-start(bf16[320,1152]{1,0:T(8,128)(2,1)S(1)} %copy-done.53), channel_id=1, source_target_pairs={{0,8},{8,16},{16,24},{24,0},{1,9},{9,17},{17,25},{25,1},{2,10},{10... | collective-permute-start | bytes 2211848 | tf_op jit(solution)/shard_map/ppermute | solution.py:1020
  609.0 77.8 %collective-permute-start.51 = (bf16[320,1536]{1,0:T(8,128)(2,1)S(1)}, bf16[320,1536]{1,0:T(8,128)(2,1)S(1)}, u32[]{:S(2)}, u32[]{:S(2)}) collective-permute-start(bf16[320,1536]{1,0:T(8,128)(2,1)S(1)} %copy-done.52), channel_id=1, source_target_pairs={{0,16},{8,24},{16,0},{24,8},{1,17},{9,25},{17,1},{25,9},{2,18},{10... | collective-permute-start | bytes 2949128 | tf_op jit(solution)/shard_map/ppermute | solution.py:1020
  659.8 27.6 %collective-permute-start.49 = (bf16[128,2560]{1,0:T(8,128)(2,1)S(1)}, bf16[128,2560]{1,0:T(8,128)(2,1)}, u32[]{:S(2)}, u32[]{:S(2)}) collective-permute-start(bf16[128,2560]{1,0:T(8,128)(2,1)S(1)} %slice_bitcast_fusion.10), channel_id=1, source_target_pairs={{0,4},{4,0},{1,5},{5,1},{2,6},{6,2},{3,7},{7,3},{8,12},{12,8},{9,1... | collective-permute-start | bytes 1966088 | tf_op jit(solution)/shard_map/ppermute | solution.py:981
  660.3 27.5 %collective-permute-start.50 = (bf16[128,2560]{1,0:T(8,128)(2,1)S(1)}, bf16[128,2560]{1,0:T(8,128)(2,1)}, u32[]{:S(2)}, u32[]{:S(2)}) collective-permute-start(bf16[128,2560]{1,0:T(8,128)(2,1)S(1)} %slice_bitcast_fusion.9), channel_id=1, source_target_pairs={{0,2},{1,3},{2,0},{3,1},{4,6},{5,7},{6,4},{7,5},{8,10},{9,11},{10,... | collective-permute-start | bytes 1966088 | tf_op jit(solution)/shard_map/ppermute | solution.py:985
  662.0 91.8 %collective-permute-start.53 = (bf16[320,1152]{1,0:T(8,128)(2,1)}, bf16[320,1152]{1,0:T(8,128)(2,1)S(1)}, u32[]{:S(2)}, u32[]{:S(2)}) collective-permute-start(bf16[320,1152]{1,0:T(8,128)(2,1)} %get-tuple-element.307), channel_id=1, source_target_pairs={{0,16},{8,24},{16,0},{24,8},{1,17},{9,25},{17,1},{25,9},{2,18},{10... | collective-permute-start | bytes 2211848 | tf_op jit(solution)/shard_map/ppermute | solution.py:1020
  687.8 66.0 %collective-permute-start.54 = (bf16[320,1152]{1,0:T(8,128)(2,1)}, bf16[320,1152]{1,0:T(8,128)(2,1)}, u32[]{:S(2)}, u32[]{:S(2)}) collective-permute-start(bf16[320,1152]{1,0:T(8,128)(2,1)} %collective-permute-done.35), channel_id=1, source_target_pairs={{0,4},{4,0},{1,5},{5,1},{2,6},{6,2},{3,7},{7,3},{8,12},{12,8},{9,1... | collective-permute-start | bytes 2211848 | tf_op jit(solution)/shard_map/ppermute | solution.py:981
  689.2 64.6 %collective-permute-start.55 = (bf16[320,1536]{1,0:T(8,128)(2,1)}, bf16[320,1536]{1,0:T(8,128)(2,1)}, u32[]{:S(2)}, u32[]{:S(2)}) collective-permute-start(bf16[320,1536]{1,0:T(8,128)(2,1)} %get-tuple-element.309), channel_id=1, source_target_pairs={{0,4},{4,0},{1,5},{5,1},{2,6},{6,2},{3,7},{7,3},{8,12},{12,8},{9,1... | collective-permute-start | bytes 2949128 | tf_op jit(solution)/shard_map/ppermute | solution.py:981
  689.8 64.0 %collective-permute-start.56 = (bf16[320,1536]{1,0:T(8,128)(2,1)}, bf16[320,1536]{1,0:T(8,128)(2,1)}, u32[]{:S(2)}, u32[]{:S(2)}) collective-permute-start(bf16[320,1536]{1,0:T(8,128)(2,1)} %collective-permute-done.44), channel_id=1, source_target_pairs={{0,4},{4,0},{1,5},{5,1},{2,6},{6,2},{3,7},{7,3},{8,12},{12,8},{9,1... | collective-permute-start | bytes 2949128 | tf_op jit(solution)/shard_map/ppermute | solution.py:981
  691.2 62.6 %collective-permute-start.57 = (bf16[320,1536]{1,0:T(8,128)(2,1)}, bf16[320,1536]{1,0:T(8,128)(2,1)}, u32[]{:S(2)}, u32[]{:S(2)}) collective-permute-start(bf16[320,1536]{1,0:T(8,128)(2,1)} %get-tuple-element.315), channel_id=1, source_target_pairs={{0,24},{8,0},{16,8},{24,16},{1,25},{9,1},{17,9},{25,17},{2,26},{10... | collective-permute-start | bytes 2949128 | tf_op jit(solution)/shard_map/ppermute | solution.py:1020
  761.3 66.5 %collective-permute-start.61 = (bf16[320,1536]{1,0:T(8,128)(2,1)}, bf16[320,1536]{1,0:T(8,128)(2,1)}, u32[]{:S(2)}, u32[]{:S(2)}) collective-permute-start(bf16[320,1536]{1,0:T(8,128)(2,1)} %get-tuple-element.326), channel_id=1, source_target_pairs={{0,16},{8,24},{16,0},{24,8},{1,17},{9,25},{17,1},{25,9},{2,18},{10... | collective-permute-start | bytes 2949128 | tf_op jit(solution)/shard_map/ppermute | solution.py:1020
  761.4 66.4 %collective-permute-start.62 = (bf16[320,1536]{1,0:T(8,128)(2,1)}, bf16[320,1536]{1,0:T(8,128)(2,1)}, u32[]{:S(2)}, u32[]{:S(2)}) collective-permute-start(bf16[320,1536]{1,0:T(8,128)(2,1)} %get-tuple-element.327), channel_id=1, source_target_pairs={{0,8},{8,16},{16,24},{24,0},{1,9},{9,17},{17,25},{25,1},{2,10},{10... | collective-permute-start | bytes 2949128 | tf_op jit(solution)/shard_map/ppermute | solution.py:1020
  763.1 64.6 %collective-permute-start.63 = (bf16[320,1536]{1,0:T(8,128)(2,1)}, bf16[320,1536]{1,0:T(8,128)(2,1)}, u32[]{:S(2)}, u32[]{:S(2)}) collective-permute-start(bf16[320,1536]{1,0:T(8,128)(2,1)} %copy-done.50), channel_id=1, source_target_pairs={{0,4},{4,0},{1,5},{5,1},{2,6},{6,2},{3,7},{7,3},{8,12},{12,8},{9,1... | collective-permute-start | bytes 2949128 | tf_op jit(solution)/shard_map/ppermute | solution.py:981
  771.6 40.9 %collective-permute-start.59 = (bf16[2,128,2560]{2,1,0:T(8,128)(2,1)}, bf16[2,128,2560]{2,1,0:T(8,128)(2,1)}, u32[]{:S(2)}, u32[]{:S(2)}) collective-permute-start(bf16[2,128,2560]{2,1,0:T(8,128)(2,1)} %fusion.23), channel_id=1, source_target_pairs={{0,2},{1,3},{2,0},{3,1},{4,6},{5,7},{6,4},{7,5},{8,10},{9,11},{10,... | collective-permute-start | bytes 3932168 | tf_op jit(solution)/shard_map/ppermute | solution.py:985
  773.0 42.1 %collective-permute-start.60 = (bf16[2,128,2560]{2,1,0:T(8,128)(2,1)}, bf16[2,128,2560]{2,1,0:T(8,128)(2,1)}, u32[]{:S(2)}, u32[]{:S(2)}) collective-permute-start(bf16[2,128,2560]{2,1,0:T(8,128)(2,1)} %get-tuple-element.608), channel_id=1, source_target_pairs={{0,4},{4,0},{1,5},{5,1},{2,6},{6,2},{3,7},{7,3},{8,12},{12,8},{9,1... | collective-permute-start | bytes 3932168 | tf_op jit(solution)/shard_map/ppermute | solution.py:981
  831.4 34.2 %collective-permute-start.66 = (bf16[320,1536]{1,0:T(8,128)(2,1)}, bf16[320,1536]{1,0:T(8,128)(2,1)S(1)}, u32[]{:S(2)}, u32[]{:S(2)}) collective-permute-start(bf16[320,1536]{1,0:T(8,128)(2,1)} %collective-permute-done.45), channel_id=1, source_target_pairs={{0,4},{4,0},{1,5},{5,1},{2,6},{6,2},{3,7},{7,3},{8,12},{12,8},{9,1... | collective-permute-start | bytes 2949128 | tf_op jit(solution)/shard_map/ppermute | solution.py:981
  832.9 32.8 %collective-permute-start.67 = (bf16[320,896]{1,0:T(8,128)(2,1)S(1)}, bf16[320,896]{1,0:T(8,128)(2,1)S(1)}, u32[]{:S(2)}, u32[]{:S(2)}) collective-permute-start(bf16[320,896]{1,0:T(8,128)(2,1)S(1)} %copy-done.58), channel_id=1, source_target_pairs={{0,24},{8,0},{16,8},{24,16},{1,25},{9,1},{17,9},{25,17},{2,26},{10... | collective-permute-start | bytes 1720328 | tf_op jit(solution)/shard_map/ppermute | solution.py:1020
  832.9 49.2 %collective-permute-start.68 = (bf16[320,896]{1,0:T(8,128)(2,1)S(1)}, bf16[320,896]{1,0:T(8,128)(2,1)S(1)}, u32[]{:S(2)}, u32[]{:S(2)}) collective-permute-start(bf16[320,896]{1,0:T(8,128)(2,1)S(1)} %copy-done.57), channel_id=1, source_target_pairs={{0,16},{8,24},{16,0},{24,8},{1,17},{9,25},{17,1},{25,9},{2,18},{10... | collective-permute-start | bytes 1720328 | tf_op jit(solution)/shard_map/ppermute | solution.py:1020
  845.5 36.7 %collective-permute-start.69 = (bf16[320,896]{1,0:T(8,128)(2,1)S(1)}, bf16[320,896]{1,0:T(8,128)(2,1)S(1)}, u32[]{:S(2)}, u32[]{:S(2)}) collective-permute-start(bf16[320,896]{1,0:T(8,128)(2,1)S(1)} %copy-done.56), channel_id=1, source_target_pairs={{0,8},{8,16},{16,24},{24,0},{1,9},{9,17},{17,25},{25,1},{2,10},{10... | collective-permute-start | bytes 1720328 | tf_op jit(solution)/shard_map/ppermute | solution.py:1020
  882.2 78.7 %collective-permute-start.73 = (bf16[320,896]{1,0:T(8,128)(2,1)}, bf16[320,896]{1,0:T(8,128)(2,1)S(1)}, u32[]{:S(2)}, u32[]{:S(2)}) collective-permute-start(bf16[320,896]{1,0:T(8,128)(2,1)} %get-tuple-element.341), channel_id=1, source_target_pairs={{0,4},{4,0},{1,5},{5,1},{2,6},{6,2},{3,7},{7,3},{8,12},{12,8},{9,1... | collective-permute-start | bytes 1720328 | tf_op jit(solution)/shard_map/ppermute | solution.py:981
  883.7 72.9 %collective-permute-start.70 = (bf16[320,896]{1,0:T(8,128)(2,1)}, bf16[320,896]{1,0:T(8,128)(2,1)}, u32[]{:S(2)}, u32[]{:S(2)}) collective-permute-start(bf16[320,896]{1,0:T(8,128)(2,1)} %get-tuple-element.346), channel_id=1, source_target_pairs={{0,24},{8,0},{16,8},{24,16},{1,25},{9,1},{17,9},{25,17},{2,26},{10... | collective-permute-start | bytes 1720328 | tf_op jit(solution)/shard_map/ppermute | solution.py:1020
  883.7 72.9 %collective-permute-start.71 = (bf16[320,896]{1,0:T(8,128)(2,1)}, bf16[320,896]{1,0:T(8,128)(2,1)}, u32[]{:S(2)}, u32[]{:S(2)}) collective-permute-start(bf16[320,896]{1,0:T(8,128)(2,1)} %get-tuple-element.347), channel_id=1, source_target_pairs={{0,16},{8,24},{16,0},{24,8},{1,17},{9,25},{17,1},{25,9},{2,18},{10... | collective-permute-start | bytes 1720328 | tf_op jit(solution)/shard_map/ppermute | solution.py:1020
  885.6 71.0 %collective-permute-start.72 = (bf16[320,896]{1,0:T(8,128)(2,1)}, bf16[320,896]{1,0:T(8,128)(2,1)}, u32[]{:S(2)}, u32[]{:S(2)}) collective-permute-start(bf16[320,896]{1,0:T(8,128)(2,1)} %get-tuple-element.348), channel_id=1, source_target_pairs={{0,8},{8,16},{16,24},{24,0},{1,9},{9,17},{17,25},{25,1},{2,10},{10... | collective-permute-start | bytes 1720328 | tf_op jit(solution)/shard_map/ppermute | solution.py:1020
  889.1 71.9 %collective-permute-start.74 = (bf16[3,320,896]{2,1,0:T(8,128)(2,1)}, bf16[3,320,896]{2,1,0:T(8,128)(2,1)S(1)}, u32[]{:S(2)}, u32[]{:S(2)}) collective-permute-start(bf16[3,320,896]{2,1,0:T(8,128)(2,1)} %pad_maximum_fusion.3), channel_id=1, source_target_pairs={{0,4},{4,0},{1,5},{5,1},{2,6},{6,2},{3,7},{7,3},{8,12},{12,8},{9,1... | collective-permute-start | bytes 5160968 | tf_op jit(solution)/shard_map/ppermute | solution.py:981
  (74 other events, 921.0 us)
Sparse Core Ops, SparseCore 0:
  9.9 80.4 all-gather.2
  595.4 91.1 all-gather.4

commit v3 on v2

--- a/solution.py
+++ b/solution.py
@@ -97,7 +97,7 @@
     project, output = projection_selector(), output_selector()
     padded = np.zeros((OUTPUT_PACK, HEADS * LANES), np.float32)
     padded[: output.shape[0]] = output
-    return ((0, project[:, : HEADS * LANES]), (0, project[:, HEADS * LANES :]), (0, None), (1, padded))
+    return ((0, project), (0, None), (1, padded))
 
 
 def gains_selector():
@@ -411,9 +411,8 @@
     )
 
 
-def projection_grad_kernel(place_ref, grad_query, grad_pair, tokens, wide, kept, sent, gain_sums):
-    grad = dot(grad_query[...], wide[:, : HEADS * LANES], NT)
-    grad = grad + dot(grad_pair[...], wide[:, HEADS * LANES :], NT)
+def projection_grad_kernel(place_ref, grad_heads, tokens, wide, kept, sent, gain_sums):
+    grad = dot(grad_heads[...], wide[...], NT)
     write_piece(seen_from(place_ref, pl.program_id(0)), kept, sent, grad.astype(low_type))
     value = tokens[...].astype(f32)
     inverse = lax.rsqrt(jnp.mean(value * value, axis=-1, keepdims=True) + epsilon)
@@ -429,7 +428,7 @@
         gain_sums[...] += sums
 
 
-def project_grad(place, grad_query, grad_pair, tokens, wide):
+def project_grad(place, grad_heads, tokens, wide):
     total, width = tokens.shape
     tile = lambda columns: pl.BlockSpec((TILE, columns), lambda i, *_: (i, 0))
     return pl.pallas_call(
@@ -438,8 +437,7 @@
             num_scalar_prefetch=1,
             grid=(total // TILE,),
             in_specs=[
-                tile(HEADS * LANES),
-                tile(2 * LANES),
+                tile(WIDE),
                 tile(width),
                 resident((width, WIDE)),
             ],
@@ -449,7 +447,7 @@
         compiler_params=params(),
         cost_estimate=SHORT,
         name="projection_grad",
-    )(place, grad_query, grad_pair, tokens, wide)
+    )(place, grad_heads, tokens, wide)
 
 
 def pack_kernel(place_ref, gating, down, *outs):
@@ -1050,6 +1048,21 @@
         two = jnp.stack([value[cut:], by_y])
         return one, two, swap(one), across(two, 2)
 
+    def gather_pieces(parts):
+        one, two, one_y, two_x = parts
+        pieces = {(0, 0, 0): one[0], (0, 1, 0): one[1], (0, 0, 1): two[0], (1, 0, 1): two[1]}
+        pieces |= {(1, 0, 0): one_y[0], (1, 1, 0): one_y[1], (0, 1, 1): two_x[0], (1, 1, 1): two_x[1]}
+        early = across(jnp.concatenate([one, two], axis=0), 1)
+        late_one, late_two = across(one_y, 1), across(two_x, 1)
+        far = {(0, 0, 0): early[0], (0, 1, 0): early[1], (0, 0, 1): early[2], (1, 0, 1): early[3]}
+        far |= {(1, 0, 0): late_one[0], (1, 1, 0): late_one[1], (0, 1, 1): late_two[0], (1, 1, 1): late_two[1]}
+        found = []
+        for by_y in range(2):
+            for by_x in range(2):
+                for group in (pieces, far):
+                    found += [group[by_y, by_x, 0], group[by_y, by_x, 1]]
+        return jnp.concatenate(found, axis=0)
+
     def gather_last(parts):
         one, two, one_y, two_x = parts
         ones = [one[0], one[1], one_y[0], one_y[1]]
@@ -1107,14 +1120,15 @@
     attention_shard = halves(*pick(packed))
     attention_blocks = gather_hops(attention_shard)
     output_kept, output_sent = pick(output_parts)
-    output_shard = halves(output_kept, after(output_sent, attention_shard))
+    output_came = swap(after(output_sent, attention_shard))
+    output_shard = halves(output_kept, output_sent, output_came)
     output_blocks = gather_hops(after(output_shard, attention_blocks[1:2]))
 
     feed_parts = pack_feed(after(place, attention_shard), gating_weight, down_weight)
     tokens_all = after(tokens_all, feed_parts)
     kept, sent = feed_parts[: len(CHUNKS)], feed_parts[len(CHUNKS) :]
     feed_shards, came = [], []
-    last = attention_shard
+    last = output_came
     for a, b in zip(kept, sent):
         came.append(swap(after(b, last)))
         last = halves(a, b, came[-1])
@@ -1153,7 +1167,7 @@
     two = relay(two)
     normed_parts = after(gather_second(gather_first(normed_two)), two)
     two = relay(two)
-    normed_two_all = gather_last(normed_parts)
+    normed_two_all = gather_pieces(normed_parts)
     hid, grad_pair = feed(place, normed_two_all, cotangent_all, one)
     theirs, mine = sides(weight_grad(place, blocks, [(normed_two_all, grad_pair), (cotangent_all, hid)]))
     theirs_one = deliver(theirs)
@@ -1188,7 +1202,8 @@
     grad_query, grad_pair = attend_grad(
         place, grad_hidden_all, heads, totals, starts, cosine, sine, output_blocks, sequence
     )
-    *partial, gain_sums = project_grad(place, grad_query, grad_pair, tokens_all, wide)
+    grad_heads = jnp.concatenate([grad_query, grad_pair], axis=1)
+    *partial, gain_sums = project_grad(place, grad_heads, tokens_all, wide)
     grad_gains = jnp.stack([jnp.sum(gain_sums, axis=0), grad_gain_two], axis=0)
     grad_gains = jnp.concatenate([grad_gains, jnp.zeros((6, width), f32)], axis=0).astype(low_type)
     partial = after(partial, mine_one, others_one, others_two, mine_two[1:2])
@@ -1199,8 +1214,7 @@
             place,
             blocks,
             [
-                (normed_one, after(grad_query, *parts)),
-                (normed_one, grad_pair),
+                (normed_one, after(grad_heads, *parts)),
                 (grad_gains, jnp.asarray(gains_selector(), low_type)),
                 (grad_hidden_all, mixed),
             ],

time: 1010 us -> 993 us (0.983)
  waiting for transfers between devices: 364 us -> 330 us
  local copies, waits for them, and re-layouts: 47.2 us -> 64.4 us
    ppermute x27, waiting for transfers between devices: 119 us -> 95.5 us  [swap(): return lax.ppermute(value, 'pair', [(0, 1), (1, 0)])]
    unnamed x152, local copies, waits for them, and re-layouts: 27.1 us -> 42.6 us
    ppermute x30, waiting for transfers between devices: 153 us -> 137 us  [hop(): lax.ppermute(value, 'ring', [(i, (i + step) % ring) for i in range(ring)])]
    ppermute x20 -> x22, waiting for transfers between devices: 85.2 us -> 85.3 us  [across(): return lax.ppermute(value, 'tensor', [(i, i ^ bit) for i in range(count)])]
  transfers between devices with their start and end apart: 79 -> 81, of which waited for: 27 -> 30; matrix products, arithmetic and copies ran while one was open for 10% -> 12% of each run, Pallas kernels for 38% -> 38%
where the time goes in v3:
time: 993 us; the launch traced here: 987 us
  Pallas kernels  376 us (38%)
  waiting for transfers between devices  330 us (33%)
  starting transfers between devices  119 us (12%)
  other arithmetic  82 us (8%)
  local copies, waits for them, and re-layouts  64.4 us (6%)
  between operations  15.6 us (2%)
    ppermute x30, waiting for transfers between devices, hop(): lax.ppermute(value, 'ring', [(i, (i + step) % ring) for i in range(ring)])  137 us
    ppermute x27, waiting for transfers between devices, swap(): return lax.ppermute(value, 'pair', [(0, 1), (1, 0)])  95.5 us
    ppermute x22, waiting for transfers between devices, across(): return lax.ppermute(value, 'tensor', [(i, i ^ bit) for i in range(count)])  85.3 us
    pallas_call x3, Pallas kernels, weight_grad(): pl.pallas_call(functools.partial(weight_grad_kernel, spans, selected, spl...  84 us
    ppermute x30, starting transfers between devices, hop(): lax.ppermute(value, 'ring', [(i, (i + step) % ring) for i in range(ring)])  74.3 us
    pallas_call x1, Pallas kernels, feed_update(): pl.pallas_call(feed_update_kernel, grid_spec=pltpu.PrefetchScalarGridSpec...  62.4 us
    pallas_call x2, Pallas kernels, spread(): pl.pallas_call(functools.partial(spread_kernel, tuple((len(blocks) for bl...  47.6 us
    pallas_call x2, Pallas kernels, feed(): pl.pallas_call(functools.partial(feed_kernel, len(blocks), tiles), grid_s...  45.5 us
  transfers between devices with their start and end apart: 81, of which 30 were waited for; matrix products, arithmetic and copies ran while one was open for 12% of the time, Pallas kernels for 38%

profile of v3, /device:TPU:0, one launch (start us, length us, event | category | flops | bytes accessed | tf_op | source)
XLA Modules:
  0.0 986.9 jit_solution(6460180464765073122)
XLA Ops:
  10.9 3.0 collective-permute-start
  15.5 6.2 collective-permute-done.4
  24.6 3.7 fusion.42
  28.4 2.1 collective-permute-start.1
  30.5 9.1 pack_feed.1
  40.1 2.5 pad_maximum_fusion.5
  42.6 2.6 collective-permute-start.2
  47.5 23.9 %collective-permute-start.9 = (bf16[640,320]{1,0:T(8,128)(2,1)}, bf16[640,320]{1,0:T(8,128)(2,1)}, u32[]{:S(2)}, u32[]{:S(2)}) collective-permute-start(bf16[640,320]{1,0:T(8,128)(2,1)} %pad_maximum_fusion.17.refs_0_), channel_id=1, source_target_pairs={{0,8},{8,16},{16,24},{24,0},{1,9},{9,17},{17,25},{25,1},{2,10},{10... | collective-permute-start | bytes 1228808 | tf_op jit(solution)/shard_map/ppermute | solution.py:1018
  71.5 2.4 collective-permute-start.10
  73.9 2.9 collective-permute-start.11
  77.9 11.4 %all-gather.3.cloned.1.call-done.tokens = bf16[2048,2560]{1,0:T(8,128)(2,1)} async-done(((bf16[256,2560]{1,0:T(8,128)(2,1)}), bf16[2048,2560]{1,0:T(8,128)(2,1)}) %all-gather.3.cloned.1.call-update) | async-done | bytes 10485776 | tf_op jit(solution)/shard_map/all_gather | solution.py:1102
  92.6 20.2 %projection.1 = (bf16[2048,2560]{1,0:T(8,128)(2,1)}, bf16[2048,768]{1,0:T(8,128)(2,1)}, f32[8,2560]{1,0:T(8,128)}, bf16[2560,768]{1,0:T(8,128)(2,1)}) custom-call(s32[4]{0:T(128)} %pad_add_fusion.1.place_ref, bf16[2048,2560]{1,0:T(8,128)(2,1)} %all-gather.3.cloned.1.call-done.tokens, bf16[640,512]{1,0:T(8,128)(2,1)} %copy-done.41, ...), custom_call_target="tpu_custom_call" | custom-call | flops 8053063680 | bytes 32768000 | tf_op jit(solution)/shard_map/projection/pallas_call | solution.py:173
  112.8 20.9 %collective-permute-start.14 = (bf16[640,1152]{1,0:T(8,128)(2,1)S(1)}, bf16[640,1152]{1,0:T(8,128)(2,1)S(1)}, u32[]{:S(2)}, u32[]{:S(2)}) collective-permute-start(bf16[640,1152]{1,0:T(8,128)(2,1)S(1)} %pad_maximum_fusion.9.refs_0_.refs_2_), channel_id=1, source_target_pairs={{0,8},{8,16},{16,24},{24,0},{1,9},{9,17},{17,25},{25,1},{2,10},{10... | collective-permute-start | bytes 4423688 | tf_op jit(solution)/shard_map/ppermute | solution.py:1018
  139.0 31.4 %attention.1 = (bf16[2048,512]{1,0:T(8,128)(2,1)}, f32[8,2048]{1,0:T(8,128)}, bf16[1024,2560]{1,0:T(8,128)(2,1)}, bf16[1024,2560]{1,0:T(8,128)(2,1)}) custom-call(s32[4]{0:T(128)} %pad_add_fusion.1.place_ref, bf16[2048,768]{1,0:T(8,128)(2,1)} %get-tuple-element.227.query.key.value, bf16[2048,768]{1,0:T(8,128)(2,1)} %get-tuple-element.227.query.key.value, ...), custom_call_target="tpu_custom_call" | custom-call | flops 20000000000 | bytes 20971520 | tf_op jit(solution)/shard_map/attention/pallas_call | solution.py:267
  171.2 8.2 collective-permute-done.15
  183.7 23.4 %collective-permute-done.16.refs_2_.refs_4_ = bf16[640,1152]{1,0:T(8,128)(2,1)S(1)} collective-permute-done((bf16[640,1152]{1,0:T(8,128)(2,1)S(1)}, bf16[640,1152]{1,0:T(8,128)(2,1)S(1)}, u32[]{:S(2)}, u32[]{:S(2)}) %collective-permute-start.16) | collective-permute-done | bytes 1474592 | tf_op jit(solution)/shard_map/ppermute | solution.py:1018
  217.4 21.0 %collective-permute-done.23 = bf16[320,1536]{1,0:T(8,128)(2,1)S(1)} collective-permute-done((bf16[320,1536]{1,0:T(8,128)(2,1)S(1)}, bf16[320,1536]{1,0:T(8,128)(2,1)S(1)}, u32[]{:S(2)}, u32[]{:S(2)}) %collective-permute-start.23) | collective-permute-done | bytes 983072 | tf_op jit(solution)/shard_map/ppermute | solution.py:979
  238.7 12.1 %collective-permute-done.19.refs_3_.refs_5_ = bf16[640,1152]{1,0:T(8,128)(2,1)S(1)} collective-permute-done((bf16[640,1152]{1,0:T(8,128)(2,1)S(1)}, bf16[640,1152]{1,0:T(8,128)(2,1)S(1)}, u32[]{:S(2)}, u32[]{:S(2)}) %collective-permute-start.19) | collective-permute-done | bytes 1474592 | tf_op jit(solution)/shard_map/ppermute | solution.py:1018
  251.0 15.1 %collective-permute-done.18 = bf16[2,128,2560]{2,1,0:T(8,128)(2,1)S(1)} collective-permute-done((bf16[2,128,2560]{2,1,0:T(8,128)(2,1)S(1)}, bf16[2,128,2560]{2,1,0:T(8,128)(2,1)S(1)}, u32[]{:S(2)}, u32[]{:S(2)}) %collective-permute-start.18) | collective-permute-done | bytes 1310752 | tf_op jit(solution)/shard_map/ppermute | solution.py:979
  268.8 2.1 bitcast_dynamic-update-slice_fusion.16
  285.3 11.5 %collective-permute-done.24.refs_1_.refs_7_ = bf16[640,1536]{1,0:T(8,128)(2,1)S(1)} collective-permute-done((bf16[640,1536]{1,0:T(8,128)(2,1)S(1)}, bf16[640,1536]{1,0:T(8,128)(2,1)S(1)}, u32[]{:S(2)}, u32[]{:S(2)}) %collective-permute-start.24) | collective-permute-done | bytes 1966112 | tf_op jit(solution)/shard_map/ppermute | solution.py:1018
  302.5 12.3 %collective-permute-done.25 = bf16[128,2560]{1,0:T(8,128)(2,1)S(1)} collective-permute-done((bf16[128,2560]{1,0:T(8,128)(2,1)S(1)}, bf16[128,2560]{1,0:T(8,128)(2,1)S(1)}, u32[]{:S(2)}, u32[]{:S(2)}) %collective-permute-start.25) | collective-permute-done | bytes 655392 | tf_op jit(solution)/shard_map/ppermute | solution.py:983
  318.0 28.9 %collective-permute-done.29.refs_2_.refs_8_ = bf16[640,1536]{1,0:T(8,128)(2,1)S(1)} collective-permute-done((bf16[640,1536]{1,0:T(8,128)(2,1)S(1)}, bf16[640,1536]{1,0:T(8,128)(2,1)S(1)}, u32[]{:S(2)}, u32[]{:S(2)}) %collective-permute-start.29) | collective-permute-done | bytes 1966112 | tf_op jit(solution)/shard_map/ppermute | solution.py:1018
  364.5 20.8 %feed.2 = (bf16[2048,384]{1,0:T(8,128)(2,1)}, bf16[2048,768]{1,0:T(8,128)(2,1)}) custom-call(s32[4]{0:T(128)} %pad_add_fusion.1.place_ref, bf16[2048,2560]{1,0:T(8,128)(2,1)} %fusion.34.normed.refs_0_, bf16[2048,2560]{1,0:T(8,128)(2,1)} %slice_dynamic-update-slice_fusion.grad_out.refs_1_, bf16[640,1152]{1,0:T(8,128)(2,1)} %copy-done.3, ...), custom_call_target="tpu_custom_call" | custom-call | flops 12079595520 | bytes 26869760 | tf_op jit(solution)/shard_map/feed/pallas_call | solution.py:526
  385.3 23.6 %weight_grad.3 = (bf16[320,1152]{1,0:T(8,128)(2,1)}, bf16[320,1152]{1,0:T(8,128)(2,1)}, bf16[320,1152]{1,0:T(8,128)(2,1)}, bf16[320,1152]{1,0:T(8,128)(2,1)}, bf...) custom-call(s32[4]{0:T(128)} %pad_add_fusion.1.place_ref, ...), custom_call_target="tpu_custom_call" | custom-call | flops 12079595520 | bytes 25690112 | tf_op jit(solution)/shard_map/weight_grad/pallas_call | solution.py:650
  409.6 2.1 collective-permute-start.35
  412.3 24.7 %feed.3 = (bf16[2048,512]{1,0:T(8,128)(2,1)}, bf16[2048,1024]{1,0:T(8,128)(2,1)}) custom-call(s32[4]{0:T(128)} %pad_add_fusion.1.place_ref, bf16[2048,2560]{1,0:T(8,128)(2,1)} %fusion.34.normed.refs_0_, bf16[2048,2560]{1,0:T(8,128)(2,1)} %slice_dynamic-update-slice_fusion.grad_out.refs_1_, bf16[640,1536]{1,0:T(8,128)(2,1)} %copy-done.2, ...), custom_call_target="tpu_custom_call" | custom-call | flops 16106127360 | bytes 28835840 | tf_op jit(solution)/shard_map/feed/pallas_call | solution.py:526
  437.0 28.7 %spread.2 = (bf16[1024,2560]{1,0:T(8,128)(2,1)}, bf16[1024,2560]{1,0:T(8,128)(2,1)}) custom-call(s32[4]{0:T(128)} %pad_add_fusion.1.place_ref, bf16[2048,768]{1,0:T(8,128)(2,1)} %get-tuple-element.261.refs_2_.refs_0_, bf16[2048,1024]{1,0:T(8,128)(2,1)} %get-tuple-element.270.refs_1_.refs_2_, bf16[640,1152]{1,0:T(8,128)(2,1)} %copy-done.3, ...), custom_call_target="tpu_custom_call" | custom-call | flops 1 | bytes 1 | tf_op jit(solution)/shard_map/spread/pallas_call | solution.py:569
  465.7 7.8 collective-permute-done.36
  475.6 6.8 collective-permute-done.38
  482.4 2.7 fusion.15
  485.1 3.8 fusion.17
  492.7 27.5 %weight_grad.4 = (bf16[320,1536]{1,0:T(8,128)(2,1)}, bf16[320,1536]{1,0:T(8,128)(2,1)}, bf16[320,1536]{1,0:T(8,128)(2,1)}, bf16[320,1536]{1,0:T(8,128)(2,1)}, bf...) custom-call(s32[4]{0:T(128)} %pad_add_fusion.1.place_ref, ...), custom_call_target="tpu_custom_call" | custom-call | flops 16106127360 | bytes 27262976 | tf_op jit(solution)/shard_map/weight_grad/pallas_call | solution.py:650
  521.6 15.0 %collective-permute-done.40 = bf16[2,128,2560]{2,1,0:T(8,128)(2,1)} collective-permute-done((bf16[2,128,2560]{2,1,0:T(8,128)(2,1)}, bf16[2,128,2560]{2,1,0:T(8,128)(2,1)}, u32[]{:S(2)}, u32[]{:S(2)}) %collective-permute-start.40) | collective-permute-done | bytes 1310752 | tf_op jit(solution)/shard_map/ppermute | solution.py:979
  536.6 2.2 collective-permute-start.47
  545.9 18.9 %spread.3 = (bf16[1024,2560]{1,0:T(8,128)(2,1)}, bf16[1024,2560]{1,0:T(8,128)(2,1)}) custom-call(s32[4]{0:T(128)} %pad_add_fusion.1.place_ref, bf16[2048,384]{1,0:T(8,128)(2,1)} %get-tuple-element.283.refs_3_.refs_0_, bf16[2048,512]{1,0:T(8,128)(2,1)} %get-tuple-element.284.refs_3_.refs_1_, bf16[640,1152]{1,0:T(8,128)(2,1)} %copy-done.3, ...), custom_call_target="tpu_custom_call" | custom-call | flops 1 | bytes 1 | tf_op jit(solution)/shard_map/spread/pallas_call | solution.py:569
  564.9 4.7 collective-permute-done.47
  573.5 2.9 fusion.53
  576.4 8.9 collective-permute-done.48
  591.1 45.0 %collective-permute-done.49 = bf16[2,128,2560]{2,1,0:T(8,128)(2,1)S(1)} collective-permute-done((bf16[2,128,2560]{2,1,0:T(8,128)(2,1)S(1)}, bf16[2,128,2560]{2,1,0:T(8,128)(2,1)S(1)}, u32[]{:S(2)}, u32[]{:S(2)}) %collective-permute-start.49) | collective-permute-done | bytes 1310752 | tf_op jit(solution)/shard_map/ppermute | solution.py:983
  637.3 2.7 fusion.7
  643.3 2.4 collective-permute-start.55
  645.8 22.9 %collective-permute-done.53 = bf16[320,1536]{1,0:T(8,128)(2,1)S(1)} collective-permute-done((bf16[320,1536]{1,0:T(8,128)(2,1)S(1)}, bf16[320,1536]{1,0:T(8,128)(2,1)S(1)}, u32[]{:S(2)}, u32[]{:S(2)}) %collective-permute-start.53) | collective-permute-done | bytes 983072 | tf_op jit(solution)/shard_map/ppermute | solution.py:1018
  672.3 3.2 collective-permute-start.59
  675.6 36.7 %attention_grad.1 = (bf16[2048,512]{1,0:T(8,128)(2,1)}, bf16[2048,256]{1,0:T(8,128)(2,1)}) custom-call(s32[4]{0:T(128)} %pad_add_fusion.1.place_ref, bf16[2048,2560]{1,0:T(8,128)(2,1)} %all-gather.5.cloned.1.call-done.grad_hidden.refs_2_, bf16[2048,768]{1,0:T(8,128)(2,1)} %get-tuple-element.227.query.key.value, ...), custom_call_target="tpu_custom_call" | custom-call | flops 30000001024 | bytes 20971520 | tf_op jit(solution)/shard_map/attention_grad/pallas_call | solution.py:364
  712.3 3.1 constant_dynamic-update-slice_fusion.1
  716.5 22.8 %projection_grad.1 = (bf16[1024,2560]{1,0:T(8,128)(2,1)}, bf16[1024,2560]{1,0:T(8,128)(2,1)}, f32[8,2560]{1,0:T(8,128)}) custom-call(s32[4]{0:T(128)} %pad_add_fusion.1.place_ref, bf16[2048,768]{1,0:T(8,128)(2,1)} %constant_dynamic-update-slice_fusion.grad_heads.refs_3_, bf16[2048,2560]{1,0:T(8,128)(2,1)} %all-gather.3.cloned.1.call-done.tokens, ...), custom_call_target="tpu_custom_call" | custom-call | flops 1 | bytes 1 | tf_op jit(solution)/shard_map/projection_grad/pallas_call | solution.py:434
  741.9 2.6 convert_add_fusion.5
  744.5 2.3 convert_add_fusion.6
  749.9 3.1 fusion.23
  753.0 4.2 fusion.25
  759.2 2.0 fusion.22
  761.2 33.0 %weight_grad.5 = (bf16[320,896]{1,0:T(8,128)(2,1)}, bf16[320,896]{1,0:T(8,128)(2,1)}, bf16[320,896]{1,0:T(8,128)(2,1)}, bf16[320,896]{1,0:T(8,128)(2,1)}, bf16[3...) custom-call(s32[4]{0:T(128)} %pad_add_fusion.1.place_ref, ...), custom_call_target="tpu_custom_call" | custom-call | flops 9395240960 | bytes 35127296 | tf_op jit(solution)/shard_map/weight_grad/pallas_call | solution.py:650
  794.2 6.5 collective-permute-done.62
  804.1 8.5 collective-permute-done.63.refs_6_
  819.0 11.4 %collective-permute-done.66 = bf16[128,2560]{1,0:T(8,128)(2,1)S(1)} collective-permute-done((bf16[128,2560]{1,0:T(8,128)(2,1)S(1)}, bf16[128,2560]{1,0:T(8,128)(2,1)S(1)}, u32[]{:S(2)}, u32[]{:S(2)}) %collective-permute-start.66) | collective-permute-done | bytes 655392 | tf_op jit(solution)/shard_map/ppermute | solution.py:979
  833.4 17.1 %collective-permute-done.68.refs_15_ = bf16[320,1536]{1,0:T(8,128)(2,1)S(1)} collective-permute-done((bf16[320,1536]{1,0:T(8,128)(2,1)}, bf16[320,1536]{1,0:T(8,128)(2,1)S(1)}, u32[]{:S(2)}, u32[]{:S(2)}) %collective-permute-start.68) | collective-permute-done | bytes 983072 | tf_op jit(solution)/shard_map/ppermute | solution.py:979
  850.5 17.2 %collective-permute-done.70 = bf16[320,896]{1,0:T(8,128)(2,1)S(1)} collective-permute-done((bf16[320,896]{1,0:T(8,128)(2,1)S(1)}, bf16[320,896]{1,0:T(8,128)(2,1)S(1)}, u32[]{:S(2)}, u32[]{:S(2)}) %collective-permute-start.70) | collective-permute-done | bytes 573472 | tf_op jit(solution)/shard_map/ppermute | solution.py:1018
  869.2 2.0 collective-permute-start.73
  871.2 2.0 collective-permute-start.74
  875.4 62.4 %feed_update.1 = (f32[4,320,2,1792]{3,2,1,0:T(2,128)}, f32[4,320,2,1792]{3,2,1,0:T(2,128)}, f32[320,2,1792]{2,1,0:T(2,128)}, f32[320,2,1792]{2,1,0:T(2,128)}, f3...) custom-call(s32[4]{0:T(128)} %pad_add_fusion.1.place_ref, ...), custom_call_target="tpu_custom_call" | custom-call | bytes 154828800 | tf_op jit(solution)/shard_map/feed_update/pallas_call | solution.py:798
  937.8 3.6 fusion.4
  951.0 5.4 multiply_reduce_fusion.3
  958.9 16.0 %attention_update.1 = (f32[4,320,640]{2,1,0:T(8,128)}, f32[4,320,640]{2,1,0:T(8,128)}, f32[320,640]{1,0:T(8,128)}, f32[320,640]{1,0:T(8,128)}, f32[320,640]{1,0:...) custom-call(s32[4]{0:T(128)} %pad_add_fusion.1.place_ref, ...), custom_call_target="tpu_custom_call" | custom-call | bytes 36864000 | tf_op jit(solution)/shard_map/attention_update/pallas_call | solution.py:873
  (397 shorter events, 154.9 us)
Async XLA Ops:
  7.2 82.1 %all-gather.3.cloned.1.call-start = ((), (), s32[]{:S(2)}) async-start(), calls=%async_computation | async-start | bytes 11796480 | tf_op jit(solution)/shard_map/all_gather | solution.py:1102
  8.0 661.6 %all-gather.5.cloned.1.call-start = ((), (), s32[]{:S(2)}) async-start(), calls=%async_computation.1 | async-start | bytes 11796480 | tf_op jit(solution)/shard_map/all_gather | solution.py:1194
  28.4 19.2 %collective-permute-start.1 = (bf16[640,512]{1,0:T(8,128)(2,1)S(1)}, bf16[640,512]{1,0:T(8,128)(2,1)S(1)}, u32[]{:S(2)}, u32[]{:S(2)}) collective-permute-start(bf16[640,512]{1,0:T(8,128)(2,1)S(1)} %pad_maximum_fusion.14.refs_0_), channel_id=1, source_target_pairs={{0,8},{8,16},{16,24},{24,0},{1,9},{9,17},{17,25},{25,1},{2,10},{10... | collective-permute-start | bytes 1966088 | tf_op jit(solution)/shard_map/ppermute | solution.py:1018
  39.6 34.3 %collective-permute-start.6 = (bf16[320,1152]{1,0:T(8,128)(2,1)}, bf16[320,1152]{1,0:T(8,128)(2,1)S(1)}, u32[]{:S(2)}, u32[]{:S(2)}) collective-permute-start(bf16[320,1152]{1,0:T(8,128)(2,1)} %get-tuple-element.223), channel_id=1, source_target_pairs={{0,4},{4,0},{1,5},{5,1},{2,6},{6,2},{3,7},{7,3},{8,12},{12,8},{9,1... | collective-permute-start | bytes 2211848 | tf_op jit(solution)/shard_map/ppermute | solution.py:979
  42.6 34.5 %collective-permute-start.2 = (bf16[640,512]{1,0:T(8,128)(2,1)S(1)}, bf16[640,512]{1,0:T(8,128)(2,1)S(1)}, u32[]{:S(2)}, u32[]{:S(2)}) collective-permute-start(bf16[640,512]{1,0:T(8,128)(2,1)S(1)} %pad_maximum_fusion.14.refs_0_), channel_id=1, source_target_pairs={{0,16},{8,24},{16,0},{24,8},{1,17},{9,25},{17,1},{25,9},{2,18},{10... | collective-permute-start | bytes 1966088 | tf_op jit(solution)/shard_map/ppermute | solution.py:1018
  45.2 32.7 %collective-permute-start.3 = (bf16[640,512]{1,0:T(8,128)(2,1)S(1)}, bf16[640,512]{1,0:T(8,128)(2,1)}, u32[]{:S(2)}, u32[]{:S(2)}) collective-permute-start(bf16[640,512]{1,0:T(8,128)(2,1)S(1)} %pad_maximum_fusion.14.refs_0_), channel_id=1, source_target_pairs={{0,24},{8,0},{16,8},{24,16},{1,25},{9,1},{17,9},{25,17},{2,26},{10... | collective-permute-start | bytes 1966088 | tf_op jit(solution)/shard_map/ppermute | solution.py:1018
  47.5 90.2 %collective-permute-start.9 = (bf16[640,320]{1,0:T(8,128)(2,1)}, bf16[640,320]{1,0:T(8,128)(2,1)}, u32[]{:S(2)}, u32[]{:S(2)}) collective-permute-start(bf16[640,320]{1,0:T(8,128)(2,1)} %pad_maximum_fusion.17.refs_0_), channel_id=1, source_target_pairs={{0,8},{8,16},{16,24},{24,0},{1,9},{9,17},{17,25},{25,1},{2,10},{10... | collective-permute-start | bytes 1228808 | tf_op jit(solution)/shard_map/ppermute | solution.py:1018
  71.5 66.9 %collective-permute-start.10 = (bf16[640,320]{1,0:T(8,128)(2,1)}, bf16[640,320]{1,0:T(8,128)(2,1)}, u32[]{:S(2)}, u32[]{:S(2)}) collective-permute-start(bf16[640,320]{1,0:T(8,128)(2,1)} %pad_maximum_fusion.17.refs_0_), channel_id=1, source_target_pairs={{0,16},{8,24},{16,0},{24,8},{1,17},{9,25},{17,1},{25,9},{2,18},{10... | collective-permute-start | bytes 1228808 | tf_op jit(solution)/shard_map/ppermute | solution.py:1018
  73.9 64.5 %collective-permute-start.11 = (bf16[640,320]{1,0:T(8,128)(2,1)}, bf16[640,320]{1,0:T(8,128)(2,1)}, u32[]{:S(2)}, u32[]{:S(2)}) collective-permute-start(bf16[640,320]{1,0:T(8,128)(2,1)} %pad_maximum_fusion.17.refs_0_), channel_id=1, source_target_pairs={{0,24},{8,0},{16,8},{24,16},{1,25},{9,1},{17,9},{25,17},{2,26},{10... | collective-permute-start | bytes 1228808 | tf_op jit(solution)/shard_map/ppermute | solution.py:1018
  90.6 22.2 %collective-permute-start.7 = (bf16[128,2560]{1,0:T(8,128)(2,1)S(1)}, bf16[128,2560]{1,0:T(8,128)(2,1)S(1)}, u32[]{:S(2)}, u32[]{:S(2)}) collective-permute-start(bf16[128,2560]{1,0:T(8,128)(2,1)S(1)} %get-tuple-element.635), channel_id=1, source_target_pairs={{0,2},{1,3},{2,0},{3,1},{4,6},{5,7},{6,4},{7,5},{8,10},{9,11},{10,... | collective-permute-start | bytes 1966088 | tf_op jit(solution)/shard_map/ppermute | solution.py:983
  92.1 42.9 %collective-permute-start.8 = (bf16[128,2560]{1,0:T(8,128)(2,1)}, bf16[128,2560]{1,0:T(8,128)(2,1)S(1)}, u32[]{:S(2)}, u32[]{:S(2)}) collective-permute-start(bf16[128,2560]{1,0:T(8,128)(2,1)} %get-tuple-element.634), channel_id=1, source_target_pairs={{0,4},{4,0},{1,5},{5,1},{2,6},{6,2},{3,7},{7,3},{8,12},{12,8},{9,1... | collective-permute-start | bytes 1966088 | tf_op jit(solution)/shard_map/ppermute | solution.py:979
  112.8 57.6 %collective-permute-start.14 = (bf16[640,1152]{1,0:T(8,128)(2,1)S(1)}, bf16[640,1152]{1,0:T(8,128)(2,1)S(1)}, u32[]{:S(2)}, u32[]{:S(2)}) collective-permute-start(bf16[640,1152]{1,0:T(8,128)(2,1)S(1)} %pad_maximum_fusion.9.refs_0_.refs_2_), channel_id=1, source_target_pairs={{0,8},{8,16},{16,24},{24,0},{1,9},{9,17},{17,25},{25,1},{2,10},{10... | collective-permute-start | bytes 4423688 | tf_op jit(solution)/shard_map/ppermute | solution.py:1018
  135.0 35.4 %collective-permute-start.12 = (bf16[2,128,2560]{2,1,0:T(8,128)(2,1)S(1)}, bf16[2,128,2560]{2,1,0:T(8,128)(2,1)}, u32[]{:S(2)}, u32[]{:S(2)}) collective-permute-start(bf16[2,128,2560]{2,1,0:T(8,128)(2,1)S(1)} %pad_maximum_fusion.10), channel_id=1, source_target_pairs={{0,4},{4,0},{1,5},{5,1},{2,6},{6,2},{3,7},{7,3},{8,12},{12,8},{9,1... | collective-permute-start | bytes 3932168 | tf_op jit(solution)/shard_map/ppermute | solution.py:979
  137.7 32.7 %collective-permute-start.13 = (bf16[2,128,2560]{2,1,0:T(8,128)(2,1)S(1)}, bf16[2,128,2560]{2,1,0:T(8,128)(2,1)}, u32[]{:S(2)}, u32[]{:S(2)}) collective-permute-start(bf16[2,128,2560]{2,1,0:T(8,128)(2,1)S(1)} %pad_maximum_fusion.11), channel_id=1, source_target_pairs={{0,2},{1,3},{2,0},{3,1},{4,6},{5,7},{6,4},{7,5},{8,10},{9,11},{10,... | collective-permute-start | bytes 3932168 | tf_op jit(solution)/shard_map/ppermute | solution.py:983
  170.5 36.5 %collective-permute-start.16 = (bf16[640,1152]{1,0:T(8,128)(2,1)S(1)}, bf16[640,1152]{1,0:T(8,128)(2,1)S(1)}, u32[]{:S(2)}, u32[]{:S(2)}) collective-permute-start(bf16[640,1152]{1,0:T(8,128)(2,1)S(1)} %collective-permute-done.14.refs_1_.refs_3_), channel_id=1, source_target_pairs={{0,8},{8,16},{16,24},{24,0},{1,9},{9,17},{17,25},{25,1},{2,10},{10... | collective-permute-start | bytes 4423688 | tf_op jit(solution)/shard_map/ppermute | solution.py:1018
  213.7 53.0 %collective-permute-start.20 = (bf16[1024,2560]{1,0:T(8,128)(2,1)S(1)}, bf16[1024,2560]{1,0:T(8,128)(2,1)S(1)}, u32[]{:S(2)}, u32[]{:S(2)}) collective-permute-start(bf16[1024,2560]{1,0:T(8,128)(2,1)S(1)} %bitcast_dynamic-update-slice_fusion.9), channel_id=1, source_target_pairs={{0,1},{1,0},{2,3},{3,2},{4,5},{5,4},{6,7},{7,6},{8,9},{9,8},{10,11... | collective-permute-start | bytes 15728648 | tf_op jit(solution)/shard_map/ppermute | solution.py:983
  213.8 24.6 %collective-permute-start.23 = (bf16[320,1536]{1,0:T(8,128)(2,1)S(1)}, bf16[320,1536]{1,0:T(8,128)(2,1)S(1)}, u32[]{:S(2)}, u32[]{:S(2)}) collective-permute-start(bf16[320,1536]{1,0:T(8,128)(2,1)S(1)} %copy-done.51), channel_id=1, source_target_pairs={{0,4},{4,0},{1,5},{5,1},{2,6},{6,2},{3,7},{7,3},{8,12},{12,8},{9,1... | collective-permute-start | bytes 2949128 | tf_op jit(solution)/shard_map/ppermute | solution.py:979
  214.6 36.1 %collective-permute-start.19 = (bf16[640,1152]{1,0:T(8,128)(2,1)S(1)}, bf16[640,1152]{1,0:T(8,128)(2,1)S(1)}, u32[]{:S(2)}, u32[]{:S(2)}) collective-permute-start(bf16[640,1152]{1,0:T(8,128)(2,1)S(1)} %collective-permute-done.16.refs_2_.refs_4_), channel_id=1, source_target_pairs={{0,8},{8,16},{16,24},{24,0},{1,9},{9,17},{17,25},{25,1},{2,10},{10... | collective-permute-start | bytes 4423688 | tf_op jit(solution)/shard_map/ppermute | solution.py:1018
  214.6 36.4 %collective-permute-start.17 = (bf16[2,128,2560]{2,1,0:T(8,128)(2,1)S(1)}, bf16[2,128,2560]{2,1,0:T(8,128)(2,1)S(1)}, u32[]{:S(2)}, u32[]{:S(2)}) collective-permute-start(bf16[2,128,2560]{2,1,0:T(8,128)(2,1)S(1)} %fusion.11), channel_id=1, source_target_pairs={{0,2},{1,3},{2,0},{3,1},{4,6},{5,7},{6,4},{7,5},{8,10},{9,11},{10,... | collective-permute-start | bytes 3932168 | tf_op jit(solution)/shard_map/ppermute | solution.py:983
  216.1 49.9 %collective-permute-start.18 = (bf16[2,128,2560]{2,1,0:T(8,128)(2,1)S(1)}, bf16[2,128,2560]{2,1,0:T(8,128)(2,1)S(1)}, u32[]{:S(2)}, u32[]{:S(2)}) collective-permute-start(bf16[2,128,2560]{2,1,0:T(8,128)(2,1)S(1)} %get-tuple-element.236), channel_id=1, source_target_pairs={{0,4},{4,0},{1,5},{5,1},{2,6},{6,2},{3,7},{7,3},{8,12},{12,8},{9,1... | collective-permute-start | bytes 3932168 | tf_op jit(solution)/shard_map/ppermute | solution.py:979
  250.8 46.1 %collective-permute-start.24 = (bf16[640,1536]{1,0:T(8,128)(2,1)S(1)}, bf16[640,1536]{1,0:T(8,128)(2,1)S(1)}, u32[]{:S(2)}, u32[]{:S(2)}) collective-permute-start(bf16[640,1536]{1,0:T(8,128)(2,1)S(1)} %pad_maximum_fusion.2.refs_0_.refs_6_), channel_id=1, source_target_pairs={{0,8},{8,16},{16,24},{24,0},{1,9},{9,17},{17,25},{25,1},{2,10},{10... | collective-permute-start | bytes 5898248 | tf_op jit(solution)/shard_map/ppermute | solution.py:1018
  302.5 44.4 %collective-permute-start.29 = (bf16[640,1536]{1,0:T(8,128)(2,1)S(1)}, bf16[640,1536]{1,0:T(8,128)(2,1)S(1)}, u32[]{:S(2)}, u32[]{:S(2)}) collective-permute-start(bf16[640,1536]{1,0:T(8,128)(2,1)S(1)} %collective-permute-done.24.refs_1_.refs_7_), channel_id=1, source_target_pairs={{0,8},{8,16},{16,24},{24,0},{1,9},{9,17},{17,25},{25,1},{2,10},{10... | collective-permute-start | bytes 5898248 | tf_op jit(solution)/shard_map/ppermute | solution.py:1018
  315.0 32.0 %collective-permute-start.27 = (bf16[2,128,2560]{2,1,0:T(8,128)(2,1)S(1)}, bf16[2,128,2560]{2,1,0:T(8,128)(2,1)S(1)}, u32[]{:S(2)}, u32[]{:S(2)}) collective-permute-start(bf16[2,128,2560]{2,1,0:T(8,128)(2,1)S(1)} %pad_maximum_fusion.12), channel_id=1, source_target_pairs={{0,4},{4,0},{1,5},{5,1},{2,6},{6,2},{3,7},{7,3},{8,12},{12,8},{9,1... | collective-permute-start | bytes 3932168 | tf_op jit(solution)/shard_map/ppermute | solution.py:979
  317.0 29.9 %collective-permute-start.28 = (bf16[2,128,2560]{2,1,0:T(8,128)(2,1)S(1)}, bf16[2,128,2560]{2,1,0:T(8,128)(2,1)S(1)}, u32[]{:S(2)}, u32[]{:S(2)}) collective-permute-start(bf16[2,128,2560]{2,1,0:T(8,128)(2,1)S(1)} %pad_maximum_fusion.13), channel_id=1, source_target_pairs={{0,2},{1,3},{2,0},{3,1},{4,6},{5,7},{6,4},{7,5},{8,10},{9,11},{10,... | collective-permute-start | bytes 3932168 | tf_op jit(solution)/shard_map/ppermute | solution.py:983
  348.2 64.1 %collective-permute-start.33 = (bf16[640,1536]{1,0:T(8,128)(2,1)S(1)}, bf16[640,1536]{1,0:T(8,128)(2,1)}, u32[]{:S(2)}, u32[]{:S(2)}) collective-permute-start(bf16[640,1536]{1,0:T(8,128)(2,1)S(1)} %collective-permute-done.29.refs_2_.refs_8_), channel_id=1, source_target_pairs={{0,8},{8,16},{16,24},{24,0},{1,9},{9,17},{17,25},{25,1},{2,10},{10... | collective-permute-start | bytes 5898248 | tf_op jit(solution)/shard_map/ppermute | solution.py:1018
  408.8 28.1 %collective-permute-start.34 = (bf16[320,1152]{1,0:T(8,128)(2,1)}, bf16[320,1152]{1,0:T(8,128)(2,1)S(1)}, u32[]{:S(2)}, u32[]{:S(2)}) collective-permute-start(bf16[320,1152]{1,0:T(8,128)(2,1)} %get-tuple-element.257), channel_id=1, source_target_pairs={{0,4},{4,0},{1,5},{5,1},{2,6},{6,2},{3,7},{7,3},{8,12},{12,8},{9,1... | collective-permute-start | bytes 2211848 | tf_op jit(solution)/shard_map/ppermute | solution.py:979
  409.6 56.1 %collective-permute-start.35 = (bf16[320,1152]{1,0:T(8,128)(2,1)}, bf16[320,1152]{1,0:T(8,128)(2,1)}, u32[]{:S(2)}, u32[]{:S(2)}) collective-permute-start(bf16[320,1152]{1,0:T(8,128)(2,1)} %get-tuple-element.265), channel_id=1, source_target_pairs={{0,24},{8,0},{16,8},{24,16},{1,25},{9,1},{17,9},{25,17},{2,26},{10... | collective-permute-start | bytes 2211848 | tf_op jit(solution)/shard_map/ppermute | solution.py:1018
  411.7 61.8 %collective-permute-start.36 = (bf16[320,1152]{1,0:T(8,128)(2,1)}, bf16[320,1152]{1,0:T(8,128)(2,1)}, u32[]{:S(2)}, u32[]{:S(2)}) collective-permute-start(bf16[320,1152]{1,0:T(8,128)(2,1)} %get-tuple-element.266), channel_id=1, source_target_pairs={{0,16},{8,24},{16,0},{24,8},{1,17},{9,25},{17,1},{25,9},{2,18},{10... | collective-permute-start | bytes 2211848 | tf_op jit(solution)/shard_map/ppermute | solution.py:1018
  411.7 61.8 %collective-permute-start.37 = (bf16[320,1152]{1,0:T(8,128)(2,1)}, bf16[320,1152]{1,0:T(8,128)(2,1)}, u32[]{:S(2)}, u32[]{:S(2)}) collective-permute-start(bf16[320,1152]{1,0:T(8,128)(2,1)} %get-tuple-element.267), channel_id=1, source_target_pairs={{0,8},{8,16},{16,24},{24,0},{1,9},{9,17},{17,25},{25,1},{2,10},{10... | collective-permute-start | bytes 2211848 | tf_op jit(solution)/shard_map/ppermute | solution.py:1018
  473.5 68.6 %collective-permute-start.41 = (bf16[320,1152]{1,0:T(8,128)(2,1)}, bf16[320,1152]{1,0:T(8,128)(2,1)S(1)}, u32[]{:S(2)}, u32[]{:S(2)}) collective-permute-start(bf16[320,1152]{1,0:T(8,128)(2,1)} %collective-permute-done.35), channel_id=1, source_target_pairs={{0,4},{4,0},{1,5},{5,1},{2,6},{6,2},{3,7},{7,3},{8,12},{12,8},{9,1... | collective-permute-start | bytes 2211848 | tf_op jit(solution)/shard_map/ppermute | solution.py:979
  474.8 67.3 %collective-permute-start.42 = (bf16[320,1152]{1,0:T(8,128)(2,1)}, bf16[320,1152]{1,0:T(8,128)(2,1)}, u32[]{:S(2)}, u32[]{:S(2)}) collective-permute-start(bf16[320,1152]{1,0:T(8,128)(2,1)} %collective-permute-done.36), channel_id=1, source_target_pairs={{0,4},{4,0},{1,5},{5,1},{2,6},{6,2},{3,7},{7,3},{8,12},{12,8},{9,1... | collective-permute-start | bytes 2211848 | tf_op jit(solution)/shard_map/ppermute | solution.py:979
  475.6 66.6 %collective-permute-start.43 = (bf16[320,1152]{1,0:T(8,128)(2,1)}, bf16[320,1152]{1,0:T(8,128)(2,1)}, u32[]{:S(2)}, u32[]{:S(2)}) collective-permute-start(bf16[320,1152]{1,0:T(8,128)(2,1)} %get-tuple-element.280), channel_id=1, source_target_pairs={{0,24},{8,0},{16,8},{24,16},{1,25},{9,1},{17,9},{25,17},{2,26},{10... | collective-permute-start | bytes 2211848 | tf_op jit(solution)/shard_map/ppermute | solution.py:1018
  490.5 31.1 %collective-permute-start.39 = (bf16[2,128,2560]{2,1,0:T(8,128)(2,1)}, bf16[2,128,2560]{2,1,0:T(8,128)(2,1)S(1)}, u32[]{:S(2)}, u32[]{:S(2)}) collective-permute-start(bf16[2,128,2560]{2,1,0:T(8,128)(2,1)} %fusion.15), channel_id=1, source_target_pairs={{0,2},{1,3},{2,0},{3,1},{4,6},{5,7},{6,4},{7,5},{8,10},{9,11},{10,... | collective-permute-start | bytes 3932168 | tf_op jit(solution)/shard_map/ppermute | solution.py:983
  491.4 45.3 %collective-permute-start.40 = (bf16[2,128,2560]{2,1,0:T(8,128)(2,1)}, bf16[2,128,2560]{2,1,0:T(8,128)(2,1)}, u32[]{:S(2)}, u32[]{:S(2)}) collective-permute-start(bf16[2,128,2560]{2,1,0:T(8,128)(2,1)} %get-tuple-element.612), channel_id=1, source_target_pairs={{0,4},{4,0},{1,5},{5,1},{2,6},{6,2},{3,7},{7,3},{8,12},{12,8},{9,1... | collective-permute-start | bytes 3932168 | tf_op jit(solution)/shard_map/ppermute | solution.py:979
  521.6 43.2 %collective-permute-start.46 = (bf16[320,1536]{1,0:T(8,128)(2,1)}, bf16[320,1536]{1,0:T(8,128)(2,1)}, u32[]{:S(2)}, u32[]{:S(2)}) collective-permute-start(bf16[320,1536]{1,0:T(8,128)(2,1)} %get-tuple-element.287), channel_id=1, source_target_pairs={{0,24},{8,0},{16,8},{24,16},{1,25},{9,1},{17,9},{25,17},{2,26},{10... | collective-permute-start | bytes 2949128 | tf_op jit(solution)/shard_map/ppermute | solution.py:1018
  536.6 33.0 %collective-permute-start.47 = (bf16[320,1536]{1,0:T(8,128)(2,1)}, bf16[320,1536]{1,0:T(8,128)(2,1)}, u32[]{:S(2)}, u32[]{:S(2)}) collective-permute-start(bf16[320,1536]{1,0:T(8,128)(2,1)} %get-tuple-element.288), channel_id=1, source_target_pairs={{0,8},{8,16},{16,24},{24,0},{1,9},{9,17},{17,25},{25,1},{2,10},{10... | collective-permute-start | bytes 2949128 | tf_op jit(solution)/shard_map/ppermute | solution.py:1018
  543.2 26.4 %collective-permute-start.44 = (bf16[128,2560]{1,0:T(8,128)(2,1)}, bf16[128,2560]{1,0:T(8,128)(2,1)}, u32[]{:S(2)}, u32[]{:S(2)}) collective-permute-start(bf16[128,2560]{1,0:T(8,128)(2,1)} %slice_bitcast_fusion.23), channel_id=1, source_target_pairs={{0,4},{4,0},{1,5},{5,1},{2,6},{6,2},{3,7},{7,3},{8,12},{12,8},{9,1... | collective-permute-start | bytes 1966088 | tf_op jit(solution)/shard_map/ppermute | solution.py:979
  545.4 24.2 %collective-permute-start.45 = (bf16[128,2560]{1,0:T(8,128)(2,1)}, bf16[128,2560]{1,0:T(8,128)(2,1)}, u32[]{:S(2)}, u32[]{:S(2)}) collective-permute-start(bf16[128,2560]{1,0:T(8,128)(2,1)} %slice_bitcast_fusion.22), channel_id=1, source_target_pairs={{0,2},{1,3},{2,0},{3,1},{4,6},{5,7},{6,4},{7,5},{8,10},{9,11},{10,... | collective-permute-start | bytes 1966088 | tf_op jit(solution)/shard_map/ppermute | solution.py:983
  588.9 47.3 %collective-permute-start.49 = (bf16[2,128,2560]{2,1,0:T(8,128)(2,1)S(1)}, bf16[2,128,2560]{2,1,0:T(8,128)(2,1)S(1)}, u32[]{:S(2)}, u32[]{:S(2)}) collective-permute-start(bf16[2,128,2560]{2,1,0:T(8,128)(2,1)S(1)} %fusion.19), channel_id=1, source_target_pairs={{0,2},{1,3},{2,0},{3,1},{4,6},{5,7},{6,4},{7,5},{8,10},{9,11},{10,... | collective-permute-start | bytes 3932168 | tf_op jit(solution)/shard_map/ppermute | solution.py:983
  589.5 47.8 %collective-permute-start.50 = (bf16[2,128,2560]{2,1,0:T(8,128)(2,1)S(1)}, bf16[2,128,2560]{2,1,0:T(8,128)(2,1)S(1)}, u32[]{:S(2)}, u32[]{:S(2)}) collective-permute-start(bf16[2,128,2560]{2,1,0:T(8,128)(2,1)S(1)} %fusion.20), channel_id=1, source_target_pairs={{0,4},{4,0},{1,5},{5,1},{2,6},{6,2},{3,7},{7,3},{8,12},{12,8},{9,1... | collective-permute-start | bytes 3932168 | tf_op jit(solution)/shard_map/ppermute | solution.py:979
  590.8 55.0 %collective-permute-start.54 = (bf16[320,1152]{1,0:T(8,128)(2,1)S(1)}, bf16[320,1152]{1,0:T(8,128)(2,1)}, u32[]{:S(2)}, u32[]{:S(2)}) collective-permute-start(bf16[320,1152]{1,0:T(8,128)(2,1)S(1)} %copy-done.53), channel_id=1, source_target_pairs={{0,8},{8,16},{16,24},{24,0},{1,9},{9,17},{17,25},{25,1},{2,10},{10... | collective-permute-start | bytes 2211848 | tf_op jit(solution)/shard_map/ppermute | solution.py:1018
  590.8 77.8 %collective-permute-start.53 = (bf16[320,1536]{1,0:T(8,128)(2,1)S(1)}, bf16[320,1536]{1,0:T(8,128)(2,1)S(1)}, u32[]{:S(2)}, u32[]{:S(2)}) collective-permute-start(bf16[320,1536]{1,0:T(8,128)(2,1)S(1)} %copy-done.52), channel_id=1, source_target_pairs={{0,16},{8,24},{16,0},{24,8},{1,17},{9,25},{17,1},{25,9},{2,18},{10... | collective-permute-start | bytes 2949128 | tf_op jit(solution)/shard_map/ppermute | solution.py:1018
  641.1 28.1 %collective-permute-start.51 = (bf16[128,2560]{1,0:T(8,128)(2,1)S(1)}, bf16[128,2560]{1,0:T(8,128)(2,1)}, u32[]{:S(2)}, u32[]{:S(2)}) collective-permute-start(bf16[128,2560]{1,0:T(8,128)(2,1)S(1)} %slice_bitcast_fusion.10), channel_id=1, source_target_pairs={{0,4},{4,0},{1,5},{5,1},{2,6},{6,2},{3,7},{7,3},{8,12},{12,8},{9,1... | collective-permute-start | bytes 1966088 | tf_op jit(solution)/shard_map/ppermute | solution.py:979
  641.6 28.0 %collective-permute-start.52 = (bf16[128,2560]{1,0:T(8,128)(2,1)S(1)}, bf16[128,2560]{1,0:T(8,128)(2,1)}, u32[]{:S(2)}, u32[]{:S(2)}) collective-permute-start(bf16[128,2560]{1,0:T(8,128)(2,1)S(1)} %slice_bitcast_fusion.9), channel_id=1, source_target_pairs={{0,2},{1,3},{2,0},{3,1},{4,6},{5,7},{6,4},{7,5},{8,10},{9,11},{10,... | collective-permute-start | bytes 1966088 | tf_op jit(solution)/shard_map/ppermute | solution.py:983
  643.3 96.0 %collective-permute-start.55 = (bf16[320,1152]{1,0:T(8,128)(2,1)}, bf16[320,1152]{1,0:T(8,128)(2,1)S(1)}, u32[]{:S(2)}, u32[]{:S(2)}) collective-permute-start(bf16[320,1152]{1,0:T(8,128)(2,1)} %get-tuple-element.307), channel_id=1, source_target_pairs={{0,16},{8,24},{16,0},{24,8},{1,17},{9,25},{17,1},{25,9},{2,18},{10... | collective-permute-start | bytes 2211848 | tf_op jit(solution)/shard_map/ppermute | solution.py:1018
  669.6 69.8 %collective-permute-start.56 = (bf16[320,1152]{1,0:T(8,128)(2,1)}, bf16[320,1152]{1,0:T(8,128)(2,1)}, u32[]{:S(2)}, u32[]{:S(2)}) collective-permute-start(bf16[320,1152]{1,0:T(8,128)(2,1)} %collective-permute-done.37), channel_id=1, source_target_pairs={{0,4},{4,0},{1,5},{5,1},{2,6},{6,2},{3,7},{7,3},{8,12},{12,8},{9,1... | collective-permute-start | bytes 2211848 | tf_op jit(solution)/shard_map/ppermute | solution.py:979
  670.3 69.1 %collective-permute-start.57 = (bf16[320,1536]{1,0:T(8,128)(2,1)}, bf16[320,1536]{1,0:T(8,128)(2,1)}, u32[]{:S(2)}, u32[]{:S(2)}) collective-permute-start(bf16[320,1536]{1,0:T(8,128)(2,1)} %get-tuple-element.309), channel_id=1, source_target_pairs={{0,4},{4,0},{1,5},{5,1},{2,6},{6,2},{3,7},{7,3},{8,12},{12,8},{9,1... | collective-permute-start | bytes 2949128 | tf_op jit(solution)/shard_map/ppermute | solution.py:979
  671.6 67.8 %collective-permute-start.58 = (bf16[320,1536]{1,0:T(8,128)(2,1)}, bf16[320,1536]{1,0:T(8,128)(2,1)}, u32[]{:S(2)}, u32[]{:S(2)}) collective-permute-start(bf16[320,1536]{1,0:T(8,128)(2,1)} %collective-permute-done.46), channel_id=1, source_target_pairs={{0,4},{4,0},{1,5},{5,1},{2,6},{6,2},{3,7},{7,3},{8,12},{12,8},{9,1... | collective-permute-start | bytes 2949128 | tf_op jit(solution)/shard_map/ppermute | solution.py:979
  672.3 67.1 %collective-permute-start.59 = (bf16[320,1536]{1,0:T(8,128)(2,1)}, bf16[320,1536]{1,0:T(8,128)(2,1)}, u32[]{:S(2)}, u32[]{:S(2)}) collective-permute-start(bf16[320,1536]{1,0:T(8,128)(2,1)} %get-tuple-element.315), channel_id=1, source_target_pairs={{0,24},{8,0},{16,8},{24,16},{1,25},{9,1},{17,9},{25,17},{2,26},{10... | collective-permute-start | bytes 2949128 | tf_op jit(solution)/shard_map/ppermute | solution.py:1018
  746.8 65.8 %collective-permute-start.63 = (bf16[320,1536]{1,0:T(8,128)(2,1)}, bf16[320,1536]{1,0:T(8,128)(2,1)}, u32[]{:S(2)}, u32[]{:S(2)}) collective-permute-start(bf16[320,1536]{1,0:T(8,128)(2,1)} %get-tuple-element.326), channel_id=1, source_target_pairs={{0,16},{8,24},{16,0},{24,8},{1,17},{9,25},{17,1},{25,9},{2,18},{10... | collective-permute-start | bytes 2949128 | tf_op jit(solution)/shard_map/ppermute | solution.py:1018
  746.9 65.7 %collective-permute-start.64 = (bf16[320,1536]{1,0:T(8,128)(2,1)}, bf16[320,1536]{1,0:T(8,128)(2,1)}, u32[]{:S(2)}, u32[]{:S(2)}) collective-permute-start(bf16[320,1536]{1,0:T(8,128)(2,1)} %get-tuple-element.327), channel_id=1, source_target_pairs={{0,8},{8,16},{16,24},{24,0},{1,9},{9,17},{17,25},{25,1},{2,10},{10... | collective-permute-start | bytes 2949128 | tf_op jit(solution)/shard_map/ppermute | solution.py:1018
  748.7 63.9 %collective-permute-start.65 = (bf16[320,1536]{1,0:T(8,128)(2,1)}, bf16[320,1536]{1,0:T(8,128)(2,1)}, u32[]{:S(2)}, u32[]{:S(2)}) collective-permute-start(bf16[320,1536]{1,0:T(8,128)(2,1)} %copy-done.50), channel_id=1, source_target_pairs={{0,4},{4,0},{1,5},{5,1},{2,6},{6,2},{3,7},{7,3},{8,12},{12,8},{9,1... | collective-permute-start | bytes 2949128 | tf_op jit(solution)/shard_map/ppermute | solution.py:979
  757.2 37.0 %collective-permute-start.61 = (bf16[2,128,2560]{2,1,0:T(8,128)(2,1)}, bf16[2,128,2560]{2,1,0:T(8,128)(2,1)}, u32[]{:S(2)}, u32[]{:S(2)}) collective-permute-start(bf16[2,128,2560]{2,1,0:T(8,128)(2,1)} %fusion.23), channel_id=1, source_target_pairs={{0,2},{1,3},{2,0},{3,1},{4,6},{5,7},{6,4},{7,5},{8,10},{9,11},{10,... | collective-permute-start | bytes 3932168 | tf_op jit(solution)/shard_map/ppermute | solution.py:983
  758.6 42.1 %collective-permute-start.62 = (bf16[2,128,2560]{2,1,0:T(8,128)(2,1)}, bf16[2,128,2560]{2,1,0:T(8,128)(2,1)}, u32[]{:S(2)}, u32[]{:S(2)}) collective-permute-start(bf16[2,128,2560]{2,1,0:T(8,128)(2,1)} %get-tuple-element.608), channel_id=1, source_target_pairs={{0,4},{4,0},{1,5},{5,1},{2,6},{6,2},{3,7},{7,3},{8,12},{12,8},{9,1... | collective-permute-start | bytes 3932168 | tf_op jit(solution)/shard_map/ppermute | solution.py:979
  817.0 33.5 %collective-permute-start.68 = (bf16[320,1536]{1,0:T(8,128)(2,1)}, bf16[320,1536]{1,0:T(8,128)(2,1)S(1)}, u32[]{:S(2)}, u32[]{:S(2)}) collective-permute-start(bf16[320,1536]{1,0:T(8,128)(2,1)} %collective-permute-done.47), channel_id=1, source_target_pairs={{0,4},{4,0},{1,5},{5,1},{2,6},{6,2},{3,7},{7,3},{8,12},{12,8},{9,1... | collective-permute-start | bytes 2949128 | tf_op jit(solution)/shard_map/ppermute | solution.py:979
  817.8 32.8 %collective-permute-start.69 = (bf16[320,896]{1,0:T(8,128)(2,1)S(1)}, bf16[320,896]{1,0:T(8,128)(2,1)S(1)}, u32[]{:S(2)}, u32[]{:S(2)}) collective-permute-start(bf16[320,896]{1,0:T(8,128)(2,1)S(1)} %copy-done.58), channel_id=1, source_target_pairs={{0,24},{8,0},{16,8},{24,16},{1,25},{9,1},{17,9},{25,17},{2,26},{10... | collective-permute-start | bytes 1720328 | tf_op jit(solution)/shard_map/ppermute | solution.py:1018
  817.8 50.0 %collective-permute-start.70 = (bf16[320,896]{1,0:T(8,128)(2,1)S(1)}, bf16[320,896]{1,0:T(8,128)(2,1)S(1)}, u32[]{:S(2)}, u32[]{:S(2)}) collective-permute-start(bf16[320,896]{1,0:T(8,128)(2,1)S(1)} %copy-done.57), channel_id=1, source_target_pairs={{0,16},{8,24},{16,0},{24,8},{1,17},{9,25},{17,1},{25,9},{2,18},{10... | collective-permute-start | bytes 1720328 | tf_op jit(solution)/shard_map/ppermute | solution.py:1018
  830.3 37.4 %collective-permute-start.71 = (bf16[320,896]{1,0:T(8,128)(2,1)S(1)}, bf16[320,896]{1,0:T(8,128)(2,1)S(1)}, u32[]{:S(2)}, u32[]{:S(2)}) collective-permute-start(bf16[320,896]{1,0:T(8,128)(2,1)S(1)} %copy-done.56), channel_id=1, source_target_pairs={{0,8},{8,16},{16,24},{24,0},{1,9},{9,17},{17,25},{25,1},{2,10},{10... | collective-permute-start | bytes 1720328 | tf_op jit(solution)/shard_map/ppermute | solution.py:1018
  867.7 77.9 %collective-permute-start.75 = (bf16[320,896]{1,0:T(8,128)(2,1)}, bf16[320,896]{1,0:T(8,128)(2,1)S(1)}, u32[]{:S(2)}, u32[]{:S(2)}) collective-permute-start(bf16[320,896]{1,0:T(8,128)(2,1)} %get-tuple-element.341), channel_id=1, source_target_pairs={{0,4},{4,0},{1,5},{5,1},{2,6},{6,2},{3,7},{7,3},{8,12},{12,8},{9,1... | collective-permute-start | bytes 1720328 | tf_op jit(solution)/shard_map/ppermute | solution.py:979
  869.2 72.2 %collective-permute-start.72 = (bf16[320,896]{1,0:T(8,128)(2,1)}, bf16[320,896]{1,0:T(8,128)(2,1)}, u32[]{:S(2)}, u32[]{:S(2)}) collective-permute-start(bf16[320,896]{1,0:T(8,128)(2,1)} %get-tuple-element.346), channel_id=1, source_target_pairs={{0,24},{8,0},{16,8},{24,16},{1,25},{9,1},{17,9},{25,17},{2,26},{10... | collective-permute-start | bytes 1720328 | tf_op jit(solution)/shard_map/ppermute | solution.py:1018
  869.2 72.2 %collective-permute-start.73 = (bf16[320,896]{1,0:T(8,128)(2,1)}, bf16[320,896]{1,0:T(8,128)(2,1)}, u32[]{:S(2)}, u32[]{:S(2)}) collective-permute-start(bf16[320,896]{1,0:T(8,128)(2,1)} %get-tuple-element.347), channel_id=1, source_target_pairs={{0,16},{8,24},{16,0},{24,8},{1,17},{9,25},{17,1},{25,9},{2,18},{10... | collective-permute-start | bytes 1720328 | tf_op jit(solution)/shard_map/ppermute | solution.py:1018
  871.2 70.2 %collective-permute-start.74 = (bf16[320,896]{1,0:T(8,128)(2,1)}, bf16[320,896]{1,0:T(8,128)(2,1)}, u32[]{:S(2)}, u32[]{:S(2)}) collective-permute-start(bf16[320,896]{1,0:T(8,128)(2,1)} %get-tuple-element.348), channel_id=1, source_target_pairs={{0,8},{8,16},{16,24},{24,0},{1,9},{9,17},{17,25},{25,1},{2,10},{10... | collective-permute-start | bytes 1720328 | tf_op jit(solution)/shard_map/ppermute | solution.py:1018
  874.7 71.1 %collective-permute-start.76 = (bf16[3,320,896]{2,1,0:T(8,128)(2,1)}, bf16[3,320,896]{2,1,0:T(8,128)(2,1)S(1)}, u32[]{:S(2)}, u32[]{:S(2)}) collective-permute-start(bf16[3,320,896]{2,1,0:T(8,128)(2,1)} %pad_maximum_fusion.4), channel_id=1, source_target_pairs={{0,4},{4,0},{1,5},{5,1},{2,6},{6,2},{3,7},{7,3},{8,12},{12,8},{9,1... | collective-permute-start | bytes 5160968 | tf_op jit(solution)/shard_map/ppermute | solution.py:979
  957.0 18.0 %collective-permute-start.78 = (f32[4,2,320]{2,0,1:T(4,128)S(1)}, f32[4,2,320]{2,0,1:T(4,128)S(1)}, u32[]{:S(2)}, u32[]{:S(2)}) collective-permute-start(f32[4,2,320]{2,0,1:T(4,128)S(1)} %copy.193), channel_id=1, source_target_pairs={{0,2},{1,3},{2,0},{3,1},{4,6},{5,7},{6,4},{7,5},{8,10},{9,11},{10,... | collective-permute-start | bytes 30728 | tf_op jit(solution)/shard_map/ppermute | solution.py:983
  (76 other events, 883.2 us)
Sparse Core Ops, SparseCore 0:
  9.9 79.3 all-gather.2
  576.5 92.4 all-gather.4

commit v4 on v3

--- a/solution.py
+++ b/solution.py
@@ -876,7 +876,11 @@
             num_scalar_prefetch=1,
             grid=(rows // size,),
             in_specs=[
-                pl.BlockSpec((size, value.shape[1]), lambda i, p: (i, 0)) for value in (*own, *other)
+                pl.BlockSpec((size, value.shape[1]), lambda i, p: (i, 0)) for value in (*own, other[0])
+            ]
+            + [
+                pl.BlockSpec((None, size, other[1].shape[2]), lambda i, p, k=k: (k, i, 0))
+                for k in range(REPLICA_GROUPS - 1)
             ]
             + [resident((PACK, columns))] * 2
             + [stack, stack, plane, plane] * 2,
@@ -886,7 +890,83 @@
         compiler_params=params(),
         cost_estimate=cost(0, rows * columns * 2 * 90),
         name="attention_update",
-    )(place, *own, *other, jnp.asarray(table[0], low_type), jnp.asarray(table[1], low_type), *query, *output)
+    )(place, *own, other[0], *[other[1]] * (REPLICA_GROUPS - 1), jnp.asarray(table[0], low_type), jnp.asarray(table[1], low_type), *query, *output)
+
+
+def keyvalue_update_kernel(place_ref, *refs):
+    own, other, rest = refs[:REPLICA_GROUPS], refs[REPLICA_GROUPS : 2 * REPLICA_GROUPS], refs[2 * REPLICA_GROUPS :]
+    left, right, pick, first, second, weight, moment = rest[:7]
+    first_new, second_new, delta_out, moment_new, master, copy, gains = rest[7:]
+    near = place_ref[1] == 0
+    value = weight[...]
+    total = None
+    for slot in range(REPLICA_GROUPS):
+        group = lax.rem(place_ref[2] + slot, REPLICA_GROUPS)
+        mine, theirs = own[slot][...], other[slot][...]
+        low, high = jnp.where(near, mine, theirs), jnp.where(near, theirs, mine)
+        gains[group] = dot(pick[...], low, NT) + dot(pick[...], high, NT)
+        grad = dot(left[...], low, NT) + dot(right[...], high, NT)
+        one, two, step = adam_step(
+            grad, first[group], second[group], lambda item: pl.reciprocal(item, approx=True)
+        )
+        first_new[group] = one
+        second_new[group] = two
+        total = step if total is None else total + step
+    delta = mean_step(total, value, inner_rates[1], inner_decays[1])
+    new_moment, new_weight = outer_step(value, delta, moment[...])
+    delta_out[...] = delta
+    moment_new[...] = new_moment
+    master[...] = new_weight
+    copy[...] = new_weight.astype(low_type)
+
+
+def keyvalue_update(place, own, other, first, second, weight, moment):
+    rows, kinds, columns = weight.shape
+    flat = kinds * columns
+    size = math.gcd(flat, 80)
+    table = np.zeros((2, flat, PACK), np.float32)
+    for half in range(2):
+        for kind in range(kinds):
+            for spot in range(HEAD_WIDTH):
+                table[half, kind * columns + half * HEAD_WIDTH + spot, (HEADS + kind) * HEAD_WIDTH + spot] = 1.0
+    turn = lambda value: jnp.moveaxis(value, -3, -1).reshape(value.shape[:-3] + (flat, rows))
+    back = lambda value: jnp.moveaxis(value.reshape(value.shape[:-2] + (kinds, columns, rows)), -1, -3)
+    states = [turn(value) for value in (first, second, weight, moment)]
+    plane = pl.BlockSpec((size, rows), lambda i, p: (i, 0))
+    stack = pl.BlockSpec((REPLICA_GROUPS, size, rows), lambda i, p: (0, i, 0))
+    pick = pl.BlockSpec((size, PACK), lambda i, p: (i, 0))
+    wide = jax.ShapeDtypeStruct((REPLICA_GROUPS, flat, rows), f32)
+    flat_shape = lambda dtype: jax.ShapeDtypeStruct((flat, rows), dtype)
+    *outs, gains = pl.pallas_call(
+        keyvalue_update_kernel,
+        grid_spec=pltpu.PrefetchScalarGridSpec(
+            num_scalar_prefetch=1,
+            grid=(flat // size,),
+            in_specs=[resident((rows, PACK))] * (REPLICA_GROUPS + 1)
+            + [
+                pl.BlockSpec((None, rows, PACK), lambda i, p, k=k: (k, 0, 0), pipeline_mode=pl.Buffered(1))
+                for k in range(REPLICA_GROUPS - 1)
+            ]
+            + [pick, pick, resident((8, PACK)), stack, stack, plane, plane],
+            out_specs=[stack, stack, plane, plane, plane, plane]
+            + [pl.BlockSpec((REPLICA_GROUPS, 8, rows), lambda i, p: (0, 0, 0))],
+        ),
+        out_shape=[wide, wide, flat_shape(f32), flat_shape(f32), flat_shape(f32), flat_shape(low_type)]
+        + [jax.ShapeDtypeStruct((REPLICA_GROUPS, 8, rows), f32)],
+        compiler_params=params(),
+        cost_estimate=cost(0, rows * flat * 90),
+        name="keyvalue_update",
+    )(
+        place,
+        *own,
+        other[0],
+        *[other[1]] * (REPLICA_GROUPS - 1),
+        jnp.asarray(table[0], low_type),
+        jnp.asarray(table[1], low_type),
+        jnp.asarray(gains_selector(), low_type),
+        *states,
+    )
+    return [back(value) for value in outs], gains[:, :2]
 
 
 def optimize(weight, grad, first, second, moment, rate, decay):
@@ -1185,7 +1265,7 @@
     parts = after(chip_stage(parts, theirs[0]), others_one, mine_one[1:2])
     theirs_two = deliver(theirs)
     feed_partial = spread(place, after([hid, hid_two], *parts), [one, two], 2)
-    grad_normed_two = last_stage(parts, *feed_partial, theirs_two[1:2], theirs_two[3:])
+    grad_normed_two = last_stage(parts, *feed_partial)
 
     grad_hidden_one = cotangent.astype(f32) + norm_backward(
         hidden_one, inverse_two, gain_two, grad_normed_two
@@ -1244,7 +1324,6 @@
         (first_down, second_down, down_weight, moment_down),
     )
     mine_last = after(mine_last, updated[0])
-    others_last = [others_last[0]] + [others_last[1][k] for k in range(REPLICA_GROUPS - 1)]
     attention_updated = attention_update(
         place,
         mine_last,
@@ -1253,26 +1332,16 @@
         (first_output, second_output, output_weight, moment_output),
     )
     qry, out = attention_updated[:6], attention_updated[6:]
-    columns = slice(flat, flat + 2 * HEAD_WIDTH + 2)
-    both = [jnp.stack([value[:, columns] for value in part]) for part in (mine_last, others_last)]
-    both = [jnp.where(near, both[0], both[1]), jnp.where(near, both[1], both[0])]
-    if direct:
-        both = [jnp.roll(value, spot, axis=0) for value in both]
-    both = [value.astype(f32) for value in both]
-    pair_total = jnp.concatenate(
-        [value[..., : 2 * HEAD_WIDTH].reshape(REPLICA_GROUPS, rows, 2, HEAD_WIDTH) for value in both], axis=-1
-    )
-    gains_total = jnp.swapaxes(both[0][..., 2 * HEAD_WIDTH :] + both[1][..., 2 * HEAD_WIDTH :], 1, 2)
-    gains_total = tensor_sum(gains_total)
-    kvl = optimize(
-        keyvalue_weight_full,
-        pair_total,
+    kvl, gains_total = keyvalue_update(
+        place,
+        mine_last,
+        others_last,
         keyvalue_first_moment,
         keyvalue_second_moment,
+        keyvalue_weight_full,
         keyvalue_outer_momentum,
-        inner_rates[1],
-        inner_decays[1],
-    )
+    )
+    gains_total = tensor_sum(gains_total)
     gns = optimize(
         norm_gains, gains_total, first_gains, second_gains, moment_gains, inner_rates[5], inner_decays[5]
     )

time: 993 us -> 1030 us (1.037)
  waiting for transfers between devices: 330 us -> 377 us
  Pallas kernels: 376 us -> 387 us
  local copies, waits for them, and re-layouts: 64.4 us -> 53.9 us
    ppermute x30, waiting for transfers between devices: 137 us -> 185 us  [hop(): lax.ppermute(value, 'ring', [(i, (i + step) % ring) for i in range(ring)])]
    all_gather x1, waiting for transfers between devices: 11.4 us -> 0.01 us  [per_device(): tokens_all = lax.all_gather(tokens, plane, axis=0, tiled=True)]
    pallas_call x0 -> x1, Pallas kernels: none -> 10.8 us  [keyvalue_update(): pl.pallas_call(keyvalue_update_kernel, grid_spec=pltpu.PrefetchScalarGrid...]
    unnamed x152 -> x144, local copies, waits for them, and re-layouts: 42.6 us -> 42.2 us
  transfers between devices with their start and end apart: 81 -> 81, of which waited for: 30 -> 25; matrix products, arithmetic and copies ran while one was open for 12% -> 10% of each run, Pallas kernels for 38% -> 37%
where the time goes in v4:
time: 1030 us; the launch traced here: 1020 us
  Pallas kernels  387 us (38%)
  waiting for transfers between devices  377 us (37%)
  starting transfers between devices  115 us (11%)
  other arithmetic  73.9 us (7%)
  local copies, waits for them, and re-layouts  53.9 us (5%)
  between operations  15.5 us (2%)
    ppermute x30, waiting for transfers between devices, hop(): lax.ppermute(value, 'ring', [(i, (i + step) % ring) for i in range(ring)])  185 us
    ppermute x27, waiting for transfers between devices, swap(): return lax.ppermute(value, 'pair', [(0, 1), (1, 0)])  96.1 us
    ppermute x22, waiting for transfers between devices, across(): return lax.ppermute(value, 'tensor', [(i, i ^ bit) for i in range(count)])  95.2 us
    pallas_call x3, Pallas kernels, weight_grad(): pl.pallas_call(functools.partial(weight_grad_kernel, spans, selected, spl...  84.1 us
    ppermute x30, starting transfers between devices, hop(): lax.ppermute(value, 'ring', [(i, (i + step) % ring) for i in range(ring)])  70.8 us
    pallas_call x1, Pallas kernels, feed_update(): pl.pallas_call(feed_update_kernel, grid_spec=pltpu.PrefetchScalarGridSpec...  62.6 us
    pallas_call x2, Pallas kernels, spread(): pl.pallas_call(functools.partial(spread_kernel, tuple((len(blocks) for bl...  47.6 us
    pallas_call x2, Pallas kernels, feed(): pl.pallas_call(functools.partial(feed_kernel, len(blocks), tiles), grid_s...  45.5 us
  transfers between devices with their start and end apart: 81, of which 25 were waited for; matrix products, arithmetic and copies ran while one was open for 10% of the time, Pallas kernels for 37%

profile of v4, /device:TPU:0, one launch (start us, length us, event | category | flops | bytes accessed | tf_op | source)
XLA Modules:
  0.0 1021.7 jit_solution(15479506663493102723)
XLA Ops:
  8.0 3.0 collective-permute-start.4
  16.2 7.0 collective-permute-done
  23.9 3.7 fusion.35
  27.7 2.3 collective-permute-start.1
  30.0 9.1 pack_feed.1
  40.7 2.5 pad_maximum_fusion.4
  43.2 2.3 collective-permute-start.3
  50.3 14.2 %collective-permute-done.6 = bf16[320,1152]{1,0:T(8,128)(2,1)S(1)} collective-permute-done((bf16[320,1152]{1,0:T(8,128)(2,1)}, bf16[320,1152]{1,0:T(8,128)(2,1)S(1)}, u32[]{:S(2)}, u32[]{:S(2)}) %collective-permute-start.6) | collective-permute-done | bytes 737312 | tf_op jit(solution)/shard_map/ppermute | solution.py:1059
  67.1 44.1 %collective-permute-done.2.refs_2_ = bf16[640,512]{1,0:T(8,128)(2,1)} collective-permute-done((bf16[640,512]{1,0:T(8,128)(2,1)S(1)}, bf16[640,512]{1,0:T(8,128)(2,1)}, u32[]{:S(2)}, u32[]{:S(2)}) %collective-permute-start.2) | collective-permute-done | bytes 655392 | tf_op jit(solution)/shard_map/ppermute | solution.py:1098
  114.4 20.1 %projection.1 = (bf16[2048,2560]{1,0:T(8,128)(2,1)}, bf16[2048,768]{1,0:T(8,128)(2,1)}, f32[8,2560]{1,0:T(8,128)}, bf16[2560,768]{1,0:T(8,128)(2,1)}) custom-call(s32[4]{0:T(128)} %pad_add_fusion.1.place_ref, bf16[2048,2560]{1,0:T(8,128)(2,1)} %all-gather.3.cloned.1.call-done.tokens, bf16[640,512]{1,0:T(8,128)(2,1)} %copy-done.37, ...), custom_call_target="tpu_custom_call" | custom-call | flops 8053063680 | bytes 32768000 | tf_op jit(solution)/shard_map/projection/pallas_call | solution.py:173
  140.7 31.4 %attention.1 = (bf16[2048,512]{1,0:T(8,128)(2,1)}, f32[8,2048]{1,0:T(8,128)}, bf16[1024,2560]{1,0:T(8,128)(2,1)}, bf16[1024,2560]{1,0:T(8,128)(2,1)}) custom-call(s32[4]{0:T(128)} %pad_add_fusion.1.place_ref, bf16[2048,768]{1,0:T(8,128)(2,1)} %get-tuple-element.233.query.key.value, bf16[2048,768]{1,0:T(8,128)(2,1)} %get-tuple-element.233.query.key.value, ...), custom_call_target="tpu_custom_call" | custom-call | flops 20000000000 | bytes 20971520 | tf_op jit(solution)/shard_map/attention/pallas_call | solution.py:267
  172.3 8.8 collective-permute-done.15
  185.4 23.4 %collective-permute-done.16.refs_2_.refs_4_ = bf16[640,1152]{1,0:T(8,128)(2,1)S(1)} collective-permute-done((bf16[640,1152]{1,0:T(8,128)(2,1)S(1)}, bf16[640,1152]{1,0:T(8,128)(2,1)S(1)}, u32[]{:S(2)}, u32[]{:S(2)}) %collective-permute-start.16) | collective-permute-done | bytes 1474592 | tf_op jit(solution)/shard_map/ppermute | solution.py:1098
  219.1 21.0 %collective-permute-done.23 = bf16[320,1536]{1,0:T(8,128)(2,1)S(1)} collective-permute-done((bf16[320,1536]{1,0:T(8,128)(2,1)S(1)}, bf16[320,1536]{1,0:T(8,128)(2,1)S(1)}, u32[]{:S(2)}, u32[]{:S(2)}) %collective-permute-start.23) | collective-permute-done | bytes 983072 | tf_op jit(solution)/shard_map/ppermute | solution.py:1059
  240.4 12.1 %collective-permute-done.19.refs_3_.refs_5_ = bf16[640,1152]{1,0:T(8,128)(2,1)S(1)} collective-permute-done((bf16[640,1152]{1,0:T(8,128)(2,1)S(1)}, bf16[640,1152]{1,0:T(8,128)(2,1)S(1)}, u32[]{:S(2)}, u32[]{:S(2)}) %collective-permute-start.19) | collective-permute-done | bytes 1474592 | tf_op jit(solution)/shard_map/ppermute | solution.py:1098
  252.7 15.1 %collective-permute-done.18 = bf16[2,128,2560]{2,1,0:T(8,128)(2,1)S(1)} collective-permute-done((bf16[2,128,2560]{2,1,0:T(8,128)(2,1)S(1)}, bf16[2,128,2560]{2,1,0:T(8,128)(2,1)S(1)}, u32[]{:S(2)}, u32[]{:S(2)}) %collective-permute-start.18) | collective-permute-done | bytes 1310752 | tf_op jit(solution)/shard_map/ppermute | solution.py:1059
  270.5 2.1 bitcast_dynamic-update-slice_fusion.16
  273.7 2.0 bitcast_dynamic-update-slice_fusion.14
  277.8 2.0 bitcast_dynamic-update-slice_fusion.10
  279.8 2.0 bitcast_dynamic-update-slice_fusion.8
  287.0 11.6 %collective-permute-done.24.refs_1_.refs_7_ = bf16[640,1536]{1,0:T(8,128)(2,1)S(1)} collective-permute-done((bf16[640,1536]{1,0:T(8,128)(2,1)S(1)}, bf16[640,1536]{1,0:T(8,128)(2,1)S(1)}, u32[]{:S(2)}, u32[]{:S(2)}) %collective-permute-start.24) | collective-permute-done | bytes 1966112 | tf_op jit(solution)/shard_map/ppermute | solution.py:1098
  303.4 13.8 %collective-permute-done.25 = bf16[128,2560]{1,0:T(8,128)(2,1)S(1)} collective-permute-done((bf16[128,2560]{1,0:T(8,128)(2,1)S(1)}, bf16[128,2560]{1,0:T(8,128)(2,1)S(1)}, u32[]{:S(2)}, u32[]{:S(2)}) %collective-permute-start.25) | collective-permute-done | bytes 655392 | tf_op jit(solution)/shard_map/ppermute | solution.py:1063
  319.9 28.0 %collective-permute-done.29.refs_2_.refs_8_ = bf16[640,1536]{1,0:T(8,128)(2,1)S(1)} collective-permute-done((bf16[640,1536]{1,0:T(8,128)(2,1)S(1)}, bf16[640,1536]{1,0:T(8,128)(2,1)S(1)}, u32[]{:S(2)}, u32[]{:S(2)}) %collective-permute-start.29) | collective-permute-done | bytes 1966112 | tf_op jit(solution)/shard_map/ppermute | solution.py:1098
  365.4 20.8 %feed.2 = (bf16[2048,384]{1,0:T(8,128)(2,1)}, bf16[2048,768]{1,0:T(8,128)(2,1)}) custom-call(s32[4]{0:T(128)} %pad_add_fusion.1.place_ref, bf16[2048,2560]{1,0:T(8,128)(2,1)} %fusion.27.normed.refs_0_, bf16[2048,2560]{1,0:T(8,128)(2,1)} %slice_dynamic-update-slice_fusion.grad_out.refs_1_, bf16[640,1152]{1,0:T(8,128)(2,1)} %copy-done.4, ...), custom_call_target="tpu_custom_call" | custom-call | flops 12079595520 | bytes 26869760 | tf_op jit(solution)/shard_map/feed/pallas_call | solution.py:526
  386.2 23.6 %weight_grad.3 = (bf16[320,1152]{1,0:T(8,128)(2,1)}, bf16[320,1152]{1,0:T(8,128)(2,1)}, bf16[320,1152]{1,0:T(8,128)(2,1)}, bf16[320,1152]{1,0:T(8,128)(2,1)}, bf...) custom-call(s32[4]{0:T(128)} %pad_add_fusion.1.place_ref, ...), custom_call_target="tpu_custom_call" | custom-call | flops 12079595520 | bytes 25690112 | tf_op jit(solution)/shard_map/weight_grad/pallas_call | solution.py:650
  411.1 2.1 collective-permute-start.35
  413.8 24.7 %feed.3 = (bf16[2048,512]{1,0:T(8,128)(2,1)}, bf16[2048,1024]{1,0:T(8,128)(2,1)}) custom-call(s32[4]{0:T(128)} %pad_add_fusion.1.place_ref, bf16[2048,2560]{1,0:T(8,128)(2,1)} %fusion.27.normed.refs_0_, bf16[2048,2560]{1,0:T(8,128)(2,1)} %slice_dynamic-update-slice_fusion.grad_out.refs_1_, bf16[640,1536]{1,0:T(8,128)(2,1)} %copy-done.3, ...), custom_call_target="tpu_custom_call" | custom-call | flops 16106127360 | bytes 28835840 | tf_op jit(solution)/shard_map/feed/pallas_call | solution.py:526
  438.4 28.7 %spread.2 = (bf16[1024,2560]{1,0:T(8,128)(2,1)}, bf16[1024,2560]{1,0:T(8,128)(2,1)}) custom-call(s32[4]{0:T(128)} %pad_add_fusion.1.place_ref, bf16[2048,768]{1,0:T(8,128)(2,1)} %get-tuple-element.267.refs_2_.refs_0_, bf16[2048,1024]{1,0:T(8,128)(2,1)} %get-tuple-element.276.refs_1_.refs_2_, bf16[640,1152]{1,0:T(8,128)(2,1)} %copy-done.4, ...), custom_call_target="tpu_custom_call" | custom-call | flops 1 | bytes 1 | tf_op jit(solution)/shard_map/spread/pallas_call | solution.py:569
  467.2 7.8 collective-permute-done.36
  477.0 6.8 collective-permute-done.38
  487.4 2.1 fusion.16
  491.8 27.5 %weight_grad.4 = (bf16[320,1536]{1,0:T(8,128)(2,1)}, bf16[320,1536]{1,0:T(8,128)(2,1)}, bf16[320,1536]{1,0:T(8,128)(2,1)}, bf16[320,1536]{1,0:T(8,128)(2,1)}, bf...) custom-call(s32[4]{0:T(128)} %pad_add_fusion.1.place_ref, ...), custom_call_target="tpu_custom_call" | custom-call | flops 16106127360 | bytes 27262976 | tf_op jit(solution)/shard_map/weight_grad/pallas_call | solution.py:650
  519.3 18.8 %collective-permute-done.40 = bf16[2,128,2560]{2,1,0:T(8,128)(2,1)} collective-permute-done((bf16[2,128,2560]{2,1,0:T(8,128)(2,1)}, bf16[2,128,2560]{2,1,0:T(8,128)(2,1)}, u32[]{:S(2)}, u32[]{:S(2)}) %collective-permute-start.40) | collective-permute-done | bytes 1310752 | tf_op jit(solution)/shard_map/ppermute | solution.py:1059
  545.6 18.9 %spread.3 = (bf16[1024,2560]{1,0:T(8,128)(2,1)}, bf16[1024,2560]{1,0:T(8,128)(2,1)}) custom-call(s32[4]{0:T(128)} %pad_add_fusion.1.place_ref, bf16[2048,384]{1,0:T(8,128)(2,1)} %get-tuple-element.289.refs_3_.refs_0_, bf16[2048,512]{1,0:T(8,128)(2,1)} %get-tuple-element.290.refs_3_.refs_1_, bf16[640,1152]{1,0:T(8,128)(2,1)} %copy-done.4, ...), custom_call_target="tpu_custom_call" | custom-call | flops 1 | bytes 1 | tf_op jit(solution)/shard_map/spread/pallas_call | solution.py:569
  568.4 2.9 fusion.46
  571.3 8.9 collective-permute-done.46
  582.8 2.0 fusion.19
  586.3 2.0 collective-permute-start.54
  590.2 1.9 collective-permute-start.52
  592.1 38.7 %collective-permute-done.47 = bf16[2,128,2560]{2,1,0:T(8,128)(2,1)S(1)} collective-permute-done((bf16[2,128,2560]{2,1,0:T(8,128)(2,1)S(1)}, bf16[2,128,2560]{2,1,0:T(8,128)(2,1)S(1)}, u32[]{:S(2)}, u32[]{:S(2)}) %collective-permute-start.47) | collective-permute-done | bytes 1310752 | tf_op jit(solution)/shard_map/ppermute | solution.py:1063
  632.3 2.9 fusion.7
  638.8 14.3 %collective-permute-start.55 = (bf16[320,1152]{1,0:T(8,128)(2,1)}, bf16[320,1152]{1,0:T(8,128)(2,1)S(1)}, u32[]{:S(2)}, u32[]{:S(2)}) collective-permute-start(bf16[320,1152]{1,0:T(8,128)(2,1)} %get-tuple-element.313), channel_id=1, source_target_pairs={{0,16},{8,24},{16,0},{24,8},{1,17},{9,25},{17,1},{25,9},{2,18},{10... | collective-permute-start | bytes 2211848 | tf_op jit(solution)/shard_map/ppermute | solution.py:1098
  653.1 53.1 %collective-permute-done.52 = bf16[320,1536]{1,0:T(8,128)(2,1)S(1)} collective-permute-done((bf16[320,1536]{1,0:T(8,128)(2,1)S(1)}, bf16[320,1536]{1,0:T(8,128)(2,1)S(1)}, u32[]{:S(2)}, u32[]{:S(2)}) %collective-permute-start.52) | collective-permute-done | bytes 983072 | tf_op jit(solution)/shard_map/ppermute | solution.py:1098
  710.1 36.7 %attention_grad.1 = (bf16[2048,512]{1,0:T(8,128)(2,1)}, bf16[2048,256]{1,0:T(8,128)(2,1)}) custom-call(s32[4]{0:T(128)} %pad_add_fusion.1.place_ref, bf16[2048,2560]{1,0:T(8,128)(2,1)} %all-gather.5.cloned.1.call-done.grad_hidden.refs_2_, bf16[2048,768]{1,0:T(8,128)(2,1)} %get-tuple-element.233.query.key.value, ...), custom_call_target="tpu_custom_call" | custom-call | flops 30000001024 | bytes 20971520 | tf_op jit(solution)/shard_map/attention_grad/pallas_call | solution.py:364
  746.9 3.1 constant_dynamic-update-slice_fusion.1
  751.0 22.8 %projection_grad.1 = (bf16[1024,2560]{1,0:T(8,128)(2,1)}, bf16[1024,2560]{1,0:T(8,128)(2,1)}, f32[8,2560]{1,0:T(8,128)}) custom-call(s32[4]{0:T(128)} %pad_add_fusion.1.place_ref, bf16[2048,768]{1,0:T(8,128)(2,1)} %constant_dynamic-update-slice_fusion.grad_heads.refs_3_, bf16[2048,2560]{1,0:T(8,128)(2,1)} %all-gather.3.cloned.1.call-done.tokens, ...), custom_call_target="tpu_custom_call" | custom-call | flops 1 | bytes 1 | tf_op jit(solution)/shard_map/projection_grad/pallas_call | solution.py:434
  774.2 3.1 convert_add_fusion.6
  777.2 2.3 convert_add_fusion.5
  779.5 3.4 collective-permute-start.63
  782.9 2.0 collective-permute-start.64
  786.8 3.1 fusion.22
  789.9 4.2 fusion.24
  796.1 2.0 fusion.21
  798.1 32.9 %weight_grad.5 = (bf16[320,896]{1,0:T(8,128)(2,1)}, bf16[320,896]{1,0:T(8,128)(2,1)}, bf16[320,896]{1,0:T(8,128)(2,1)}, bf16[320,896]{1,0:T(8,128)(2,1)}, bf16[3...) custom-call(s32[4]{0:T(128)} %pad_add_fusion.1.place_ref, ...), custom_call_target="tpu_custom_call" | custom-call | flops 9395240960 | bytes 35127296 | tf_op jit(solution)/shard_map/weight_grad/pallas_call | solution.py:650
  831.1 5.9 collective-permute-done.62
  843.3 4.7 collective-permute-done.63.refs_6_
  848.0 24.4 %collective-permute-start.71 = (bf16[320,896]{1,0:T(8,128)(2,1)S(1)}, bf16[320,896]{1,0:T(8,128)(2,1)S(1)}, u32[]{:S(2)}, u32[]{:S(2)}) collective-permute-start(bf16[320,896]{1,0:T(8,128)(2,1)S(1)} %copy-done.54), channel_id=1, source_target_pairs={{0,8},{8,16},{16,24},{24,0},{1,9},{9,17},{17,25},{25,1},{2,10},{10... | collective-permute-start | bytes 1720328 | tf_op jit(solution)/shard_map/ppermute | solution.py:1098
  873.7 15.2 %collective-permute-done.67 = bf16[128,2560]{1,0:T(8,128)(2,1)S(1)} collective-permute-done((bf16[128,2560]{1,0:T(8,128)(2,1)S(1)}, bf16[128,2560]{1,0:T(8,128)(2,1)S(1)}, u32[]{:S(2)}, u32[]{:S(2)}) %collective-permute-start.67) | collective-permute-done | bytes 655392 | tf_op jit(solution)/shard_map/ppermute | solution.py:1063
  891.3 12.9 %collective-permute-done.66 = bf16[128,2560]{1,0:T(8,128)(2,1)S(1)} collective-permute-done((bf16[128,2560]{1,0:T(8,128)(2,1)S(1)}, bf16[128,2560]{1,0:T(8,128)(2,1)S(1)}, u32[]{:S(2)}, u32[]{:S(2)}) %collective-permute-start.66) | collective-permute-done | bytes 655392 | tf_op jit(solution)/shard_map/ppermute | solution.py:1059
  905.5 3.9 collective-permute-start.73
  912.7 62.6 %feed_update.1 = (f32[4,320,2,1792]{3,2,1,0:T(2,128)}, f32[4,320,2,1792]{3,2,1,0:T(2,128)}, f32[320,2,1792]{2,1,0:T(2,128)}, f32[320,2,1792]{2,1,0:T(2,128)}, f3...) custom-call(s32[4]{0:T(128)} %pad_add_fusion.1.place_ref, ...), custom_call_target="tpu_custom_call" | custom-call | bytes 154828800 | tf_op jit(solution)/shard_map/feed_update/pallas_call | solution.py:798
  979.1 10.8 %keyvalue_update.1 = (f32[4,320,320]{2,1,0:T(8,128)}, f32[4,320,320]{2,1,0:T(8,128)}, f32[320,320]{1,0:T(8,128)}, f32[320,320]{1,0:T(8,128)}, f32[320,320]{1,0:T...) custom-call(s32[4]{0:T(128)} %pad_add_fusion.1.place_ref, bf16[320,896]{1,0:T(8,128)(2,1)} %get-tuple-element.372.refs_0_, ...), custom_call_target="tpu_custom_call" | custom-call | bytes 9216000 | tf_op jit(solution)/shard_map/keyvalue_update/pallas_call | solution.py:940
  993.8 3.6 fusion.4
  997.4 16.0 %attention_update.1 = (f32[4,320,640]{2,1,0:T(8,128)}, f32[4,320,640]{2,1,0:T(8,128)}, f32[320,640]{1,0:T(8,128)}, f32[320,640]{1,0:T(8,128)}, f32[320,640]{1,0:...) custom-call(s32[4]{0:T(128)} %pad_add_fusion.1.place_ref, ...), custom_call_target="tpu_custom_call" | custom-call | bytes 36864000 | tf_op jit(solution)/shard_map/attention_update/pallas_call | solution.py:873
  (365 shorter events, 140.6 us)
Async XLA Ops:
  7.2 103.9 %all-gather.3.cloned.1.call-start = ((), (), s32[]{:S(2)}) async-start(), calls=%async_computation | async-start | bytes 11796480 | tf_op jit(solution)/shard_map/all_gather | solution.py:1182
  8.0 699.5 %all-gather.5.cloned.1.call-start = ((), (), s32[]{:S(2)}) async-start(), calls=%async_computation.1 | async-start | bytes 11796480 | tf_op jit(solution)/shard_map/all_gather | solution.py:1274
  27.7 19.6 %collective-permute-start.1 = (bf16[640,512]{1,0:T(8,128)(2,1)S(1)}, bf16[640,512]{1,0:T(8,128)(2,1)S(1)}, u32[]{:S(2)}, u32[]{:S(2)}) collective-permute-start(bf16[640,512]{1,0:T(8,128)(2,1)S(1)} %pad_maximum_fusion.13.refs_0_), channel_id=1, source_target_pairs={{0,8},{8,16},{16,24},{24,0},{1,9},{9,17},{17,25},{25,1},{2,10},{10... | collective-permute-start | bytes 1966088 | tf_op jit(solution)/shard_map/ppermute | solution.py:1098
  39.1 25.4 %collective-permute-start.6 = (bf16[320,1152]{1,0:T(8,128)(2,1)}, bf16[320,1152]{1,0:T(8,128)(2,1)S(1)}, u32[]{:S(2)}, u32[]{:S(2)}) collective-permute-start(bf16[320,1152]{1,0:T(8,128)(2,1)} %get-tuple-element.229), channel_id=1, source_target_pairs={{0,4},{4,0},{1,5},{5,1},{2,6},{6,2},{3,7},{7,3},{8,12},{12,8},{9,1... | collective-permute-start | bytes 2211848 | tf_op jit(solution)/shard_map/ppermute | solution.py:1059
  43.2 23.0 %collective-permute-start.3 = (bf16[640,512]{1,0:T(8,128)(2,1)S(1)}, bf16[640,512]{1,0:T(8,128)(2,1)S(1)}, u32[]{:S(2)}, u32[]{:S(2)}) collective-permute-start(bf16[640,512]{1,0:T(8,128)(2,1)S(1)} %pad_maximum_fusion.13.refs_0_), channel_id=1, source_target_pairs={{0,24},{8,0},{16,8},{24,16},{1,25},{9,1},{17,9},{25,17},{2,26},{10... | collective-permute-start | bytes 1966088 | tf_op jit(solution)/shard_map/ppermute | solution.py:1098
  45.5 65.7 %collective-permute-start.2 = (bf16[640,512]{1,0:T(8,128)(2,1)S(1)}, bf16[640,512]{1,0:T(8,128)(2,1)}, u32[]{:S(2)}, u32[]{:S(2)}) collective-permute-start(bf16[640,512]{1,0:T(8,128)(2,1)S(1)} %pad_maximum_fusion.13.refs_0_), channel_id=1, source_target_pairs={{0,16},{8,24},{16,0},{24,8},{1,17},{9,25},{17,1},{25,9},{2,18},{10... | collective-permute-start | bytes 1966088 | tf_op jit(solution)/shard_map/ppermute | solution.py:1098
  47.2 92.2 %collective-permute-start.11 = (bf16[640,320]{1,0:T(8,128)(2,1)}, bf16[640,320]{1,0:T(8,128)(2,1)}, u32[]{:S(2)}, u32[]{:S(2)}) collective-permute-start(bf16[640,320]{1,0:T(8,128)(2,1)} %pad_maximum_fusion.14.refs_0_), channel_id=1, source_target_pairs={{0,24},{8,0},{16,8},{24,16},{1,25},{9,1},{17,9},{25,17},{2,26},{10... | collective-permute-start | bytes 1228808 | tf_op jit(solution)/shard_map/ppermute | solution.py:1098
  48.6 91.5 %collective-permute-start.10 = (bf16[640,320]{1,0:T(8,128)(2,1)}, bf16[640,320]{1,0:T(8,128)(2,1)}, u32[]{:S(2)}, u32[]{:S(2)}) collective-permute-start(bf16[640,320]{1,0:T(8,128)(2,1)} %pad_maximum_fusion.14.refs_0_), channel_id=1, source_target_pairs={{0,16},{8,24},{16,0},{24,8},{1,17},{9,25},{17,1},{25,9},{2,18},{10... | collective-permute-start | bytes 1228808 | tf_op jit(solution)/shard_map/ppermute | solution.py:1098
  64.5 75.6 %collective-permute-start.9 = (bf16[640,320]{1,0:T(8,128)(2,1)}, bf16[640,320]{1,0:T(8,128)(2,1)}, u32[]{:S(2)}, u32[]{:S(2)}) collective-permute-start(bf16[640,320]{1,0:T(8,128)(2,1)} %pad_maximum_fusion.14.refs_0_), channel_id=1, source_target_pairs={{0,8},{8,16},{16,24},{24,0},{1,9},{9,17},{17,25},{25,1},{2,10},{10... | collective-permute-start | bytes 1228808 | tf_op jit(solution)/shard_map/ppermute | solution.py:1098
  112.4 24.2 %collective-permute-start.8 = (bf16[128,2560]{1,0:T(8,128)(2,1)}, bf16[128,2560]{1,0:T(8,128)(2,1)S(1)}, u32[]{:S(2)}, u32[]{:S(2)}) collective-permute-start(bf16[128,2560]{1,0:T(8,128)(2,1)} %get-tuple-element.445), channel_id=1, source_target_pairs={{0,4},{4,0},{1,5},{5,1},{2,6},{6,2},{3,7},{7,3},{8,12},{12,8},{9,1... | collective-permute-start | bytes 1966088 | tf_op jit(solution)/shard_map/ppermute | solution.py:1059
  112.9 21.6 %collective-permute-start.7 = (bf16[128,2560]{1,0:T(8,128)(2,1)S(1)}, bf16[128,2560]{1,0:T(8,128)(2,1)S(1)}, u32[]{:S(2)}, u32[]{:S(2)}) collective-permute-start(bf16[128,2560]{1,0:T(8,128)(2,1)S(1)} %get-tuple-element.446), channel_id=1, source_target_pairs={{0,2},{1,3},{2,0},{3,1},{4,6},{5,7},{6,4},{7,5},{8,10},{9,11},{10,... | collective-permute-start | bytes 1966088 | tf_op jit(solution)/shard_map/ppermute | solution.py:1063
  134.6 37.6 %collective-permute-start.14 = (bf16[640,1152]{1,0:T(8,128)(2,1)S(1)}, bf16[640,1152]{1,0:T(8,128)(2,1)S(1)}, u32[]{:S(2)}, u32[]{:S(2)}) collective-permute-start(bf16[640,1152]{1,0:T(8,128)(2,1)S(1)} %pad_maximum_fusion.8.refs_0_.refs_2_), channel_id=1, source_target_pairs={{0,8},{8,16},{16,24},{24,0},{1,9},{9,17},{17,25},{25,1},{2,10},{10... | collective-permute-start | bytes 4423688 | tf_op jit(solution)/shard_map/ppermute | solution.py:1098
  136.6 35.5 %collective-permute-start.12 = (bf16[2,128,2560]{2,1,0:T(8,128)(2,1)S(1)}, bf16[2,128,2560]{2,1,0:T(8,128)(2,1)}, u32[]{:S(2)}, u32[]{:S(2)}) collective-permute-start(bf16[2,128,2560]{2,1,0:T(8,128)(2,1)S(1)} %pad_maximum_fusion.9), channel_id=1, source_target_pairs={{0,4},{4,0},{1,5},{5,1},{2,6},{6,2},{3,7},{7,3},{8,12},{12,8},{9,1... | collective-permute-start | bytes 3932168 | tf_op jit(solution)/shard_map/ppermute | solution.py:1059
  139.5 32.7 %collective-permute-start.13 = (bf16[2,128,2560]{2,1,0:T(8,128)(2,1)S(1)}, bf16[2,128,2560]{2,1,0:T(8,128)(2,1)}, u32[]{:S(2)}, u32[]{:S(2)}) collective-permute-start(bf16[2,128,2560]{2,1,0:T(8,128)(2,1)S(1)} %pad_maximum_fusion.10), channel_id=1, source_target_pairs={{0,2},{1,3},{2,0},{3,1},{4,6},{5,7},{6,4},{7,5},{8,10},{9,11},{10,... | collective-permute-start | bytes 3932168 | tf_op jit(solution)/shard_map/ppermute | solution.py:1063
  172.2 36.5 %collective-permute-start.16 = (bf16[640,1152]{1,0:T(8,128)(2,1)S(1)}, bf16[640,1152]{1,0:T(8,128)(2,1)S(1)}, u32[]{:S(2)}, u32[]{:S(2)}) collective-permute-start(bf16[640,1152]{1,0:T(8,128)(2,1)S(1)} %collective-permute-done.14.refs_1_.refs_3_), channel_id=1, source_target_pairs={{0,8},{8,16},{16,24},{24,0},{1,9},{9,17},{17,25},{25,1},{2,10},{10... | collective-permute-start | bytes 4423688 | tf_op jit(solution)/shard_map/ppermute | solution.py:1098
  215.4 53.0 %collective-permute-start.20 = (bf16[1024,2560]{1,0:T(8,128)(2,1)S(1)}, bf16[1024,2560]{1,0:T(8,128)(2,1)S(1)}, u32[]{:S(2)}, u32[]{:S(2)}) collective-permute-start(bf16[1024,2560]{1,0:T(8,128)(2,1)S(1)} %bitcast_dynamic-update-slice_fusion.9), channel_id=1, source_target_pairs={{0,1},{1,0},{2,3},{3,2},{4,5},{5,4},{6,7},{7,6},{8,9},{9,8},{10,11... | collective-permute-start | bytes 15728648 | tf_op jit(solution)/shard_map/ppermute | solution.py:1063
  215.5 24.6 %collective-permute-start.23 = (bf16[320,1536]{1,0:T(8,128)(2,1)S(1)}, bf16[320,1536]{1,0:T(8,128)(2,1)S(1)}, u32[]{:S(2)}, u32[]{:S(2)}) collective-permute-start(bf16[320,1536]{1,0:T(8,128)(2,1)S(1)} %copy-done.46), channel_id=1, source_target_pairs={{0,4},{4,0},{1,5},{5,1},{2,6},{6,2},{3,7},{7,3},{8,12},{12,8},{9,1... | collective-permute-start | bytes 2949128 | tf_op jit(solution)/shard_map/ppermute | solution.py:1059
  216.3 36.1 %collective-permute-start.19 = (bf16[640,1152]{1,0:T(8,128)(2,1)S(1)}, bf16[640,1152]{1,0:T(8,128)(2,1)S(1)}, u32[]{:S(2)}, u32[]{:S(2)}) collective-permute-start(bf16[640,1152]{1,0:T(8,128)(2,1)S(1)} %collective-permute-done.16.refs_2_.refs_4_), channel_id=1, source_target_pairs={{0,8},{8,16},{16,24},{24,0},{1,9},{9,17},{17,25},{25,1},{2,10},{10... | collective-permute-start | bytes 4423688 | tf_op jit(solution)/shard_map/ppermute | solution.py:1098
  216.3 36.4 %collective-permute-start.17 = (bf16[2,128,2560]{2,1,0:T(8,128)(2,1)S(1)}, bf16[2,128,2560]{2,1,0:T(8,128)(2,1)S(1)}, u32[]{:S(2)}, u32[]{:S(2)}) collective-permute-start(bf16[2,128,2560]{2,1,0:T(8,128)(2,1)S(1)} %fusion.10), channel_id=1, source_target_pairs={{0,2},{1,3},{2,0},{3,1},{4,6},{5,7},{6,4},{7,5},{8,10},{9,11},{10,... | collective-permute-start | bytes 3932168 | tf_op jit(solution)/shard_map/ppermute | solution.py:1063
  217.9 49.9 %collective-permute-start.18 = (bf16[2,128,2560]{2,1,0:T(8,128)(2,1)S(1)}, bf16[2,128,2560]{2,1,0:T(8,128)(2,1)S(1)}, u32[]{:S(2)}, u32[]{:S(2)}) collective-permute-start(bf16[2,128,2560]{2,1,0:T(8,128)(2,1)S(1)} %get-tuple-element.242), channel_id=1, source_target_pairs={{0,4},{4,0},{1,5},{5,1},{2,6},{6,2},{3,7},{7,3},{8,12},{12,8},{9,1... | collective-permute-start | bytes 3932168 | tf_op jit(solution)/shard_map/ppermute | solution.py:1059
  252.5 46.1 %collective-permute-start.24 = (bf16[640,1536]{1,0:T(8,128)(2,1)S(1)}, bf16[640,1536]{1,0:T(8,128)(2,1)S(1)}, u32[]{:S(2)}, u32[]{:S(2)}) collective-permute-start(bf16[640,1536]{1,0:T(8,128)(2,1)S(1)} %pad_maximum_fusion.2.refs_0_.refs_6_), channel_id=1, source_target_pairs={{0,8},{8,16},{16,24},{24,0},{1,9},{9,17},{17,25},{25,1},{2,10},{10... | collective-permute-start | bytes 5898248 | tf_op jit(solution)/shard_map/ppermute | solution.py:1098
  303.4 44.5 %collective-permute-start.29 = (bf16[640,1536]{1,0:T(8,128)(2,1)S(1)}, bf16[640,1536]{1,0:T(8,128)(2,1)S(1)}, u32[]{:S(2)}, u32[]{:S(2)}) collective-permute-start(bf16[640,1536]{1,0:T(8,128)(2,1)S(1)} %collective-permute-done.24.refs_1_.refs_7_), channel_id=1, source_target_pairs={{0,8},{8,16},{16,24},{24,0},{1,9},{9,17},{17,25},{25,1},{2,10},{10... | collective-permute-start | bytes 5898248 | tf_op jit(solution)/shard_map/ppermute | solution.py:1098
  317.3 30.5 %collective-permute-start.27 = (bf16[2,128,2560]{2,1,0:T(8,128)(2,1)S(1)}, bf16[2,128,2560]{2,1,0:T(8,128)(2,1)S(1)}, u32[]{:S(2)}, u32[]{:S(2)}) collective-permute-start(bf16[2,128,2560]{2,1,0:T(8,128)(2,1)S(1)} %pad_maximum_fusion.11), channel_id=1, source_target_pairs={{0,4},{4,0},{1,5},{5,1},{2,6},{6,2},{3,7},{7,3},{8,12},{12,8},{9,1... | collective-permute-start | bytes 3932168 | tf_op jit(solution)/shard_map/ppermute | solution.py:1059
  318.3 29.6 %collective-permute-start.28 = (bf16[2,128,2560]{2,1,0:T(8,128)(2,1)S(1)}, bf16[2,128,2560]{2,1,0:T(8,128)(2,1)S(1)}, u32[]{:S(2)}, u32[]{:S(2)}) collective-permute-start(bf16[2,128,2560]{2,1,0:T(8,128)(2,1)S(1)} %pad_maximum_fusion.12), channel_id=1, source_target_pairs={{0,2},{1,3},{2,0},{3,1},{4,6},{5,7},{6,4},{7,5},{8,10},{9,11},{10,... | collective-permute-start | bytes 3932168 | tf_op jit(solution)/shard_map/ppermute | solution.py:1063
  349.2 64.6 %collective-permute-start.33 = (bf16[640,1536]{1,0:T(8,128)(2,1)S(1)}, bf16[640,1536]{1,0:T(8,128)(2,1)}, u32[]{:S(2)}, u32[]{:S(2)}) collective-permute-start(bf16[640,1536]{1,0:T(8,128)(2,1)S(1)} %collective-permute-done.29.refs_2_.refs_8_), channel_id=1, source_target_pairs={{0,8},{8,16},{16,24},{24,0},{1,9},{9,17},{17,25},{25,1},{2,10},{10... | collective-permute-start | bytes 5898248 | tf_op jit(solution)/shard_map/ppermute | solution.py:1098
  409.8 28.6 %collective-permute-start.34 = (bf16[320,1152]{1,0:T(8,128)(2,1)}, bf16[320,1152]{1,0:T(8,128)(2,1)S(1)}, u32[]{:S(2)}, u32[]{:S(2)}) collective-permute-start(bf16[320,1152]{1,0:T(8,128)(2,1)} %get-tuple-element.263), channel_id=1, source_target_pairs={{0,4},{4,0},{1,5},{5,1},{2,6},{6,2},{3,7},{7,3},{8,12},{12,8},{9,1... | collective-permute-start | bytes 2211848 | tf_op jit(solution)/shard_map/ppermute | solution.py:1059
  411.1 56.1 %collective-permute-start.35 = (bf16[320,1152]{1,0:T(8,128)(2,1)}, bf16[320,1152]{1,0:T(8,128)(2,1)}, u32[]{:S(2)}, u32[]{:S(2)}) collective-permute-start(bf16[320,1152]{1,0:T(8,128)(2,1)} %get-tuple-element.271), channel_id=1, source_target_pairs={{0,24},{8,0},{16,8},{24,16},{1,25},{9,1},{17,9},{25,17},{2,26},{10... | collective-permute-start | bytes 2211848 | tf_op jit(solution)/shard_map/ppermute | solution.py:1098
  413.2 61.7 %collective-permute-start.36 = (bf16[320,1152]{1,0:T(8,128)(2,1)}, bf16[320,1152]{1,0:T(8,128)(2,1)}, u32[]{:S(2)}, u32[]{:S(2)}) collective-permute-start(bf16[320,1152]{1,0:T(8,128)(2,1)} %get-tuple-element.272), channel_id=1, source_target_pairs={{0,16},{8,24},{16,0},{24,8},{1,17},{9,25},{17,1},{25,9},{2,18},{10... | collective-permute-start | bytes 2211848 | tf_op jit(solution)/shard_map/ppermute | solution.py:1098
  413.2 61.7 %collective-permute-start.37 = (bf16[320,1152]{1,0:T(8,128)(2,1)}, bf16[320,1152]{1,0:T(8,128)(2,1)}, u32[]{:S(2)}, u32[]{:S(2)}) collective-permute-start(bf16[320,1152]{1,0:T(8,128)(2,1)} %get-tuple-element.273), channel_id=1, source_target_pairs={{0,8},{8,16},{16,24},{24,0},{1,9},{9,17},{17,25},{25,1},{2,10},{10... | collective-permute-start | bytes 2211848 | tf_op jit(solution)/shard_map/ppermute | solution.py:1098
  474.9 66.5 %collective-permute-start.41 = (bf16[320,1152]{1,0:T(8,128)(2,1)}, bf16[320,1152]{1,0:T(8,128)(2,1)S(1)}, u32[]{:S(2)}, u32[]{:S(2)}) collective-permute-start(bf16[320,1152]{1,0:T(8,128)(2,1)} %collective-permute-done.35), channel_id=1, source_target_pairs={{0,4},{4,0},{1,5},{5,1},{2,6},{6,2},{3,7},{7,3},{8,12},{12,8},{9,1... | collective-permute-start | bytes 2211848 | tf_op jit(solution)/shard_map/ppermute | solution.py:1059
  475.7 65.7 %collective-permute-start.42 = (bf16[320,1152]{1,0:T(8,128)(2,1)}, bf16[320,1152]{1,0:T(8,128)(2,1)}, u32[]{:S(2)}, u32[]{:S(2)}) collective-permute-start(bf16[320,1152]{1,0:T(8,128)(2,1)} %collective-permute-done.36), channel_id=1, source_target_pairs={{0,4},{4,0},{1,5},{5,1},{2,6},{6,2},{3,7},{7,3},{8,12},{12,8},{9,1... | collective-permute-start | bytes 2211848 | tf_op jit(solution)/shard_map/ppermute | solution.py:1059
  477.0 64.5 %collective-permute-start.43 = (bf16[320,1152]{1,0:T(8,128)(2,1)}, bf16[320,1152]{1,0:T(8,128)(2,1)}, u32[]{:S(2)}, u32[]{:S(2)}) collective-permute-start(bf16[320,1152]{1,0:T(8,128)(2,1)} %get-tuple-element.286), channel_id=1, source_target_pairs={{0,24},{8,0},{16,8},{24,16},{1,25},{9,1},{17,9},{25,17},{2,26},{10... | collective-permute-start | bytes 2211848 | tf_op jit(solution)/shard_map/ppermute | solution.py:1098
  489.5 48.5 %collective-permute-start.40 = (bf16[2,128,2560]{2,1,0:T(8,128)(2,1)}, bf16[2,128,2560]{2,1,0:T(8,128)(2,1)}, u32[]{:S(2)}, u32[]{:S(2)}) collective-permute-start(bf16[2,128,2560]{2,1,0:T(8,128)(2,1)} %get-tuple-element.428), channel_id=1, source_target_pairs={{0,4},{4,0},{1,5},{5,1},{2,6},{6,2},{3,7},{7,3},{8,12},{12,8},{9,1... | collective-permute-start | bytes 3932168 | tf_op jit(solution)/shard_map/ppermute | solution.py:1059
  490.3 47.7 %collective-permute-start.39 = (bf16[2,128,2560]{2,1,0:T(8,128)(2,1)S(1)}, bf16[2,128,2560]{2,1,0:T(8,128)(2,1)}, u32[]{:S(2)}, u32[]{:S(2)}) collective-permute-start(bf16[2,128,2560]{2,1,0:T(8,128)(2,1)S(1)} %fusion.14), channel_id=1, source_target_pairs={{0,2},{1,3},{2,0},{3,1},{4,6},{5,7},{6,4},{7,5},{8,10},{9,11},{10,... | collective-permute-start | bytes 3932168 | tf_op jit(solution)/shard_map/ppermute | solution.py:1063
  543.4 21.1 %collective-permute-start.45 = (bf16[128,2560]{1,0:T(8,128)(2,1)}, bf16[128,2560]{1,0:T(8,128)(2,1)}, u32[]{:S(2)}, u32[]{:S(2)}) collective-permute-start(bf16[128,2560]{1,0:T(8,128)(2,1)} %slice_bitcast_fusion.22), channel_id=1, source_target_pairs={{0,2},{1,3},{2,0},{3,1},{4,6},{5,7},{6,4},{7,5},{8,10},{9,11},{10,... | collective-permute-start | bytes 1966088 | tf_op jit(solution)/shard_map/ppermute | solution.py:1063
  544.8 19.7 %collective-permute-start.44 = (bf16[128,2560]{1,0:T(8,128)(2,1)}, bf16[128,2560]{1,0:T(8,128)(2,1)}, u32[]{:S(2)}, u32[]{:S(2)}) collective-permute-start(bf16[128,2560]{1,0:T(8,128)(2,1)} %slice_bitcast_fusion.23), channel_id=1, source_target_pairs={{0,4},{4,0},{1,5},{5,1},{2,6},{6,2},{3,7},{7,3},{8,12},{12,8},{9,1... | collective-permute-start | bytes 1966088 | tf_op jit(solution)/shard_map/ppermute | solution.py:1059
  582.0 48.8 %collective-permute-start.47 = (bf16[2,128,2560]{2,1,0:T(8,128)(2,1)S(1)}, bf16[2,128,2560]{2,1,0:T(8,128)(2,1)S(1)}, u32[]{:S(2)}, u32[]{:S(2)}) collective-permute-start(bf16[2,128,2560]{2,1,0:T(8,128)(2,1)S(1)} %fusion.18), channel_id=1, source_target_pairs={{0,2},{1,3},{2,0},{3,1},{4,6},{5,7},{6,4},{7,5},{8,10},{9,11},{10,... | collective-permute-start | bytes 3932168 | tf_op jit(solution)/shard_map/ppermute | solution.py:1063
  584.8 47.5 %collective-permute-start.48 = (bf16[2,128,2560]{2,1,0:T(8,128)(2,1)S(1)}, bf16[2,128,2560]{2,1,0:T(8,128)(2,1)S(1)}, u32[]{:S(2)}, u32[]{:S(2)}) collective-permute-start(bf16[2,128,2560]{2,1,0:T(8,128)(2,1)S(1)} %fusion.19), channel_id=1, source_target_pairs={{0,4},{4,0},{1,5},{5,1},{2,6},{6,2},{3,7},{7,3},{8,12},{12,8},{9,1... | collective-permute-start | bytes 3932168 | tf_op jit(solution)/shard_map/ppermute | solution.py:1059
  586.3 51.8 %collective-permute-start.54 = (bf16[320,1152]{1,0:T(8,128)(2,1)S(1)}, bf16[320,1152]{1,0:T(8,128)(2,1)}, u32[]{:S(2)}, u32[]{:S(2)}) collective-permute-start(bf16[320,1152]{1,0:T(8,128)(2,1)S(1)} %copy-done.51), channel_id=1, source_target_pairs={{0,8},{8,16},{16,24},{24,0},{1,9},{9,17},{17,25},{25,1},{2,10},{10... | collective-permute-start | bytes 2211848 | tf_op jit(solution)/shard_map/ppermute | solution.py:1098
  588.3 50.5 %collective-permute-start.51 = (bf16[320,1536]{1,0:T(8,128)(2,1)S(1)}, bf16[320,1536]{1,0:T(8,128)(2,1)S(1)}, u32[]{:S(2)}, u32[]{:S(2)}) collective-permute-start(bf16[320,1536]{1,0:T(8,128)(2,1)S(1)} %copy-done.49), channel_id=1, source_target_pairs={{0,24},{8,0},{16,8},{24,16},{1,25},{9,1},{17,9},{25,17},{2,26},{10... | collective-permute-start | bytes 2949128 | tf_op jit(solution)/shard_map/ppermute | solution.py:1098
  590.2 116.0 %collective-permute-start.52 = (bf16[320,1536]{1,0:T(8,128)(2,1)S(1)}, bf16[320,1536]{1,0:T(8,128)(2,1)S(1)}, u32[]{:S(2)}, u32[]{:S(2)}) collective-permute-start(bf16[320,1536]{1,0:T(8,128)(2,1)S(1)} %copy-done.48), channel_id=1, source_target_pairs={{0,16},{8,24},{16,0},{24,8},{1,17},{9,25},{17,1},{25,9},{2,18},{10... | collective-permute-start | bytes 2949128 | tf_op jit(solution)/shard_map/ppermute | solution.py:1098
  630.8 75.4 %collective-permute-start.53 = (bf16[320,1536]{1,0:T(8,128)(2,1)S(1)}, bf16[320,1536]{1,0:T(8,128)(2,1)S(1)}, u32[]{:S(2)}, u32[]{:S(2)}) collective-permute-start(bf16[320,1536]{1,0:T(8,128)(2,1)S(1)} %copy-done.47), channel_id=1, source_target_pairs={{0,8},{8,16},{16,24},{24,0},{1,9},{9,17},{17,25},{25,1},{2,10},{10... | collective-permute-start | bytes 2949128 | tf_op jit(solution)/shard_map/ppermute | solution.py:1098
  636.7 69.5 %collective-permute-start.49 = (bf16[128,2560]{1,0:T(8,128)(2,1)S(1)}, bf16[128,2560]{1,0:T(8,128)(2,1)}, u32[]{:S(2)}, u32[]{:S(2)}) collective-permute-start(bf16[128,2560]{1,0:T(8,128)(2,1)S(1)} %slice_bitcast_fusion.10), channel_id=1, source_target_pairs={{0,4},{4,0},{1,5},{5,1},{2,6},{6,2},{3,7},{7,3},{8,12},{12,8},{9,1... | collective-permute-start | bytes 1966088 | tf_op jit(solution)/shard_map/ppermute | solution.py:1059
  638.1 69.3 %collective-permute-start.50 = (bf16[128,2560]{1,0:T(8,128)(2,1)S(1)}, bf16[128,2560]{1,0:T(8,128)(2,1)}, u32[]{:S(2)}, u32[]{:S(2)}) collective-permute-start(bf16[128,2560]{1,0:T(8,128)(2,1)S(1)} %slice_bitcast_fusion.9), channel_id=1, source_target_pairs={{0,2},{1,3},{2,0},{3,1},{4,6},{5,7},{6,4},{7,5},{8,10},{9,11},{10,... | collective-permute-start | bytes 1966088 | tf_op jit(solution)/shard_map/ppermute | solution.py:1063
  638.8 135.1 %collective-permute-start.55 = (bf16[320,1152]{1,0:T(8,128)(2,1)}, bf16[320,1152]{1,0:T(8,128)(2,1)S(1)}, u32[]{:S(2)}, u32[]{:S(2)}) collective-permute-start(bf16[320,1152]{1,0:T(8,128)(2,1)} %get-tuple-element.313), channel_id=1, source_target_pairs={{0,16},{8,24},{16,0},{24,8},{1,17},{9,25},{17,1},{25,9},{2,18},{10... | collective-permute-start | bytes 2211848 | tf_op jit(solution)/shard_map/ppermute | solution.py:1098
  707.4 66.5 %collective-permute-start.56 = (bf16[320,1152]{1,0:T(8,128)(2,1)}, bf16[320,1152]{1,0:T(8,128)(2,1)}, u32[]{:S(2)}, u32[]{:S(2)}) collective-permute-start(bf16[320,1152]{1,0:T(8,128)(2,1)} %collective-permute-done.37), channel_id=1, source_target_pairs={{0,4},{4,0},{1,5},{5,1},{2,6},{6,2},{3,7},{7,3},{8,12},{12,8},{9,1... | collective-permute-start | bytes 2211848 | tf_op jit(solution)/shard_map/ppermute | solution.py:1059
  708.1 65.8 %collective-permute-start.57 = (bf16[320,1536]{1,0:T(8,128)(2,1)}, bf16[320,1536]{1,0:T(8,128)(2,1)S(1)}, u32[]{:S(2)}, u32[]{:S(2)}) collective-permute-start(bf16[320,1536]{1,0:T(8,128)(2,1)} %get-tuple-element.315), channel_id=1, source_target_pairs={{0,4},{4,0},{1,5},{5,1},{2,6},{6,2},{3,7},{7,3},{8,12},{12,8},{9,1... | collective-permute-start | bytes 2949128 | tf_op jit(solution)/shard_map/ppermute | solution.py:1059
  709.5 64.5 %collective-permute-start.58 = (bf16[320,1536]{1,0:T(8,128)(2,1)}, bf16[320,1536]{1,0:T(8,128)(2,1)}, u32[]{:S(2)}, u32[]{:S(2)}) collective-permute-start(bf16[320,1536]{1,0:T(8,128)(2,1)} %copy-done.50), channel_id=1, source_target_pairs={{0,4},{4,0},{1,5},{5,1},{2,6},{6,2},{3,7},{7,3},{8,12},{12,8},{9,1... | collective-permute-start | bytes 2949128 | tf_op jit(solution)/shard_map/ppermute | solution.py:1059
  710.1 63.8 %collective-permute-start.59 = (bf16[320,1536]{1,0:T(8,128)(2,1)}, bf16[320,1536]{1,0:T(8,128)(2,1)}, u32[]{:S(2)}, u32[]{:S(2)}) collective-permute-start(bf16[320,1536]{1,0:T(8,128)(2,1)} %get-tuple-element.321), channel_id=1, source_target_pairs={{0,24},{8,0},{16,8},{24,16},{1,25},{9,1},{17,9},{25,17},{2,26},{10... | collective-permute-start | bytes 2949128 | tf_op jit(solution)/shard_map/ppermute | solution.py:1098
  779.5 68.5 %collective-permute-start.63 = (bf16[320,1536]{1,0:T(8,128)(2,1)}, bf16[320,1536]{1,0:T(8,128)(2,1)}, u32[]{:S(2)}, u32[]{:S(2)}) collective-permute-start(bf16[320,1536]{1,0:T(8,128)(2,1)} %get-tuple-element.332), channel_id=1, source_target_pairs={{0,16},{8,24},{16,0},{24,8},{1,17},{9,25},{17,1},{25,9},{2,18},{10... | collective-permute-start | bytes 2949128 | tf_op jit(solution)/shard_map/ppermute | solution.py:1098
  782.9 65.1 %collective-permute-start.64 = (bf16[320,1536]{1,0:T(8,128)(2,1)}, bf16[320,1536]{1,0:T(8,128)(2,1)}, u32[]{:S(2)}, u32[]{:S(2)}) collective-permute-start(bf16[320,1536]{1,0:T(8,128)(2,1)} %get-tuple-element.333), channel_id=1, source_target_pairs={{0,8},{8,16},{16,24},{24,0},{1,9},{9,17},{17,25},{25,1},{2,10},{10... | collective-permute-start | bytes 2949128 | tf_op jit(solution)/shard_map/ppermute | solution.py:1098
  785.7 86.8 %collective-permute-start.65 = (bf16[320,1536]{1,0:T(8,128)(2,1)}, bf16[320,1536]{1,0:T(8,128)(2,1)}, u32[]{:S(2)}, u32[]{:S(2)}) collective-permute-start(bf16[320,1536]{1,0:T(8,128)(2,1)} %copy-done.45), channel_id=1, source_target_pairs={{0,4},{4,0},{1,5},{5,1},{2,6},{6,2},{3,7},{7,3},{8,12},{12,8},{9,1... | collective-permute-start | bytes 2949128 | tf_op jit(solution)/shard_map/ppermute | solution.py:1059
  794.1 42.9 %collective-permute-start.62 = (bf16[2,128,2560]{2,1,0:T(8,128)(2,1)}, bf16[2,128,2560]{2,1,0:T(8,128)(2,1)}, u32[]{:S(2)}, u32[]{:S(2)}) collective-permute-start(bf16[2,128,2560]{2,1,0:T(8,128)(2,1)} %get-tuple-element.424), channel_id=1, source_target_pairs={{0,4},{4,0},{1,5},{5,1},{2,6},{6,2},{3,7},{7,3},{8,12},{12,8},{9,1... | collective-permute-start | bytes 3932168 | tf_op jit(solution)/shard_map/ppermute | solution.py:1059
  795.0 43.1 %collective-permute-start.61 = (bf16[2,128,2560]{2,1,0:T(8,128)(2,1)}, bf16[2,128,2560]{2,1,0:T(8,128)(2,1)}, u32[]{:S(2)}, u32[]{:S(2)}) collective-permute-start(bf16[2,128,2560]{2,1,0:T(8,128)(2,1)} %fusion.22), channel_id=1, source_target_pairs={{0,2},{1,3},{2,0},{3,1},{4,6},{5,7},{6,4},{7,5},{8,10},{9,11},{10,... | collective-permute-start | bytes 3932168 | tf_op jit(solution)/shard_map/ppermute | solution.py:1063
  837.0 67.3 %collective-permute-start.68 = (bf16[320,1536]{1,0:T(8,128)(2,1)}, bf16[320,1536]{1,0:T(8,128)(2,1)S(1)}, u32[]{:S(2)}, u32[]{:S(2)}) collective-permute-start(bf16[320,1536]{1,0:T(8,128)(2,1)} %copy-done.44), channel_id=1, source_target_pairs={{0,4},{4,0},{1,5},{5,1},{2,6},{6,2},{3,7},{7,3},{8,12},{12,8},{9,1... | collective-permute-start | bytes 2949128 | tf_op jit(solution)/shard_map/ppermute | solution.py:1059
  838.1 66.2 %collective-permute-start.69 = (bf16[320,896]{1,0:T(8,128)(2,1)}, bf16[320,896]{1,0:T(8,128)(2,1)S(1)}, u32[]{:S(2)}, u32[]{:S(2)}) collective-permute-start(bf16[320,896]{1,0:T(8,128)(2,1)} %get-tuple-element.344), channel_id=1, source_target_pairs={{0,24},{8,0},{16,8},{24,16},{1,25},{9,1},{17,9},{25,17},{2,26},{10... | collective-permute-start | bytes 1720328 | tf_op jit(solution)/shard_map/ppermute | solution.py:1098
  848.0 56.2 %collective-permute-start.70 = (bf16[320,896]{1,0:T(8,128)(2,1)S(1)}, bf16[320,896]{1,0:T(8,128)(2,1)S(1)}, u32[]{:S(2)}, u32[]{:S(2)}) collective-permute-start(bf16[320,896]{1,0:T(8,128)(2,1)S(1)} %copy-done.55), channel_id=1, source_target_pairs={{0,16},{8,24},{16,0},{24,8},{1,17},{9,25},{17,1},{25,9},{2,18},{10... | collective-permute-start | bytes 1720328 | tf_op jit(solution)/shard_map/ppermute | solution.py:1098
  848.0 56.2 %collective-permute-start.71 = (bf16[320,896]{1,0:T(8,128)(2,1)S(1)}, bf16[320,896]{1,0:T(8,128)(2,1)S(1)}, u32[]{:S(2)}, u32[]{:S(2)}) collective-permute-start(bf16[320,896]{1,0:T(8,128)(2,1)S(1)} %copy-done.54), channel_id=1, source_target_pairs={{0,8},{8,16},{16,24},{24,0},{1,9},{9,17},{17,25},{25,1},{2,10},{10... | collective-permute-start | bytes 1720328 | tf_op jit(solution)/shard_map/ppermute | solution.py:1098
  904.3 73.5 %collective-permute-start.75 = (bf16[320,896]{1,0:T(8,128)(2,1)}, bf16[320,896]{1,0:T(8,128)(2,1)S(1)}, u32[]{:S(2)}, u32[]{:S(2)}) collective-permute-start(bf16[320,896]{1,0:T(8,128)(2,1)} %get-tuple-element.347), channel_id=1, source_target_pairs={{0,4},{4,0},{1,5},{5,1},{2,6},{6,2},{3,7},{7,3},{8,12},{12,8},{9,1... | collective-permute-start | bytes 1720328 | tf_op jit(solution)/shard_map/ppermute | solution.py:1059
  905.4 72.3 %collective-permute-start.72 = (bf16[320,896]{1,0:T(8,128)(2,1)}, bf16[320,896]{1,0:T(8,128)(2,1)}, u32[]{:S(2)}, u32[]{:S(2)}) collective-permute-start(bf16[320,896]{1,0:T(8,128)(2,1)} %get-tuple-element.352), channel_id=1, source_target_pairs={{0,24},{8,0},{16,8},{24,16},{1,25},{9,1},{17,9},{25,17},{2,26},{10... | collective-permute-start | bytes 1720328 | tf_op jit(solution)/shard_map/ppermute | solution.py:1098
  905.5 72.3 %collective-permute-start.73 = (bf16[320,896]{1,0:T(8,128)(2,1)}, bf16[320,896]{1,0:T(8,128)(2,1)}, u32[]{:S(2)}, u32[]{:S(2)}) collective-permute-start(bf16[320,896]{1,0:T(8,128)(2,1)} %get-tuple-element.353), channel_id=1, source_target_pairs={{0,16},{8,24},{16,0},{24,8},{1,17},{9,25},{17,1},{25,9},{2,18},{10... | collective-permute-start | bytes 1720328 | tf_op jit(solution)/shard_map/ppermute | solution.py:1098
  909.4 68.4 %collective-permute-start.74 = (bf16[320,896]{1,0:T(8,128)(2,1)}, bf16[320,896]{1,0:T(8,128)(2,1)}, u32[]{:S(2)}, u32[]{:S(2)}) collective-permute-start(bf16[320,896]{1,0:T(8,128)(2,1)} %get-tuple-element.354), channel_id=1, source_target_pairs={{0,8},{8,16},{16,24},{24,0},{1,9},{9,17},{17,25},{25,1},{2,10},{10... | collective-permute-start | bytes 1720328 | tf_op jit(solution)/shard_map/ppermute | solution.py:1098
  911.4 66.4 %collective-permute-start.76 = (bf16[3,320,896]{2,1,0:T(8,128)(2,1)}, bf16[3,320,896]{2,1,0:T(8,128)(2,1)S(1)}, u32[]{:S(2)}, u32[]{:S(2)}) collective-permute-start(bf16[3,320,896]{2,1,0:T(8,128)(2,1)} %pad_maximum_fusion.3), channel_id=1, source_target_pairs={{0,4},{4,0},{1,5},{5,1},{2,6},{6,2},{3,7},{7,3},{8,12},{12,8},{9,1... | collective-permute-start | bytes 5160968 | tf_op jit(solution)/shard_map/ppermute | solution.py:1059
  992.7 20.7 %collective-permute-start.78 = (f32[4,2,320]{2,1,0:T(2,128)S(1)}, f32[4,2,320]{2,1,0:T(2,128)S(1)}, u32[]{:S(2)}, u32[]{:S(2)}) collective-permute-start(f32[4,2,320]{2,1,0:T(2,128)S(1)} %slice_add_fusion), channel_id=1, source_target_pairs={{0,2},{1,3},{2,0},{3,1},{4,6},{5,7},{6,4},{7,5},{8,10},{9,11},{10,... | collective-permute-start | bytes 30728 | tf_op jit(solution)/shard_map/ppermute | solution.py:1063
  (73 other events, 1100.3 us)
Sparse Core Ops, SparseCore 0:
  9.9 79.3 all-gather.2
  571.4 98.2 all-gather.4
